TPU v7x, 32 devices: a whole 2x2x4 slice. The times are simulated.
32 devices in a mesh: seq: 8 (over z, y), res: 4 (over x, core).
Axes of the slice: x: 2, y: 2, z: 4, core: 2. Of those that a mesh axis runs over, the one named last changes fastest.
Arguments:
- alignment_embedding: bfloat16 [128, 128, 768], P('seq', 'res'), may hold values from -12 to 12
- probe_projector: bfloat16 [768, 768], replicated, may hold values from -0.21875 to 0.21875
- lookup_projector: bfloat16 [768, 768], replicated, may hold values from -0.21875 to 0.21875
- content_projector: bfloat16 [768, 768], replicated, may hold values from -0.21875 to 0.21875
- final_projector: bfloat16 [768, 768], replicated, may hold values from -0.21875 to 0.21875
Outputs:
- mixed: bfloat16 [128, 128, 768], P('seq', 'res')
All inputs are finite; a program needn't handle non-finite values.
Results may differ from a plain program's by a relative error of at most 0.01.
Values may be sent and summed in bfloat16 or wider, within the bound.
No kernel may reach another device: no remote copies, remote signals or barrier semaphores. Data moves between devices by JAX's collectives and lax.ppermute only.
A program may use at most 128 MiB of HBM per device.

v0:
```python
import math

import jax
import jax.numpy as jnp
from jax import lax
from jax.sharding import PartitionSpec as P

H = 12


def reshape_by_group(inputs, weight, attention_groups):
    sequence_number, site_number, embed_size = inputs.shape
    out = jnp.dot(
        inputs.reshape(sequence_number * site_number, embed_size),
        weight,
        preferred_element_type=jnp.float32,
    )
    return out.astype(jnp.bfloat16).reshape(
        sequence_number, site_number, attention_groups, embed_size // attention_groups
    )


def body(
    alignment_embedding, probe_projector, lookup_projector, content_projector, final_projector
):
    sequence_number, site_number, embed_size = alignment_embedding.shape
    attention_groups = H
    head_size = embed_size // attention_groups
    seq_count = lax.axis_size("seq")
    scale = 1.0 / math.sqrt(head_size * sequence_number * seq_count)
    probe_tensor = reshape_by_group(alignment_embedding, probe_projector, attention_groups)
    gathered = lax.all_gather(alignment_embedding, "res", axis=1, tiled=True)
    all_keys = reshape_by_group(gathered, lookup_projector, attention_groups)
    all_values = reshape_by_group(gathered, content_projector, attention_groups)
    logits = jnp.einsum(
        "rihe,rjhe->hij", probe_tensor, all_keys, preferred_element_type=jnp.float32
    )
    summed = lax.psum(logits, "seq")
    probs = jax.nn.softmax(summed * scale, axis=-1).astype(jnp.bfloat16)
    attended = jnp.einsum("hij,rjhe->rihe", probs, all_values, preferred_element_type=jnp.float32)
    attended = attended.astype(jnp.bfloat16).reshape(sequence_number * site_number, embed_size)
    mixed = jnp.dot(attended, final_projector, preferred_element_type=jnp.float32).astype(
        jnp.bfloat16
    )
    return mixed.reshape(sequence_number, site_number, embed_size)


def solution(mesh):
    placed = (P("seq", "res", None), P(), P(), P(), P())
    return jax.shard_map(
        body, mesh=mesh, in_specs=placed, out_specs=P("seq", "res", None), check_vma=False
    )
```

profile of v0, /device:TPU:0, one launch (start us, length us, event | category | flops | bytes accessed | tf_op | source)
XLA Modules:
  0.0 147.9 jit_solution(13583169047443538152)
XLA Ops:
  6.5 0.0 copy-start
  6.5 0.0 all-gather.2.cloned.1.call-start
  6.5 0.7 all-gather.2.cloned.1.call-update
  7.3 0.0 all-reduce.2.cloned.1.call-start
  7.3 3.2 %convolution_convert_fusion.3 = bf16[512,768]{1,0:T(8,128)(2,1)} fusion(bf16[512,768]{1,0:T(8,128)(2,1)} %bitcast.37, bf16[768,768]{1,0:T(8,128)(2,1)} %param.6), kind=kOutput, calls=%fused_computation.8 | convolution fusion | flops 604372992 | bytes 2752512 | tf_op jit(solution)/shard_map/dot_general | solution.py:13
  10.5 2.7 %reshape.27 = bf16[16,32,12,64]{3,2,1,0:T(8,128)(2,1)S(1)} reshape(bf16[512,768]{1,0:T(8,128)(2,1)} %convolution_convert_fusion.3) | data formatting | bytes 1572864 | tf_op jit(solution)/shard_map/reshape | solution.py:18
  13.2 4.1 %copy.15 = bf16[16,32,12,64]{1,0,3,2:T(8,128)(2,1)} copy(bf16[16,32,12,64]{3,2,1,0:T(8,128)(2,1)S(1)} %reshape.27) | data formatting | bytes 1572864 | tf_op jit(solution)/shard_map/reshape | solution.py:18
  17.3 22.9 %all-gather.2.cloned.1.call-done = bf16[16,128,768]{2,1,0:T(8,128)(2,1)} async-done(((bf16[16,32,768]{2,1,0:T(8,128)(2,1)}), bf16[16,128,768]{2,1,0:T(8,128)(2,1)}) %all-gather.2.cloned.1.call-update) | async-done | bytes 3145744 | tf_op jit(solution)/shard_map/all_gather | solution.py:32
  40.2 6.2 %convolution_convert_fusion = bf16[2048,768]{1,0:T(8,128)(2,1)} fusion(bf16[2048,768]{1,0:T(8,128)(2,1)} %bitcast.38, bf16[768,768]{1,0:T(8,128)(2,1)S(1)} %copy-done), kind=kOutput, calls=%fused_computation.1 | convolution fusion | flops 2417491968 | bytes 7471104 | tf_op jit(solution)/shard_map/dot_general | solution.py:13
  46.4 4.7 %copy.10 = bf16[2048,768]{0,1:T(8,128)(2,1)} copy(bf16[2048,768]{1,0:T(8,128)(2,1)} %convolution_convert_fusion) | data formatting | bytes 6291456 | tf_op jit(solution)/shard_map/convert_element_type | solution.py:18
  51.1 3.1 %copy.21 = bf16[96,8,16,128]{3,2,1,0:T(8,128)(2,1)S(1)} copy(bf16[96,8,16,128]{3,1,2,0:T(8,128)(2,1)} %bitcast.33) | data formatting | bytes 6291456
  54.2 0.0 copy-done.1
  54.2 0.0 copy-start.2
  54.2 1.7 %convolution_bitcast_fusion = f32[12,32,128]{2,1,0:T(8,128)} fusion(bf16[16,32,12,64]{1,0,3,2:T(8,128)(2,1)S(1)} %copy-done.1, bf16[16,128,12,64]{1,0,3,2:T(8,128)(2,1)S(1)} %bitcast.36), kind=kOutput, calls=%fused_computation.11 | convolution fusion | flops 100663296 | bytes 4128768 | tf_op jit(solution)/shard_map/rihe,rjhe->hij/dot_general | solution.py:35
  55.8 0.0 all-reduce.2.cloned.1.call-update
  55.9 6.2 %convolution_convert_fusion.1 = bf16[2048,768]{1,0:T(8,128)(2,1)} fusion(bf16[2048,768]{1,0:T(8,128)(2,1)} %bitcast.39, bf16[768,768]{1,0:T(8,128)(2,1)S(1)} %copy-done.2), kind=kOutput, calls=%fused_computation.2 | convolution fusion | flops 2417491968 | bytes 7471104 | tf_op jit(solution)/shard_map/dot_general | solution.py:13
  62.1 4.8 %copy.9 = bf16[2048,768]{0,1:T(8,128)(2,1)} copy(bf16[2048,768]{1,0:T(8,128)(2,1)} %convolution_convert_fusion.1) | data formatting | bytes 6291456 | tf_op jit(solution)/shard_map/convert_element_type | solution.py:18
  66.8 4.6 %copy.20 = bf16[96,8,16,128]{3,2,1,0:T(8,128)(2,1)} copy(bf16[96,8,16,128]{3,1,2,0:T(8,128)(2,1)} %bitcast.34) | data formatting | bytes 6291456
  71.4 54.6 %all-reduce.2.cloned.1.call-done = f32[12,32,128]{2,1,0:T(8,128)} async-done(((f32[12,32,128]{2,1,0:T(8,128)}), f32[12,32,128]{2,1,0:T(8,128)}) %all-reduce.2.cloned.1.call-update) | async-done | bytes 196624 | tf_op jit(solution)/shard_map/psum | solution.py:38
  126.1 1.1 fusion.22
  127.2 6.2 %fusion.6 = bf16[16,32,12,64]{3,1,0,2:T(8,128)(2,1)} fusion(bf16[16,128,12,64]{1,0,3,2:T(8,128)(2,1)} %bitcast.35, f32[12,32]{1,0:T(8,128)S(1)} %fusion.22, f32[12,32,128]{2,1,0:T(8,128)} %all-reduce.2.cloned.1.call-done), kind=kOutput, calls=%fused_computation.6 | convolution fusion | flops 101253632 | bytes 4130304 | tf_op jit(solution)/shard_map/hij,rjhe->rihe/dot_general | solution.py:40
  133.4 2.5 %copy.14 = bf16[16,32,12,64]{3,2,1,0:T(8,128)(2,1)S(1)} copy(bf16[16,32,12,64]{3,1,0,2:T(8,128)(2,1)} %fusion.6) | data formatting | bytes 1572864 | tf_op jit(solution)/shard_map/convert_element_type | solution.py:41
  135.8 2.0 %reshape.29 = bf16[512,768]{1,0:T(8,128)(2,1)} reshape(bf16[16,32,12,64]{3,2,1,0:T(8,128)(2,1)S(1)} %copy.14) | data formatting | bytes 1572864 | tf_op jit(solution)/shard_map/reshape | solution.py:41
  137.9 3.2 %convolution_convert_fusion.2 = bf16[512,768]{1,0:T(8,128)(2,1)} fusion(bf16[512,768]{1,0:T(8,128)(2,1)} %reshape.29, bf16[768,768]{1,0:T(8,128)(2,1)} %param.9), kind=kOutput, calls=%fused_computation.7 | convolution fusion | flops 604372992 | bytes 2752512 | tf_op jit(solution)/shard_map/dot_general | solution.py:42
  (3 shorter events, 0.0 us)
Async XLA Ops:
  6.5 33.7 %copy-start = (bf16[768,768]{1,0:T(8,128)(2,1)S(1)}, bf16[768,768]{1,0:T(8,128)(2,1)}, u32[]{:S(2)}) copy-start(bf16[768,768]{1,0:T(8,128)(2,1)} %param.7) | copy-start | bytes 3538948
  6.5 33.6 %all-gather.2.cloned.1.call-start = ((), (), s32[]{:S(2)}) async-start(), calls=%async_computation | async-start | bytes 3932160 | tf_op jit(solution)/shard_map/all_gather | solution.py:32
  7.3 118.8 %all-reduce.2.cloned.1.call-start = ((), (), s32[]{:S(2)}) async-start(), calls=%async_computation.1 | async-start | bytes 393216 | tf_op jit(solution)/shard_map/psum | solution.py:38
  51.1 3.1 %copy-start.1 = (bf16[16,32,12,64]{1,0,3,2:T(8,128)(2,1)S(1)}, bf16[16,32,12,64]{1,0,3,2:T(8,128)(2,1)}, u32[]{:S(2)}) copy-start(bf16[16,32,12,64]{1,0,3,2:T(8,128)(2,1)} %copy.15) | copy-start | bytes 2359300
  54.2 1.7 %copy-start.2 = (bf16[768,768]{1,0:T(8,128)(2,1)S(1)}, bf16[768,768]{1,0:T(8,128)(2,1)}, u32[]{:S(2)}) copy-start(bf16[768,768]{1,0:T(8,128)(2,1)} %param.8) | copy-start | bytes 3538948
Sparse Core Ops, SparseCore 0:
  8.9 31.2 all-gather.1
  56.0 70.0 all-reduce.1
where the time goes:
time: 148 us
  waiting for transfers between devices  78.2 us (53%)
  local copies, waits for them, and re-layouts  28.4 us (19%)
  matrix products  26.6 us (18%)
  between operations  13.5 us (9%)
    psum x1, waiting for transfers between devices, body(): summed = lax.psum(logits, 'seq')  54.6 us
    all_gather x1, waiting for transfers between devices, body(): gathered = lax.all_gather(alignment_embedding, 'res', axis=1, tiled=True)  22.9 us
    dot_general x3, matrix products, reshape_by_group(): jnp.dot(inputs.reshape(sequence_number * site_number, embed_size), weight...  15.6 us
    convert_element_type x2, local copies, waits for them, and re-layouts, reshape_by_group(): out.astype(jnp.bfloat16)  9.45 us
    unnamed x8, local copies, waits for them, and re-layouts  7.65 us
    reshape x2, local copies, waits for them, and re-layouts, reshape_by_group(): out.astype(jnp.bfloat16)  6.82 us
    dot_general x1, matrix products, body(): jnp.einsum('hij,rjhe->rihe', probs, all_values, preferred_element_type=jn...  6.15 us
    dot_general x1, matrix products, body(): jnp.dot(attended, final_projector, preferred_element_type=jnp.float32)  3.17 us
  transfers between devices with their start and end apart: 2, of which 2 were waited for; matrix products, arithmetic and copies ran while one was open for 17% of the time, Pallas kernels for 0%

commit v1 on v0

v1 whole, which is shorter than its diff:
```python
import functools
import math

import jax
import jax.numpy as jnp
from jax import lax
from jax.experimental import pallas as pl
from jax.experimental.pallas import tpu as pltpu
from jax.sharding import PartitionSpec as P

H = 12
GROUP = 4
F32, BF16 = jnp.float32, jnp.bfloat16


def reshape_by_group(inputs, weight, attention_groups):
    sequence_number, site_number, embed_size = inputs.shape
    out = jnp.dot(
        inputs.reshape(sequence_number * site_number, embed_size),
        weight,
        preferred_element_type=F32,
    )
    return out.astype(BF16).reshape(
        sequence_number, site_number, attention_groups, embed_size // attention_groups
    )


def plain_body(
    alignment_embedding, probe_projector, lookup_projector, content_projector, final_projector
):
    sequence_number, site_number, embed_size = alignment_embedding.shape
    head_size = embed_size // H
    scale = 1.0 / math.sqrt(head_size * sequence_number * lax.axis_size("seq"))
    probe_tensor = reshape_by_group(alignment_embedding, probe_projector, H)
    gathered = lax.all_gather(alignment_embedding, "res", axis=1, tiled=True)
    all_keys = reshape_by_group(gathered, lookup_projector, H)
    all_values = reshape_by_group(gathered, content_projector, H)
    logits = jnp.einsum("rihe,rjhe->hij", probe_tensor, all_keys, preferred_element_type=F32)
    summed = lax.psum(logits, "seq")
    probs = jax.nn.softmax(summed * scale, axis=-1).astype(BF16)
    attended = jnp.einsum("hij,rjhe->rihe", probs, all_values, preferred_element_type=F32)
    attended = attended.astype(BF16).reshape(sequence_number * site_number, embed_size)
    mixed = jnp.dot(attended, final_projector, preferred_element_type=F32).astype(BF16)
    return mixed.reshape(sequence_number, site_number, embed_size)


def call(kernel, outs, args, flops=0, scratch=()):
    shapes = [jax.ShapeDtypeStruct(s, d) for s, d in outs]
    moved = sum(a.size * a.dtype.itemsize for a in list(args) + shapes)
    return pl.pallas_call(
        kernel,
        out_shape=shapes,
        in_specs=[pl.BlockSpec(memory_space=pltpu.VMEM)] * len(args),
        out_specs=[pl.BlockSpec(memory_space=pltpu.VMEM)] * len(shapes),
        scratch_shapes=list(scratch),
        cost_estimate=pl.CostEstimate(flops=flops, bytes_accessed=moved, transcendentals=0),
        compiler_params=pltpu.CompilerParams(vmem_limit_bytes=40 * 1024 * 1024),
    )(*args)


def matmul(x, w):
    return jnp.dot(x, w, preferred_element_type=F32).astype(BF16)


def by_head(block, head_size):
    heads = block.shape[1] // head_size
    lane = lax.broadcasted_iota(jnp.int32, block.shape, 1) // head_size
    zero = jnp.zeros_like(block)
    return jnp.concatenate([jnp.where(lane == h, block, zero) for h in range(heads)], axis=0)


def against(probe, keys):
    return lax.dot_general(probe, keys, (((1,), (1,)), ((), ())), preferred_element_type=F32)


def kernel_near(rows, sites, width, x_own, x_twin, wq, wk, q_out, k_out, logits_out):
    q_out[...] = matmul(x_own[...], wq[...])
    for t, x in enumerate((x_own, x_twin)):
        k = matmul(x[...], wk[...])
        for r in range(rows):
            k_out[r, t * sites : (t + 1) * sites, :] = k[r * sites : (r + 1) * sites, :]
    stack = GROUP * sites
    for g in range(H // GROUP):
        lanes = slice(g * width, (g + 1) * width)
        total = jnp.zeros((stack, 2 * sites), F32)
        for r in range(rows):
            probe = by_head(q_out[r * sites : (r + 1) * sites, lanes], width // GROUP)
            total = total + against(probe, k_out[r, :, lanes])
        logits_out[g * stack : (g + 1) * stack, :] = total


def kernel_far(
    rows, sites, width, x_far, x_far_twin, wq, wk, q_own, k_near, near, *refs
):
    parts, (far_k, far_q, ahead, back) = refs[:GROUP], refs[GROUP:]
    half = rows // 2
    came = (1 - lax.axis_index("res") // 2) * half
    me = lax.rem(lax.axis_index("seq"), GROUP)
    for t, x in enumerate((x_far, x_far_twin)):
        k = matmul(x[...], wk[...])
        for r in range(half):
            far_k[r, t * sites : (t + 1) * sites, :] = k[r * sites : (r + 1) * sites, :]
    far_q[...] = matmul(x_far[...], wq[...])
    stack = GROUP * sites
    for g in range(H // GROUP):
        lanes = slice(g * width, (g + 1) * width)
        one = jnp.zeros((stack, 2 * sites), F32)
        two = jnp.zeros((stack, 2 * sites), F32)
        for r in range(half):
            own = q_own[pl.ds((came + r) * sites, sites), lanes]
            one = one + against(by_head(own, width // GROUP), far_k[r, :, lanes])
            other = far_q[r * sites : (r + 1) * sites, lanes]
            two = two + against(by_head(other, width // GROUP), k_near[came + r, :, lanes])
        rows_g = slice(g * stack, (g + 1) * stack)
        ahead[rows_g, :] = jnp.concatenate([near[rows_g, :], one], axis=1)
        back[rows_g, :] = two
    size = H * sites // GROUP
    for k in range(GROUP):
        at = lax.bitwise_xor(me, k) * size
        parts[k][:size, :] = ahead[pl.ds(at, size), :]
        parts[k][size:, :] = jnp.concatenate(
            [back[pl.ds(at, size // 2), :], back[pl.ds(at + size // 2, size // 2), :]], axis=1
        )


def kernel_sum(size, a, b, c, d, ahead, back):
    ahead[...] = (a[:size, :] + b[:size, :]) + (c[:size, :] + d[:size, :])
    back[...] = (a[size:, :] + b[size:, :]) + (c[size:, :] + d[size:, :])


def kernel_softmax(scale, ahead, ahead_z, back_x, back_xz, out):
    far = back_x[...] + back_xz[...]
    half = far.shape[1] // 2
    far = jnp.concatenate([far[:, :half], far[:, half:]], axis=0)
    far = jnp.concatenate([jnp.zeros_like(far), far], axis=1)
    logits = (ahead[...] + ahead_z[...] + far) * scale
    e = jnp.exp(logits - jnp.max(logits, axis=1, keepdims=True))
    out[...] = (e / jnp.sum(e, axis=1, keepdims=True)).astype(BF16)


def kernel_values(sites, *refs):
    w, outs = refs[-1 - (len(refs) - 1) // 3], refs[-((len(refs) - 1) // 3) :]
    for n, out in enumerate(outs):
        for t in range(2):
            v = matmul(refs[2 * n + t][...], w[...])
            for r in range(out.shape[0]):
                out[r, t * sites : (t + 1) * sites, :] = v[r * sites : (r + 1) * sites, :]


def kernel_last(rows, sites, width, p0, p1, p2, p3, v_near, v_first, v_second, wo, out, probs, att):
    half = rows // 2
    place = lax.axis_index("res") // 2
    me = lax.rem(lax.axis_index("seq"), GROUP)
    size = H * sites // GROUP
    for k, p in enumerate((p0, p1, p2, p3)):
        probs[pl.ds(lax.bitwise_xor(me, k) * size, size), :] = p[...]
    stack, head = GROUP * sites, width // GROUP
    lane = lax.broadcasted_iota(jnp.int32, (sites, width), 1) // head
    for n, (far, start) in enumerate(((v_first, (1 - place) * half), (v_second, place * half))):
        for r in range(half):
            for g in range(H // GROUP):
                lanes = slice(g * width, (g + 1) * width)
                v = jnp.concatenate([v_near[start + r, :, lanes], far[r, :, lanes]], axis=0)
                full = jnp.dot(
                    probs[g * stack : (g + 1) * stack, :], v, preferred_element_type=F32
                )
                one = full[:sites]
                for h in range(1, GROUP):
                    one = jnp.where(lane == h, full[h * sites : (h + 1) * sites], one)
                att[r * sites : (r + 1) * sites, lanes] = one.astype(BF16)
        out[pl.ds(start * sites, half * sites), :] = matmul(att[...], wo[...])


def swap(x, axis, bit):
    count = lax.axis_size(axis)
    return lax.ppermute(x, axis, [(i, i ^ bit) for i in range(count)])


def body(x, wq, wk, wv, wo):
    rows, sites, embed = x.shape
    half, width = rows // 2, embed // (H // GROUP)
    n_seq, n_res = lax.axis_size("seq"), lax.axis_size("res")
    scale = 1.0 / math.sqrt(embed // H * rows * n_seq)
    flat, half_flat = (rows * sites, embed), (half * sites, embed)
    place = lax.axis_index("res") // 2
    own = x.reshape(flat)
    cost = 2 * rows * sites * embed * embed

    sent_first = lax.dynamic_slice_in_dim(own, place * half * sites, half * sites)
    far_first = swap(sent_first, "res", 2)
    twin = swap(own, "res", 1)
    far_first_twin = swap(far_first, "res", 1)
    sent_second = lax.dynamic_slice_in_dim(own, (1 - place) * half * sites, half * sites)
    sent_second, _ = lax.optimization_barrier((sent_second, far_first))
    far_second = swap(sent_second, "res", 2)
    far_second_twin = swap(far_second, "res", 1)

    q, k_near, near = call(
        functools.partial(kernel_near, rows, sites, width),
        [(flat, BF16), ((rows, 2 * sites, embed), BF16), ((H * sites, 2 * sites), F32)],
        (own, twin, wq, wk),
        4 * cost,
    )
    size = H * sites // GROUP
    part = (size + size // 2, 4 * sites)
    parts = call(
        functools.partial(kernel_far, rows, sites, width),
        [(part, F32)] * GROUP,
        (far_first, far_first_twin, wq, wk, q, k_near, near),
        2 * cost,
        [
            pltpu.VMEM((half, 2 * sites, embed), BF16),
            pltpu.VMEM(half_flat, BF16),
            pltpu.VMEM((H * sites, 4 * sites), F32),
            pltpu.VMEM((H * sites, 2 * sites), F32),
        ],
    )
    came = [swap(parts[k], "seq", k) for k in range(1, GROUP)]
    ahead, back = call(
        functools.partial(kernel_sum, size),
        [((size, 4 * sites), F32), ((size // 2, 4 * sites), F32)],
        (parts[0], *came),
    )
    ahead_z = swap(ahead, "seq", GROUP)
    back_x = swap(back, "res", 2)
    cross = [
        (s * n_res + r, (s ^ GROUP) * n_res + (r ^ 2)) for s in range(n_seq) for r in range(n_res)
    ]
    back_xz = lax.ppermute(back, ("seq", "res"), cross)
    (probs,) = call(
        functools.partial(kernel_softmax, scale),
        [((size, 4 * sites), BF16)],
        (ahead, ahead_z, back_x, back_xz),
    )
    others = [swap(probs, "seq", k) for k in range(1, GROUP)]

    v_near, v_first = call(
        functools.partial(kernel_values, sites),
        [((rows, 2 * sites, embed), BF16), ((half, 2 * sites, embed), BF16)],
        (own, twin, far_first, far_first_twin, wv),
        3 * cost,
    )
    (v_second,) = call(
        functools.partial(kernel_values, sites),
        [((half, 2 * sites, embed), BF16)],
        (far_second, far_second_twin, wv),
        cost,
    )
    (out,) = call(
        functools.partial(kernel_last, rows, sites, width),
        [(flat, BF16)],
        (probs, *others, v_near, v_first, v_second, wo),
        2 * cost,
        [pltpu.VMEM((H * sites, 4 * sites), BF16), pltpu.VMEM(half_flat, BF16)],
    )
    return out.reshape(rows, sites, embed)


def solution(mesh):
    placed = (P("seq", "res", None), P(), P(), P(), P())
    fits = mesh.shape["res"] == 4 and mesh.shape["seq"] == 2 * GROUP
    return jax.shard_map(
        body if fits else plain_body,
        mesh=mesh,
        in_specs=placed,
        out_specs=P("seq", "res", None),
        check_vma=False,
    )
```

time: 148 us -> 59.2 us (0.40)
  waiting for transfers between devices: 78.2 us -> 27.7 us
  matrix products: 26.6 us -> 0 us
  local copies, waits for them, and re-layouts: 28.4 us -> 3.69 us
  starting transfers between devices: 0.04 us -> 16.3 us
  between operations: 13.5 us -> 0.13 us
  Pallas kernels: 0 us -> 11.1 us
    psum x1 -> x0, waiting for transfers between devices: 54.6 us -> none  [body(): summed = lax.psum(logits, 'seq')]
    ppermute x0 -> x14, waiting for transfers between devices: none -> 27.7 us  [the longest x13 26 us: swap(): return lax.ppermute(x, axis, [(i, i ^ bit) for i in range(count)])]
    dot_general x6 -> x0, matrix products: 26.6 us -> none  [the longest x3 15.6 us: reshape_by_group(): jnp.dot(inputs.reshape(sequence_number * site_number, embed_size), weight...]
    all_gather x1 -> x0, waiting for transfers between devices: 22.9 us -> none  [body(): gathered = lax.all_gather(alignment_embedding, 'res', axis=1, tiled=True)]
    ppermute x0 -> x14, starting transfers between devices: none -> 16.3 us  [the longest x13 13.8 us: swap(): return lax.ppermute(x, axis, [(i, i ^ bit) for i in range(count)])]
    convert_element_type x3 -> x0, local copies, waits for them, and re-layouts: 11.9 us -> none  [the longest x2 9.45 us: reshape_by_group(): out.astype(jnp.bfloat16)]
    pallas_call x0 -> x7, Pallas kernels: none -> 11.1 us  [call(): pl.pallas_call(kernel, out_shape=shapes, in_specs=[pl.BlockSpec(memory_sp...]
    reshape x3 -> x0, local copies, waits for them, and re-layouts: 8.85 us -> none  [the longest x2 6.82 us: reshape_by_group(): out.astype(jnp.bfloat16)]
  transfers between devices with their start and end apart: 2 -> 14, of which waited for: 2 -> 8; matrix products, arithmetic and copies ran while one was open for 17% -> 0% of each run, Pallas kernels for 0% -> 14%
where the time goes in v1:
time: 59.2 us; the launch traced here: 59 us
  waiting for transfers between devices  27.7 us (47%)
  starting transfers between devices  16.3 us (28%)
  Pallas kernels  11.1 us (19%)
  local copies, waits for them, and re-layouts  3.69 us (6%)
    ppermute x13, waiting for transfers between devices, swap(): return lax.ppermute(x, axis, [(i, i ^ bit) for i in range(count)])  26 us
    ppermute x13, starting transfers between devices, swap(): return lax.ppermute(x, axis, [(i, i ^ bit) for i in range(count)])  13.8 us
    pallas_call x7, Pallas kernels, call(): pl.pallas_call(kernel, out_shape=shapes, in_specs=[pl.BlockSpec(memory_sp...  11.1 us
    ppermute x1, starting transfers between devices, body(): back_xz = lax.ppermute(back, ('seq', 'res'), cross)  2.56 us
    unnamed x14, local copies, waits for them, and re-layouts  2.42 us
    ppermute x1, waiting for transfers between devices, body(): back_xz = lax.ppermute(back, ('seq', 'res'), cross)  1.76 us
    dynamic_slice x1, local copies, waits for them, and re-layouts, body(): lax.dynamic_slice_in_dim(own, (1 - place) * half * sites, half * sites)  1.26 us
  transfers between devices with their start and end apart: 14, of which 8 were waited for; matrix products, arithmetic and copies ran while one was open for 0% of the time, Pallas kernels for 14%

profile of v1, /device:TPU:0, one launch (start us, length us, event | category | flops | bytes accessed | tf_op | source)
XLA Modules:
  0.0 59.0 jit_solution(4632531048665410434)
XLA Ops:
  0.0 1.3 %constant_dynamic-slice_fusion = (bf16[256,768]{1,0:T(8,128)(2,1)S(1)}, bf16[256,768]{1,0:T(8,128)(2,1)S(1)}) fusion(bf16[512,768]{1,0:T(8,128)(2,1)} %bitcast.2, s32[]{:T(128)S(6)} %select_n.13, s32[]{:T(128)S(6)} %select_n.12), kind=kLoop, calls=%fused_computation | loop fusion | bytes 1572872 | tf_op jit(solution)/shard_map/dynamic_slice | solution.py:193
  1.3 3.0 %collective-permute-start = (bf16[256,768]{1,0:T(8,128)(2,1)S(1)}, bf16[256,768]{1,0:T(8,128)(2,1)S(1)}, u32[]{:S(2)}, u32[]{:S(2)}) collective-permute-start(bf16[256,768]{1,0:T(8,128)(2,1)S(1)} %get-tuple-element.30), channel_id=1, source_target_pairs={{0,2},{1,3},{2,0},{3,1},{4,6},{5,7},{6,4},{7,5},{8,10},{9,11},{10,... | collective-permute-start | bytes 1179656 | tf_op jit(solution)/shard_map/ppermute | solution.py:176
  4.3 9.1 %collective-permute-done.x_far.refs_2_ = bf16[256,768]{1,0:T(8,128)(2,1)S(1)} collective-permute-done((bf16[256,768]{1,0:T(8,128)(2,1)S(1)}, bf16[256,768]{1,0:T(8,128)(2,1)S(1)}, u32[]{:S(2)}, u32[]{:S(2)}) %collective-permute-start) | collective-permute-done | bytes 393248 | tf_op jit(solution)/shard_map/ppermute | solution.py:176
  13.4 1.7 %collective-permute-start.12 = (bf16[256,768]{1,0:T(8,128)(2,1)S(1)}, bf16[256,768]{1,0:T(8,128)(2,1)S(1)}, u32[]{:S(2)}, u32[]{:S(2)}) collective-permute-start(bf16[256,768]{1,0:T(8,128)(2,1)S(1)} %get-tuple-element.28), channel_id=1, source_target_pairs={{0,2},{1,3},{2,0},{3,1},{4,6},{5,7},{6,4},{7,5},{8,10},{9,11},{10,... | collective-permute-start | bytes 1179656 | tf_op jit(solution)/shard_map/ppermute | solution.py:176
  15.1 8.6 %collective-permute-done.12.refs_0_ = bf16[256,768]{1,0:T(8,128)(2,1)S(1)} collective-permute-done((bf16[256,768]{1,0:T(8,128)(2,1)S(1)}, bf16[256,768]{1,0:T(8,128)(2,1)S(1)}, u32[]{:S(2)}, u32[]{:S(2)}) %collective-permute-start.12) | collective-permute-done | bytes 393248 | tf_op jit(solution)/shard_map/ppermute | solution.py:176
  23.7 1.3 %copy-done.2 = bf16[768,768]{1,0:T(8,128)(2,1)S(1)} copy-done((bf16[768,768]{1,0:T(8,128)(2,1)S(1)}, bf16[768,768]{1,0:T(8,128)(2,1)}, u32[]{:S(2)}) %copy-start.2) | copy-done | bytes 1179672
  25.0 1.1 %copy-done.5 = bf16[16,32,768]{2,1,0:T(8,128)(2,1)S(1)} copy-done((bf16[16,32,768]{2,1,0:T(8,128)(2,1)S(1)}, bf16[16,32,768]{2,1,0:T(8,128)(2,1)}, u32[]{:S(2)}) %copy-start.5) | copy-done | bytes 786456
  26.1 2.9 %shard_map.55 = (bf16[512,768]{1,0:T(8,128)(2,1)S(1)}, bf16[16,64,768]{2,1,0:T(8,128)(2,1)S(1)}, f32[384,64]{1,0:T(8,128)S(1)}) custom-call(bf16[512,768]{1,0:T(8,128)(2,1)S(1)} %bitcast.4, bf16[512,768]{1,0:T(8,128)(2,1)S(1)} %collective-permute-done.2.x_twin.refs_1_, bf16[768,768]{1,0:T(8,128)(2,1)S(1)} %copy-done.1, bf16[768,768]{1,0:T(8,128)(2,1)S(1)} %copy-done.2), custom_call_target="tpu_custom_call" | custom-call | flops 2415919104 | bytes 6389760 | tf_op jit(solution)/shard_map/pallas_call | solution.py:50
  29.1 2.3 %shard_map.56 = (f32[144,128]{1,0:T(8,128)S(1)}, f32[144,128]{1,0:T(8,128)S(1)}, f32[144,128]{1,0:T(8,128)S(1)}, f32[144,128]{1,0:T(8,128)S(1)}) custom-call(bf16[256,768]{1,0:T(8,128)(2,1)S(1)} %collective-permute-done.x_far.refs_2_, bf16[256,768]{1,0:T(8,128)(2,1)S(1)} %collective-permute-done.1.x_far_twin.refs_3_, bf16[768,768]{1,0:T(8,128)(2,1)S(1)} %copy-done.1, ...), custom_call_target="tpu_custom_call" | custom-call | flops 1207959552 | bytes 5898240 | tf_op jit(solution)/shard_map/pallas_call | solution.py:50
  31.4 1.5 %collective-permute-start.3 = (f32[144,128]{1,0:T(8,128)S(1)}, f32[144,128]{1,0:T(8,128)S(1)}, u32[]{:S(2)}, u32[]{:S(2)}) collective-permute-start(f32[144,128]{1,0:T(8,128)S(1)} %get-tuple-element.21), channel_id=1, source_target_pairs={{0,4},{4,0},{8,12},{12,8},{16,20},{20,16},{24,28},{28,24},{1,5},{5... | collective-permute-start | bytes 221192 | tf_op jit(solution)/shard_map/ppermute | solution.py:176
  33.0 1.6 %collective-permute-start.4 = (f32[144,128]{1,0:T(8,128)S(1)}, f32[144,128]{1,0:T(8,128)S(1)}, u32[]{:S(2)}, u32[]{:S(2)}) collective-permute-start(f32[144,128]{1,0:T(8,128)S(1)} %get-tuple-element.22), channel_id=1, source_target_pairs={{0,8},{4,12},{8,0},{12,4},{16,24},{20,28},{24,16},{28,20},{1,9},{5... | collective-permute-start | bytes 221192 | tf_op jit(solution)/shard_map/ppermute | solution.py:176
  35.0 1.2 %collective-permute-done.3.b = f32[144,128]{1,0:T(8,128)S(1)} collective-permute-done((f32[144,128]{1,0:T(8,128)S(1)}, f32[144,128]{1,0:T(8,128)S(1)}, u32[]{:S(2)}, u32[]{:S(2)}) %collective-permute-start.3) | collective-permute-done | bytes 73760 | tf_op jit(solution)/shard_map/ppermute | solution.py:176
  36.2 1.6 %collective-permute-done.4.c = f32[144,128]{1,0:T(8,128)S(1)} collective-permute-done((f32[144,128]{1,0:T(8,128)S(1)}, f32[144,128]{1,0:T(8,128)S(1)}, u32[]{:S(2)}, u32[]{:S(2)}) %collective-permute-start.4) | collective-permute-done | bytes 73760 | tf_op jit(solution)/shard_map/ppermute | solution.py:176
  37.8 2.0 %collective-permute-done.5.d = f32[144,128]{1,0:T(8,128)S(1)} collective-permute-done((f32[144,128]{1,0:T(8,128)S(1)}, f32[144,128]{1,0:T(8,128)S(1)}, u32[]{:S(2)}, u32[]{:S(2)}) %collective-permute-start.5) | collective-permute-done | bytes 73760 | tf_op jit(solution)/shard_map/ppermute | solution.py:176
  39.8 1.6 %collective-permute-start.7 = (f32[48,128]{1,0:T(8,128)S(1)}, f32[48,128]{1,0:T(8,128)S(1)}, u32[]{:S(2)}, u32[]{:S(2)}) collective-permute-start(f32[48,128]{1,0:T(8,128)S(1)} %get-tuple-element.25), channel_id=1, source_target_pairs={{0,2},{1,3},{2,0},{3,1},{4,6},{5,7},{6,4},{7,5},{8,10},{9,11},{10,... | collective-permute-start | bytes 73736 | tf_op jit(solution)/shard_map/ppermute | solution.py:176
  41.4 2.6 %collective-permute-start.8 = (f32[48,128]{1,0:T(8,128)S(1)}, f32[48,128]{1,0:T(8,128)S(1)}, u32[]{:S(2)}, u32[]{:S(2)}) collective-permute-start(f32[48,128]{1,0:T(8,128)S(1)} %get-tuple-element.25), channel_id=1, source_target_pairs={{0,18},{1,19},{2,16},{3,17},{4,22},{5,23},{6,20},{7,21},{8,26},{9,... | collective-permute-start | bytes 73736 | tf_op jit(solution)/shard_map/ppermute | solution.py:229
  44.3 2.0 %shard_map.59 = (bf16[16,64,768]{2,1,0:T(8,128)(2,1)S(1)}, bf16[8,64,768]{2,1,0:T(8,128)(2,1)S(1)}) custom-call(bf16[512,768]{1,0:T(8,128)(2,1)S(1)} %bitcast.5, bf16[512,768]{1,0:T(8,128)(2,1)S(1)} %collective-permute-done.2.x_twin.refs_1_, bf16[256,768]{1,0:T(8,128)(2,1)S(1)} %collective-permute-done.x_far.refs_2_, ...), custom_call_target="tpu_custom_call" | custom-call | flops 1811939328 | bytes 5898240 | tf_op jit(solution)/shard_map/pallas_call | solution.py:50
  46.3 1.8 %collective-permute-done.8.back_xz = f32[48,128]{1,0:T(8,128)S(1)} collective-permute-done((f32[48,128]{1,0:T(8,128)S(1)}, f32[48,128]{1,0:T(8,128)S(1)}, u32[]{:S(2)}, u32[]{:S(2)}) %collective-permute-start.8) | collective-permute-done | bytes 24608 | tf_op jit(solution)/shard_map/ppermute | solution.py:229
  48.0 1.4 %collective-permute-done.6.ahead_z = f32[96,128]{1,0:T(8,128)S(1)} collective-permute-done((f32[96,128]{1,0:T(8,128)S(1)}, f32[96,128]{1,0:T(8,128)S(1)}, u32[]{:S(2)}, u32[]{:S(2)}) %collective-permute-start.6) | collective-permute-done | bytes 49184 | tf_op jit(solution)/shard_map/ppermute | solution.py:176
  49.9 1.6 %collective-permute-start.10 = (bf16[96,128]{1,0:T(8,128)(2,1)S(1)}, bf16[96,128]{1,0:T(8,128)(2,1)S(1)}, u32[]{:S(2)}, u32[]{:S(2)}) collective-permute-start(bf16[96,128]{1,0:T(8,128)(2,1)S(1)} %shard_map.58.p0), channel_id=1, source_target_pairs={{0,8},{4,12},{8,0},{12,4},{16,24},{20,28},{24,16},{28,20},{1,9},{5... | collective-permute-start | bytes 73736 | tf_op jit(solution)/shard_map/ppermute | solution.py:176
  51.5 1.8 %collective-permute-start.11 = (bf16[96,128]{1,0:T(8,128)(2,1)S(1)}, bf16[96,128]{1,0:T(8,128)(2,1)S(1)}, u32[]{:S(2)}, u32[]{:S(2)}) collective-permute-start(bf16[96,128]{1,0:T(8,128)(2,1)S(1)} %shard_map.58.p0), channel_id=1, source_target_pairs={{0,12},{4,8},{8,4},{12,0},{16,28},{20,24},{24,20},{28,16},{1,13},{... | collective-permute-start | bytes 73736 | tf_op jit(solution)/shard_map/ppermute | solution.py:176
  53.3 0.8 %shard_map.60.v_second = bf16[8,64,768]{2,1,0:T(8,128)(2,1)S(1)} custom-call(bf16[256,768]{1,0:T(8,128)(2,1)S(1)} %collective-permute-done.12.refs_0_, bf16[256,768]{1,0:T(8,128)(2,1)S(1)} %collective-permute-done.13.refs_1_, bf16[768,768]{1,0:T(8,128)(2,1)S(1)} %copy-done.4), custom_call_target="tpu_custom_call" | custom-call | flops 603979776 | bytes 2752512 | tf_op jit(solution)/shard_map/pallas_call | solution.py:50
  54.1 2.1 %collective-permute-done.11.p3 = bf16[96,128]{1,0:T(8,128)(2,1)S(1)} collective-permute-done((bf16[96,128]{1,0:T(8,128)(2,1)S(1)}, bf16[96,128]{1,0:T(8,128)(2,1)S(1)}, u32[]{:S(2)}, u32[]{:S(2)}) %collective-permute-start.11) | collective-permute-done | bytes 24608 | tf_op jit(solution)/shard_map/ppermute | solution.py:176
  56.2 2.7 %shard_map.61 = bf16[512,768]{1,0:T(8,128)(2,1)} custom-call(bf16[96,128]{1,0:T(8,128)(2,1)S(1)} %shard_map.58.p0, bf16[96,128]{1,0:T(8,128)(2,1)S(1)} %collective-permute-done.9.p1, bf16[96,128]{1,0:T(8,128)(2,1)S(1)} %collective-permute-done.10.p2, bf16[96,128]{1,0:T(8,128)(2,1)S(1)} %collective-permute-done.11.p3, ...), custom_call_target="tpu_custom_call" | custom-call | flops 1207959552 | bytes 5210112 | tf_op jit(solution)/shard_map/pallas_call | solution.py:50
  (26 shorter events, 1.3 us)
Async XLA Ops:
  0.0 23.7 %copy-start.1 = (bf16[768,768]{1,0:T(8,128)(2,1)S(1)}, bf16[768,768]{1,0:T(8,128)(2,1)}, u32[]{:S(2)}) copy-start(bf16[768,768]{1,0:T(8,128)(2,1)} %wq.3) | copy-start | bytes 3538948
  1.3 12.1 %collective-permute-start = (bf16[256,768]{1,0:T(8,128)(2,1)S(1)}, bf16[256,768]{1,0:T(8,128)(2,1)S(1)}, u32[]{:S(2)}, u32[]{:S(2)}) collective-permute-start(bf16[256,768]{1,0:T(8,128)(2,1)S(1)} %get-tuple-element.30), channel_id=1, source_target_pairs={{0,2},{1,3},{2,0},{3,1},{4,6},{5,7},{6,4},{7,5},{8,10},{9,11},{10,... | collective-permute-start | bytes 1179656 | tf_op jit(solution)/shard_map/ppermute | solution.py:176
  4.3 19.4 %collective-permute-start.2 = (bf16[512,768]{1,0:T(8,128)(2,1)}, bf16[512,768]{1,0:T(8,128)(2,1)S(1)}, u32[]{:S(2)}, u32[]{:S(2)}) collective-permute-start(bf16[512,768]{1,0:T(8,128)(2,1)} %bitcast.3), channel_id=1, source_target_pairs={{0,1},{1,0},{2,3},{3,2},{4,5},{5,4},{6,7},{7,6},{8,9},{9,8},{10,11... | collective-permute-start | bytes 2359304 | tf_op jit(solution)/shard_map/ppermute | solution.py:176
  13.4 10.3 %collective-permute-start.12 = (bf16[256,768]{1,0:T(8,128)(2,1)S(1)}, bf16[256,768]{1,0:T(8,128)(2,1)S(1)}, u32[]{:S(2)}, u32[]{:S(2)}) collective-permute-start(bf16[256,768]{1,0:T(8,128)(2,1)S(1)} %get-tuple-element.28), channel_id=1, source_target_pairs={{0,2},{1,3},{2,0},{3,1},{4,6},{5,7},{6,4},{7,5},{8,10},{9,11},{10,... | collective-permute-start | bytes 1179656 | tf_op jit(solution)/shard_map/ppermute | solution.py:176
  15.1 13.9 %collective-permute-start.1 = (bf16[256,768]{1,0:T(8,128)(2,1)S(1)}, bf16[256,768]{1,0:T(8,128)(2,1)S(1)}, u32[]{:S(2)}, u32[]{:S(2)}) collective-permute-start(bf16[256,768]{1,0:T(8,128)(2,1)S(1)} %collective-permute-done.x_far.refs_2_), channel_id=1, source_target_pairs={{0,1},{1,0},{2,3},{3,2},{4,5},{5,4},{6,7},{7,6},{8,9},{9,8},{10,11... | collective-permute-start | bytes 1179656 | tf_op jit(solution)/shard_map/ppermute | solution.py:176
  23.7 29.6 %collective-permute-start.13 = (bf16[256,768]{1,0:T(8,128)(2,1)S(1)}, bf16[256,768]{1,0:T(8,128)(2,1)S(1)}, u32[]{:S(2)}, u32[]{:S(2)}) collective-permute-start(bf16[256,768]{1,0:T(8,128)(2,1)S(1)} %collective-permute-done.12.refs_0_), channel_id=1, source_target_pairs={{0,1},{1,0},{2,3},{3,2},{4,5},{5,4},{6,7},{7,6},{8,9},{9,8},{10,11... | collective-permute-start | bytes 1179656 | tf_op jit(solution)/shard_map/ppermute | solution.py:176
  23.7 1.3 %copy-start.2 = (bf16[768,768]{1,0:T(8,128)(2,1)S(1)}, bf16[768,768]{1,0:T(8,128)(2,1)}, u32[]{:S(2)}) copy-start(bf16[768,768]{1,0:T(8,128)(2,1)} %wk.3) | copy-start | bytes 3538948
  25.0 1.1 %copy-start.5 = (bf16[16,32,768]{2,1,0:T(8,128)(2,1)S(1)}, bf16[16,32,768]{2,1,0:T(8,128)(2,1)}, u32[]{:S(2)}) copy-start(bf16[16,32,768]{2,1,0:T(8,128)(2,1)} %param.5) | copy-start | bytes 2359300
  26.1 3.0 %copy-start.3 = (bf16[768,768]{1,0:T(8,128)(2,1)S(1)}, bf16[768,768]{1,0:T(8,128)(2,1)}, u32[]{:S(2)}) copy-start(bf16[768,768]{1,0:T(8,128)(2,1)} %wk.3) | copy-start | bytes 3538948
  29.1 15.2 %copy-start.4 = (bf16[768,768]{1,0:T(8,128)(2,1)S(1)}, bf16[768,768]{1,0:T(8,128)(2,1)}, u32[]{:S(2)}) copy-start(bf16[768,768]{1,0:T(8,128)(2,1)} %refs_2_.1) | copy-start | bytes 3538948
  29.1 15.2 %copy-start.6 = (bf16[16,32,768]{2,1,0:T(8,128)(2,1)S(1)}, bf16[16,32,768]{2,1,0:T(8,128)(2,1)}, u32[]{:S(2)}) copy-start(bf16[16,32,768]{2,1,0:T(8,128)(2,1)} %param.5) | copy-start | bytes 2359300
  31.4 4.7 %collective-permute-start.3 = (f32[144,128]{1,0:T(8,128)S(1)}, f32[144,128]{1,0:T(8,128)S(1)}, u32[]{:S(2)}, u32[]{:S(2)}) collective-permute-start(f32[144,128]{1,0:T(8,128)S(1)} %get-tuple-element.21), channel_id=1, source_target_pairs={{0,4},{4,0},{8,12},{12,8},{16,20},{20,16},{24,28},{28,24},{1,5},{5... | collective-permute-start | bytes 221192 | tf_op jit(solution)/shard_map/ppermute | solution.py:176
  33.0 4.8 %collective-permute-start.4 = (f32[144,128]{1,0:T(8,128)S(1)}, f32[144,128]{1,0:T(8,128)S(1)}, u32[]{:S(2)}, u32[]{:S(2)}) collective-permute-start(f32[144,128]{1,0:T(8,128)S(1)} %get-tuple-element.22), channel_id=1, source_target_pairs={{0,8},{4,12},{8,0},{12,4},{16,24},{20,28},{24,16},{28,20},{1,9},{5... | collective-permute-start | bytes 221192 | tf_op jit(solution)/shard_map/ppermute | solution.py:176
  34.5 5.3 %collective-permute-start.5 = (f32[144,128]{1,0:T(8,128)S(1)}, f32[144,128]{1,0:T(8,128)S(1)}, u32[]{:S(2)}, u32[]{:S(2)}) collective-permute-start(f32[144,128]{1,0:T(8,128)S(1)} %get-tuple-element.23), channel_id=1, source_target_pairs={{0,12},{4,8},{8,4},{12,0},{16,28},{20,24},{24,20},{28,16},{1,13},{... | collective-permute-start | bytes 221192 | tf_op jit(solution)/shard_map/ppermute | solution.py:176
  39.8 6.5 %collective-permute-start.7 = (f32[48,128]{1,0:T(8,128)S(1)}, f32[48,128]{1,0:T(8,128)S(1)}, u32[]{:S(2)}, u32[]{:S(2)}) collective-permute-start(f32[48,128]{1,0:T(8,128)S(1)} %get-tuple-element.25), channel_id=1, source_target_pairs={{0,2},{1,3},{2,0},{3,1},{4,6},{5,7},{6,4},{7,5},{8,10},{9,11},{10,... | collective-permute-start | bytes 73736 | tf_op jit(solution)/shard_map/ppermute | solution.py:176
  41.4 6.7 %collective-permute-start.8 = (f32[48,128]{1,0:T(8,128)S(1)}, f32[48,128]{1,0:T(8,128)S(1)}, u32[]{:S(2)}, u32[]{:S(2)}) collective-permute-start(f32[48,128]{1,0:T(8,128)S(1)} %get-tuple-element.25), channel_id=1, source_target_pairs={{0,18},{1,19},{2,16},{3,17},{4,22},{5,23},{6,20},{7,21},{8,26},{9,... | collective-permute-start | bytes 73736 | tf_op jit(solution)/shard_map/ppermute | solution.py:229
  43.9 5.5 %collective-permute-start.6 = (f32[96,128]{1,0:T(8,128)S(1)}, f32[96,128]{1,0:T(8,128)S(1)}, u32[]{:S(2)}, u32[]{:S(2)}) collective-permute-start(f32[96,128]{1,0:T(8,128)S(1)} %get-tuple-element.24.ahead), channel_id=1, source_target_pairs={{0,16},{4,20},{8,24},{12,28},{16,0},{20,4},{24,8},{28,12},{1,17},{... | collective-permute-start | bytes 147464 | tf_op jit(solution)/shard_map/ppermute | solution.py:176
  49.8 6.5 %copy-start = (bf16[768,768]{1,0:T(8,128)(2,1)S(1)}, bf16[768,768]{1,0:T(8,128)(2,1)}, u32[]{:S(2)}) copy-start(bf16[768,768]{1,0:T(8,128)(2,1)} %wo.1) | copy-start | bytes 3538948
  49.8 4.3 %collective-permute-start.9 = (bf16[96,128]{1,0:T(8,128)(2,1)S(1)}, bf16[96,128]{1,0:T(8,128)(2,1)S(1)}, u32[]{:S(2)}, u32[]{:S(2)}) collective-permute-start(bf16[96,128]{1,0:T(8,128)(2,1)S(1)} %shard_map.58.p0), channel_id=1, source_target_pairs={{0,4},{4,0},{8,12},{12,8},{16,20},{20,16},{24,28},{28,24},{1,5},{5... | collective-permute-start | bytes 73736 | tf_op jit(solution)/shard_map/ppermute | solution.py:176
  49.9 4.2 %collective-permute-start.10 = (bf16[96,128]{1,0:T(8,128)(2,1)S(1)}, bf16[96,128]{1,0:T(8,128)(2,1)S(1)}, u32[]{:S(2)}, u32[]{:S(2)}) collective-permute-start(bf16[96,128]{1,0:T(8,128)(2,1)S(1)} %shard_map.58.p0), channel_id=1, source_target_pairs={{0,8},{4,12},{8,0},{12,4},{16,24},{20,28},{24,16},{28,20},{1,9},{5... | collective-permute-start | bytes 73736 | tf_op jit(solution)/shard_map/ppermute | solution.py:176
  51.5 4.7 %collective-permute-start.11 = (bf16[96,128]{1,0:T(8,128)(2,1)S(1)}, bf16[96,128]{1,0:T(8,128)(2,1)S(1)}, u32[]{:S(2)}, u32[]{:S(2)}) collective-permute-start(bf16[96,128]{1,0:T(8,128)(2,1)S(1)} %shard_map.58.p0), channel_id=1, source_target_pairs={{0,12},{4,8},{8,4},{12,0},{16,28},{20,24},{24,20},{28,16},{1,13},{... | collective-permute-start | bytes 73736 | tf_op jit(solution)/shard_map/ppermute | solution.py:176

commit v2 on v1

--- a/solution.py
+++ b/solution.py
@@ -44,17 +44,19 @@
     return mixed.reshape(sequence_number, site_number, embed_size)
 
 
-def call(kernel, outs, args, flops=0, scratch=()):
+def call(kernel, outs, args, flops=0, scratch=(), space=pltpu.VMEM):
     shapes = [jax.ShapeDtypeStruct(s, d) for s, d in outs]
+    if space == pltpu.HBM:
+        args = [pltpu.with_memory_space_constraint(a, space) for a in args]
     moved = sum(a.size * a.dtype.itemsize for a in list(args) + shapes)
     return pl.pallas_call(
         kernel,
         out_shape=shapes,
-        in_specs=[pl.BlockSpec(memory_space=pltpu.VMEM)] * len(args),
+        in_specs=[pl.BlockSpec(memory_space=space)] * len(args),
         out_specs=[pl.BlockSpec(memory_space=pltpu.VMEM)] * len(shapes),
         scratch_shapes=list(scratch),
         cost_estimate=pl.CostEstimate(flops=flops, bytes_accessed=moved, transcendentals=0),
-        compiler_params=pltpu.CompilerParams(vmem_limit_bytes=40 * 1024 * 1024),
+        compiler_params=pltpu.CompilerParams(vmem_limit_bytes=4 * 1024 * 1024),
     )(*args)
 
 
@@ -73,53 +75,106 @@
     return lax.dot_general(probe, keys, (((1,), (1,)), ((), ())), preferred_element_type=F32)
 
 
-def kernel_near(rows, sites, width, x_own, x_twin, wq, wk, q_out, k_out, logits_out):
-    q_out[...] = matmul(x_own[...], wq[...])
-    for t, x in enumerate((x_own, x_twin)):
-        k = matmul(x[...], wk[...])
-        for r in range(rows):
-            k_out[r, t * sites : (t + 1) * sites, :] = k[r * sites : (r + 1) * sites, :]
+def places(rows, sites, embed):
+    counts = dict(q=rows * sites, k=2 * rows * sites, v=2 * rows * sites, near=H * sites)
+    counts.update(wq=embed, wk=embed, wv=embed)
+    at, start = {}, 0
+    for name, count in counts.items():
+        at[name] = start
+        start += count
+    return at, start
+
+
+def thirds(x):
+    high = x.astype(BF16)
+    rest = x - high.astype(F32)
+    middle = rest.astype(BF16)
+    return high, middle, (rest - middle.astype(F32)).astype(BF16)
+
+
+def kernel_part(count, other, x, out, sem):
+    place = lax.axis_index("res") // 2
+    start = (1 - place if other else place) * count
+    copy = pltpu.make_async_copy(x.at[pl.ds(start, count)], out, sem)
+    copy.start()
+    copy.wait()
+
+
+def kernel_near(rows, sites, width, own, twin, wq, wk, wv, kept, x_own, x_twin, sems):
+    embed = wq.shape[0]
+    at, _ = places(rows, sites, embed)
+    copies = {}
+    moves = [("own", own, x_own), ("twin", twin, x_twin)]
+    moves += [(n, w, kept.at[pl.ds(at[n], embed)]) for n, w in (("wq", wq), ("wk", wk), ("wv", wv))]
+    for n, (name, source, target) in enumerate(moves):
+        copies[name] = pltpu.make_async_copy(source, target, sems.at[n])
+    for name in ("wq", "own", "wk", "twin", "wv"):
+        copies[name].start()
+    copies["own"].wait()
+    copies["wq"].wait()
+    kept[at["q"] : at["q"] + rows * sites, :] = matmul(x_own[...], kept[at["wq"] : at["wq"] + embed, :])
+    copies["wk"].wait()
+    copies["twin"].wait()
+
+    def both(weight, start):
+        for t, x in enumerate((x_own, x_twin)):
+            y = matmul(x[...], kept[at[weight] : at[weight] + embed, :])
+            for r in range(rows):
+                to = start + (2 * r + t) * sites
+                kept[to : to + sites, :] = y[r * sites : (r + 1) * sites, :]
+
+    both("wk", at["k"])
+    copies["wv"].wait()
+    both("wv", at["v"])
     stack = GROUP * sites
     for g in range(H // GROUP):
         lanes = slice(g * width, (g + 1) * width)
         total = jnp.zeros((stack, 2 * sites), F32)
         for r in range(rows):
-            probe = by_head(q_out[r * sites : (r + 1) * sites, lanes], width // GROUP)
-            total = total + against(probe, k_out[r, :, lanes])
-        logits_out[g * stack : (g + 1) * stack, :] = total
-
-
-def kernel_far(
-    rows, sites, width, x_far, x_far_twin, wq, wk, q_own, k_near, near, *refs
-):
+            q = kept[at["q"] + r * sites : at["q"] + (r + 1) * sites, lanes]
+            k = kept[at["k"] + 2 * r * sites : at["k"] + 2 * (r + 1) * sites, lanes]
+            total = total + against(by_head(q, width // GROUP), k)
+        here = slice(at["near"] + g * stack, at["near"] + (g + 1) * stack)
+        for n, part in enumerate(thirds(total)):
+            kept[here, n * 2 * GROUP * sites : n * 2 * GROUP * sites + 2 * sites] = part
+
+
+def kernel_far(rows, sites, width, x_far, x_far_twin, kept, *refs):
     parts, (far_k, far_q, ahead, back) = refs[:GROUP], refs[GROUP:]
-    half = rows // 2
+    embed, half = x_far.shape[1], rows // 2
+    at, _ = places(rows, sites, embed)
     came = (1 - lax.axis_index("res") // 2) * half
     me = lax.rem(lax.axis_index("seq"), GROUP)
     for t, x in enumerate((x_far, x_far_twin)):
-        k = matmul(x[...], wk[...])
+        k = matmul(x[...], kept[at["wk"] : at["wk"] + embed, :])
         for r in range(half):
             far_k[r, t * sites : (t + 1) * sites, :] = k[r * sites : (r + 1) * sites, :]
-    far_q[...] = matmul(x_far[...], wq[...])
+    far_q[...] = matmul(x_far[...], kept[at["wq"] : at["wq"] + embed, :])
     stack = GROUP * sites
     for g in range(H // GROUP):
         lanes = slice(g * width, (g + 1) * width)
         one = jnp.zeros((stack, 2 * sites), F32)
         two = jnp.zeros((stack, 2 * sites), F32)
         for r in range(half):
-            own = q_own[pl.ds((came + r) * sites, sites), lanes]
+            own = kept[pl.ds(at["q"] + (came + r) * sites, sites), lanes]
             one = one + against(by_head(own, width // GROUP), far_k[r, :, lanes])
             other = far_q[r * sites : (r + 1) * sites, lanes]
-            two = two + against(by_head(other, width // GROUP), k_near[came + r, :, lanes])
+            k = kept[pl.ds(at["k"] + 2 * (came + r) * sites, 2 * sites), lanes]
+            two = two + against(by_head(other, width // GROUP), k)
         rows_g = slice(g * stack, (g + 1) * stack)
-        ahead[rows_g, :] = jnp.concatenate([near[rows_g, :], one], axis=1)
+        here = slice(at["near"] + g * stack, at["near"] + (g + 1) * stack)
+        near = [
+            kept[here, n * 2 * GROUP * sites : n * 2 * GROUP * sites + 2 * sites].astype(F32)
+            for n in range(3)
+        ]
+        ahead[rows_g, :] = jnp.concatenate([near[0] + near[1] + near[2], one], axis=1)
         back[rows_g, :] = two
     size = H * sites // GROUP
     for k in range(GROUP):
-        at = lax.bitwise_xor(me, k) * size
-        parts[k][:size, :] = ahead[pl.ds(at, size), :]
+        to = lax.bitwise_xor(me, k) * size
+        parts[k][:size, :] = ahead[pl.ds(to, size), :]
         parts[k][size:, :] = jnp.concatenate(
-            [back[pl.ds(at, size // 2), :], back[pl.ds(at + size // 2, size // 2), :]], axis=1
+            [back[pl.ds(to, size // 2), :], back[pl.ds(to + size // 2, size // 2), :]], axis=1
         )
 
 
@@ -138,17 +193,17 @@
     out[...] = (e / jnp.sum(e, axis=1, keepdims=True)).astype(BF16)
 
 
-def kernel_values(sites, *refs):
-    w, outs = refs[-1 - (len(refs) - 1) // 3], refs[-((len(refs) - 1) // 3) :]
-    for n, out in enumerate(outs):
-        for t in range(2):
-            v = matmul(refs[2 * n + t][...], w[...])
-            for r in range(out.shape[0]):
-                out[r, t * sites : (t + 1) * sites, :] = v[r * sites : (r + 1) * sites, :]
-
-
-def kernel_last(rows, sites, width, p0, p1, p2, p3, v_near, v_first, v_second, wo, out, probs, att):
+def kernel_values(sites, start, x, x_twin, kept, out):
+    w = kept[start : start + x.shape[1], :]
+    for t, block in enumerate((x, x_twin)):
+        v = matmul(block[...], w)
+        for r in range(out.shape[0]):
+            out[r, t * sites : (t + 1) * sites, :] = v[r * sites : (r + 1) * sites, :]
+
+
+def kernel_last(rows, sites, width, p0, p1, p2, p3, kept, v_first, v_second, wo, out, probs, att):
     half = rows // 2
+    at, _ = places(rows, sites, wo.shape[0])
     place = lax.axis_index("res") // 2
     me = lax.rem(lax.axis_index("seq"), GROUP)
     size = H * sites // GROUP
@@ -160,7 +215,8 @@
         for r in range(half):
             for g in range(H // GROUP):
                 lanes = slice(g * width, (g + 1) * width)
-                v = jnp.concatenate([v_near[start + r, :, lanes], far[r, :, lanes]], axis=0)
+                near = kept[pl.ds(at["v"] + 2 * (start + r) * sites, 2 * sites), lanes]
+                v = jnp.concatenate([near, far[r, :, lanes]], axis=0)
                 full = jnp.dot(
                     probs[g * stack : (g + 1) * stack, :], v, preferred_element_type=F32
                 )
@@ -182,31 +238,41 @@
     n_seq, n_res = lax.axis_size("seq"), lax.axis_size("res")
     scale = 1.0 / math.sqrt(embed // H * rows * n_seq)
     flat, half_flat = (rows * sites, embed), (half * sites, embed)
-    place = lax.axis_index("res") // 2
     own = x.reshape(flat)
     cost = 2 * rows * sites * embed * embed
 
-    sent_first = lax.dynamic_slice_in_dim(own, place * half * sites, half * sites)
+    def part(x, other):
+        return call(
+            functools.partial(kernel_part, half * sites, other),
+            [(half_flat, BF16)],
+            (x,),
+            scratch=[pltpu.SemaphoreType.DMA],
+            space=pltpu.HBM,
+        )[0]
+
+    sent_first = part(own, False)
     far_first = swap(sent_first, "res", 2)
+    later, sent_first = lax.optimization_barrier((own, sent_first))
+    sent_second = part(later, True)
+    far_second = swap(sent_second, "res", 2)
     twin = swap(own, "res", 1)
+    at, total = places(rows, sites, embed)
+    (kept,) = call(
+        functools.partial(kernel_near, rows, sites, width),
+        [((total, embed), BF16)],
+        (own, twin, wq, wk, wv),
+        6 * cost,
+        [pltpu.VMEM(flat, BF16), pltpu.VMEM(flat, BF16), pltpu.SemaphoreType.DMA((5,))],
+        pltpu.HBM,
+    )
+    far_first, kept = lax.optimization_barrier((far_first, kept))
     far_first_twin = swap(far_first, "res", 1)
-    sent_second = lax.dynamic_slice_in_dim(own, (1 - place) * half * sites, half * sites)
-    sent_second, _ = lax.optimization_barrier((sent_second, far_first))
-    far_second = swap(sent_second, "res", 2)
-    far_second_twin = swap(far_second, "res", 1)
-
-    q, k_near, near = call(
-        functools.partial(kernel_near, rows, sites, width),
-        [(flat, BF16), ((rows, 2 * sites, embed), BF16), ((H * sites, 2 * sites), F32)],
-        (own, twin, wq, wk),
-        4 * cost,
-    )
     size = H * sites // GROUP
     part = (size + size // 2, 4 * sites)
     parts = call(
         functools.partial(kernel_far, rows, sites, width),
         [(part, F32)] * GROUP,
-        (far_first, far_first_twin, wq, wk, q, k_near, near),
+        (far_first, far_first_twin, kept),
         2 * cost,
         [
             pltpu.VMEM((half, 2 * sites, embed), BF16),
@@ -227,29 +293,32 @@
         (s * n_res + r, (s ^ GROUP) * n_res + (r ^ 2)) for s in range(n_seq) for r in range(n_res)
     ]
     back_xz = lax.ppermute(back, ("seq", "res"), cross)
+    (v_first,) = call(
+        functools.partial(kernel_values, sites, at["wv"]),
+        [((half, 2 * sites, embed), BF16)],
+        (far_first, far_first_twin, kept),
+        cost,
+    )
+    ahead_z, back_x, back_xz, v_first = lax.optimization_barrier((ahead_z, back_x, back_xz, v_first))
     (probs,) = call(
         functools.partial(kernel_softmax, scale),
         [((size, 4 * sites), BF16)],
         (ahead, ahead_z, back_x, back_xz),
     )
+    far_second, probs = lax.optimization_barrier((far_second, probs))
+    far_second_twin = swap(far_second, "res", 1)
     others = [swap(probs, "seq", k) for k in range(1, GROUP)]
 
-    v_near, v_first = call(
-        functools.partial(kernel_values, sites),
-        [((rows, 2 * sites, embed), BF16), ((half, 2 * sites, embed), BF16)],
-        (own, twin, far_first, far_first_twin, wv),
-        3 * cost,
-    )
     (v_second,) = call(
-        functools.partial(kernel_values, sites),
+        functools.partial(kernel_values, sites, at["wv"]),
         [((half, 2 * sites, embed), BF16)],
-        (far_second, far_second_twin, wv),
+        (far_second, far_second_twin, kept),
         cost,
     )
     (out,) = call(
         functools.partial(kernel_last, rows, sites, width),
         [(flat, BF16)],
-        (probs, *others, v_near, v_first, v_second, wo),
+        (probs, *others, kept, v_first, v_second, wo),
         2 * cost,
         [pltpu.VMEM((H * sites, 4 * sites), BF16), pltpu.VMEM(half_flat, BF16)],
     )

time: 59.2 us -> 45.8 us (0.77)
  waiting for transfers between devices: 27.7 us -> 12.8 us
  Pallas kernels: 11.1 us -> 15.4 us
  local copies, waits for them, and re-layouts: 3.69 us -> 0.89 us
    ppermute x13, waiting for transfers between devices: 26 us -> 11.9 us  [swap(): return lax.ppermute(x, axis, [(i, i ^ bit) for i in range(count)])]
    pallas_call x7 -> x9, Pallas kernels: 11.1 us -> 15.4 us  [call(): pl.pallas_call(kernel, out_shape=shapes, in_specs=[pl.BlockSpec(memory_sp...]
    unnamed x14 -> x4, local copies, waits for them, and re-layouts: 2.42 us -> 0.89 us
    dynamic_slice x1 -> x0, local copies, waits for them, and re-layouts: 1.26 us -> none  [body(): lax.dynamic_slice_in_dim(own, (1 - place) * half * sites, half * sites)]
    ppermute x1, waiting for transfers between devices: 1.76 us -> 0.86 us  [body(): back_xz = lax.ppermute(back, ('seq', 'res'), cross)]
  transfers between devices with their start and end apart: 14 -> 14, of which waited for: 8 -> 9; matrix products, arithmetic and copies ran while one was open for 0% -> 0% of each run, Pallas kernels for 14% -> 28%
where the time goes in v2:
time: 45.8 us; the launch traced here: 45.6 us
  starting transfers between devices  16.4 us (36%)
  Pallas kernels  15.4 us (34%)
  waiting for transfers between devices  12.8 us (28%)
  local copies, waits for them, and re-layouts  0.89 us (2%)
    pallas_call x9, Pallas kernels, call(): pl.pallas_call(kernel, out_shape=shapes, in_specs=[pl.BlockSpec(memory_sp...  15.4 us
    ppermute x13, starting transfers between devices, swap(): return lax.ppermute(x, axis, [(i, i ^ bit) for i in range(count)])  13.7 us
    ppermute x13, waiting for transfers between devices, swap(): return lax.ppermute(x, axis, [(i, i ^ bit) for i in range(count)])  11.9 us
    ppermute x1, starting transfers between devices, body(): back_xz = lax.ppermute(back, ('seq', 'res'), cross)  2.73 us
  transfers between devices with their start and end apart: 14, of which 9 were waited for; matrix products, arithmetic and copies ran while one was open for 0% of the time, Pallas kernels for 28%

profile of v2, /device:TPU:0, one launch (start us, length us, event | category | flops | bytes accessed | tf_op | source)
XLA Modules:
  0.0 45.6 jit_solution(13700662348431387211)
XLA Ops:
  0.5 1.0 %shard_map.55 = bf16[256,768]{1,0:T(8,128)(2,1)S(1)} custom-call(bf16[512,768]{1,0:T(8,128)(2,1)} %bitcast.3), custom_call_target="tpu_custom_call" | custom-call | bytes 1179648 | tf_op jit(solution)/shard_map/pallas_call | solution.py:52
  1.5 2.6 %collective-permute-start.1 = (bf16[256,768]{1,0:T(8,128)(2,1)S(1)}, bf16[256,768]{1,0:T(8,128)(2,1)S(1)}, u32[]{:S(2)}, u32[]{:S(2)}) collective-permute-start(bf16[256,768]{1,0:T(8,128)(2,1)S(1)} %shard_map.55), channel_id=1, source_target_pairs={{0,2},{1,3},{2,0},{3,1},{4,6},{5,7},{6,4},{7,5},{8,10},{9,11},{10,... | collective-permute-start | bytes 1179656 | tf_op jit(solution)/shard_map/ppermute | solution.py:232
  4.0 0.9 %copy-done.1 = bf16[512,768]{1,0:T(8,128)(2,1)} copy-done((bf16[512,768]{1,0:T(8,128)(2,1)}, bf16[512,768]{1,0:T(8,128)(2,1)S(1)}, u32[]{:S(2)}) %copy-start.1) | copy-done | bytes 786456
  4.9 6.4 %shard_map.57.kept = bf16[5248,768]{1,0:T(8,128)(2,1)S(1)} custom-call(bf16[512,768]{1,0:T(8,128)(2,1)} %bitcast.4, bf16[512,768]{1,0:T(8,128)(2,1)} %copy-done.1, bf16[768,768]{1,0:T(8,128)(2,1)} %wq.1, bf16[768,768]{1,0:T(8,128)(2,1)} %wk.1, bf16[768,768]{1,0:T(8,128)(2,1)} %wv.1), custom_call_target="tpu_custom_call" | custom-call | flops 3623878656 | bytes 13172736 | tf_op jit(solution)/shard_map/pallas_call | solution.py:52
  11.3 2.5 %collective-permute-done.1.x_far.x = bf16[256,768]{1,0:T(8,128)(2,1)S(1)} collective-permute-done((bf16[256,768]{1,0:T(8,128)(2,1)S(1)}, bf16[256,768]{1,0:T(8,128)(2,1)S(1)}, u32[]{:S(2)}, u32[]{:S(2)}) %collective-permute-start.1) | collective-permute-done | bytes 393248 | tf_op jit(solution)/shard_map/ppermute | solution.py:232
  13.8 1.0 %shard_map.56 = bf16[256,768]{1,0:T(8,128)(2,1)S(1)} custom-call(bf16[512,768]{1,0:T(8,128)(2,1)} %bitcast.5), custom_call_target="tpu_custom_call" | custom-call | bytes 1179648 | tf_op jit(solution)/shard_map/pallas_call | solution.py:52
  14.8 1.8 %collective-permute-start = (bf16[256,768]{1,0:T(8,128)(2,1)S(1)}, bf16[256,768]{1,0:T(8,128)(2,1)S(1)}, u32[]{:S(2)}, u32[]{:S(2)}) collective-permute-start(bf16[256,768]{1,0:T(8,128)(2,1)S(1)} %shard_map.56), channel_id=1, source_target_pairs={{0,2},{1,3},{2,0},{3,1},{4,6},{5,7},{6,4},{7,5},{8,10},{9,11},{10,... | collective-permute-start | bytes 1179656 | tf_op jit(solution)/shard_map/ppermute | solution.py:232
  16.6 2.3 %shard_map.58 = (f32[144,128]{1,0:T(8,128)S(1)}, f32[144,128]{1,0:T(8,128)S(1)}, f32[144,128]{1,0:T(8,128)S(1)}, f32[144,128]{1,0:T(8,128)S(1)}) custom-call(bf16[256,768]{1,0:T(8,128)(2,1)S(1)} %collective-permute-done.1.x_far.x, bf16[256,768]{1,0:T(8,128)(2,1)S(1)} %collective-permute-done.3.x_far_twin.x_twin, bf16[5248,768]{1,0:T(8,128)(2,1)S(1)} %shard_map.57.kept), custom_call_target="tpu_custom_call" | custom-call | flops 1207959552 | bytes 9142272 | tf_op jit(solution)/shard_map/pallas_call | solution.py:52
  19.0 1.6 %collective-permute-start.4 = (f32[144,128]{1,0:T(8,128)S(1)}, f32[144,128]{1,0:T(8,128)S(1)}, u32[]{:S(2)}, u32[]{:S(2)}) collective-permute-start(f32[144,128]{1,0:T(8,128)S(1)} %get-tuple-element.24), channel_id=1, source_target_pairs={{0,4},{4,0},{8,12},{12,8},{16,20},{20,16},{24,28},{28,24},{1,5},{5... | collective-permute-start | bytes 221192 | tf_op jit(solution)/shard_map/ppermute | solution.py:232
  20.6 1.6 %collective-permute-start.5 = (f32[144,128]{1,0:T(8,128)S(1)}, f32[144,128]{1,0:T(8,128)S(1)}, u32[]{:S(2)}, u32[]{:S(2)}) collective-permute-start(f32[144,128]{1,0:T(8,128)S(1)} %get-tuple-element.25), channel_id=1, source_target_pairs={{0,8},{4,12},{8,0},{12,4},{16,24},{20,28},{24,16},{28,20},{1,9},{5... | collective-permute-start | bytes 221192 | tf_op jit(solution)/shard_map/ppermute | solution.py:232
  22.5 0.9 %collective-permute-done.4.b = f32[144,128]{1,0:T(8,128)S(1)} collective-permute-done((f32[144,128]{1,0:T(8,128)S(1)}, f32[144,128]{1,0:T(8,128)S(1)}, u32[]{:S(2)}, u32[]{:S(2)}) %collective-permute-start.4) | collective-permute-done | bytes 73760 | tf_op jit(solution)/shard_map/ppermute | solution.py:232
  23.4 2.0 %collective-permute-done.5.c = f32[144,128]{1,0:T(8,128)S(1)} collective-permute-done((f32[144,128]{1,0:T(8,128)S(1)}, f32[144,128]{1,0:T(8,128)S(1)}, u32[]{:S(2)}, u32[]{:S(2)}) %collective-permute-start.5) | collective-permute-done | bytes 73760 | tf_op jit(solution)/shard_map/ppermute | solution.py:232
  25.5 1.9 %collective-permute-done.6.d = f32[144,128]{1,0:T(8,128)S(1)} collective-permute-done((f32[144,128]{1,0:T(8,128)S(1)}, f32[144,128]{1,0:T(8,128)S(1)}, u32[]{:S(2)}, u32[]{:S(2)}) %collective-permute-start.6) | collective-permute-done | bytes 73760 | tf_op jit(solution)/shard_map/ppermute | solution.py:232
  27.4 2.7 %collective-permute-start.9 = (f32[48,128]{1,0:T(8,128)S(1)}, f32[48,128]{1,0:T(8,128)S(1)}, u32[]{:S(2)}, u32[]{:S(2)}) collective-permute-start(f32[48,128]{1,0:T(8,128)S(1)} %get-tuple-element.28), channel_id=1, source_target_pairs={{0,18},{1,19},{2,16},{3,17},{4,22},{5,23},{6,20},{7,21},{8,26},{9,... | collective-permute-start | bytes 73736 | tf_op jit(solution)/shard_map/ppermute | solution.py:295
  30.1 1.4 %collective-permute-start.8 = (f32[48,128]{1,0:T(8,128)S(1)}, f32[48,128]{1,0:T(8,128)S(1)}, u32[]{:S(2)}, u32[]{:S(2)}) collective-permute-start(f32[48,128]{1,0:T(8,128)S(1)} %get-tuple-element.28), channel_id=1, source_target_pairs={{0,2},{1,3},{2,0},{3,1},{4,6},{5,7},{6,4},{7,5},{8,10},{9,11},{10,... | collective-permute-start | bytes 73736 | tf_op jit(solution)/shard_map/ppermute | solution.py:232
  31.9 0.8 %shard_map.60.v_first = bf16[8,64,768]{2,1,0:T(8,128)(2,1)S(1)} custom-call(bf16[256,768]{1,0:T(8,128)(2,1)S(1)} %collective-permute-done.1.x_far.x, bf16[256,768]{1,0:T(8,128)(2,1)S(1)} %collective-permute-done.3.x_far_twin.x_twin, bf16[5248,768]{1,0:T(8,128)(2,1)S(1)} %shard_map.57.kept), custom_call_target="tpu_custom_call" | custom-call | flops 603979776 | bytes 9633792 | tf_op jit(solution)/shard_map/pallas_call | solution.py:52
  32.6 0.9 %collective-permute-done.9.back_xz = f32[48,128]{1,0:T(8,128)S(1)} collective-permute-done((f32[48,128]{1,0:T(8,128)S(1)}, f32[48,128]{1,0:T(8,128)S(1)}, u32[]{:S(2)}, u32[]{:S(2)}) %collective-permute-start.9) | collective-permute-done | bytes 24608 | tf_op jit(solution)/shard_map/ppermute | solution.py:295
  34.0 3.1 %collective-permute-done.7.ahead_z = f32[96,128]{1,0:T(8,128)S(1)} collective-permute-done((f32[96,128]{1,0:T(8,128)S(1)}, f32[96,128]{1,0:T(8,128)S(1)}, u32[]{:S(2)}, u32[]{:S(2)}) %collective-permute-start.7) | collective-permute-done | bytes 49184 | tf_op jit(solution)/shard_map/ppermute | solution.py:232
  37.5 0.9 %collective-permute-start.12 = (bf16[96,128]{1,0:T(8,128)(2,1)S(1)}, bf16[96,128]{1,0:T(8,128)(2,1)S(1)}, u32[]{:S(2)}, u32[]{:S(2)}) collective-permute-start(bf16[96,128]{1,0:T(8,128)(2,1)S(1)} %shard_map.61.p0), channel_id=1, source_target_pairs={{0,12},{4,8},{8,4},{12,0},{16,28},{20,24},{24,20},{28,16},{1,13},{... | collective-permute-start | bytes 73736 | tf_op jit(solution)/shard_map/ppermute | solution.py:232
  38.3 0.7 %collective-permute-start.11 = (bf16[96,128]{1,0:T(8,128)(2,1)S(1)}, bf16[96,128]{1,0:T(8,128)(2,1)S(1)}, u32[]{:S(2)}, u32[]{:S(2)}) collective-permute-start(bf16[96,128]{1,0:T(8,128)(2,1)S(1)} %shard_map.61.p0), channel_id=1, source_target_pairs={{0,8},{4,12},{8,0},{12,4},{16,24},{20,28},{24,16},{28,20},{1,9},{5... | collective-permute-start | bytes 73736 | tf_op jit(solution)/shard_map/ppermute | solution.py:232
  39.0 2.0 %collective-permute-start.10 = (bf16[96,128]{1,0:T(8,128)(2,1)S(1)}, bf16[96,128]{1,0:T(8,128)(2,1)S(1)}, u32[]{:S(2)}, u32[]{:S(2)}) collective-permute-start(bf16[96,128]{1,0:T(8,128)(2,1)S(1)} %shard_map.61.p0), channel_id=1, source_target_pairs={{0,4},{4,0},{8,12},{12,8},{16,20},{20,16},{24,28},{28,24},{1,5},{5... | collective-permute-start | bytes 73736 | tf_op jit(solution)/shard_map/ppermute | solution.py:232
  41.0 0.8 %shard_map.62.v_second = bf16[8,64,768]{2,1,0:T(8,128)(2,1)S(1)} custom-call(bf16[256,768]{1,0:T(8,128)(2,1)S(1)} %collective-permute-done.x, bf16[256,768]{1,0:T(8,128)(2,1)S(1)} %collective-permute-done.13.x_twin, bf16[5248,768]{1,0:T(8,128)(2,1)S(1)} %shard_map.57.kept), custom_call_target="tpu_custom_call" | custom-call | flops 603979776 | bytes 9633792 | tf_op jit(solution)/shard_map/pallas_call | solution.py:52
  42.3 0.6 %collective-permute-done.10.p1 = bf16[96,128]{1,0:T(8,128)(2,1)S(1)} collective-permute-done((bf16[96,128]{1,0:T(8,128)(2,1)S(1)}, bf16[96,128]{1,0:T(8,128)(2,1)S(1)}, u32[]{:S(2)}, u32[]{:S(2)}) %collective-permute-start.10) | collective-permute-done | bytes 24608 | tf_op jit(solution)/shard_map/ppermute | solution.py:232
  42.9 2.7 %shard_map.63 = bf16[512,768]{1,0:T(8,128)(2,1)} custom-call(bf16[96,128]{1,0:T(8,128)(2,1)S(1)} %shard_map.61.p0, bf16[96,128]{1,0:T(8,128)(2,1)S(1)} %collective-permute-done.10.p1, bf16[96,128]{1,0:T(8,128)(2,1)S(1)} %collective-permute-done.11.p2, bf16[96,128]{1,0:T(8,128)(2,1)S(1)} %collective-permute-done.12.p3, bf16[5248,768]{1,0:T(8,128)(2,1)S(1)} %shard_map.57.kept, ...), custom_call_target="tpu_custom_call" | custom-call | flops 1207959552 | bytes 11698176 | tf_op jit(solution)/shard_map/pallas_call | solution.py:52
  (17 shorter events, 2.5 us)
Async XLA Ops:
  0.0 4.0 %collective-permute-start.2 = (bf16[512,768]{1,0:T(8,128)(2,1)}, bf16[512,768]{1,0:T(8,128)(2,1)S(1)}, u32[]{:S(2)}, u32[]{:S(2)}) collective-permute-start(bf16[512,768]{1,0:T(8,128)(2,1)} %bitcast.2), channel_id=1, source_target_pairs={{0,1},{1,0},{2,3},{3,2},{4,5},{5,4},{6,7},{7,6},{8,9},{9,8},{10,11... | collective-permute-start | bytes 2359304 | tf_op jit(solution)/shard_map/ppermute | solution.py:232
  1.5 12.3 %collective-permute-start.1 = (bf16[256,768]{1,0:T(8,128)(2,1)S(1)}, bf16[256,768]{1,0:T(8,128)(2,1)S(1)}, u32[]{:S(2)}, u32[]{:S(2)}) collective-permute-start(bf16[256,768]{1,0:T(8,128)(2,1)S(1)} %shard_map.55), channel_id=1, source_target_pairs={{0,2},{1,3},{2,0},{3,1},{4,6},{5,7},{6,4},{7,5},{8,10},{9,11},{10,... | collective-permute-start | bytes 1179656 | tf_op jit(solution)/shard_map/ppermute | solution.py:232
  4.0 0.9 %copy-start.1 = (bf16[512,768]{1,0:T(8,128)(2,1)}, bf16[512,768]{1,0:T(8,128)(2,1)S(1)}, u32[]{:S(2)}) copy-start(bf16[512,768]{1,0:T(8,128)(2,1)S(1)} %collective-permute-done.2.twin) | copy-start | bytes 2359300
  13.8 2.8 %collective-permute-start.3 = (bf16[256,768]{1,0:T(8,128)(2,1)S(1)}, bf16[256,768]{1,0:T(8,128)(2,1)S(1)}, u32[]{:S(2)}, u32[]{:S(2)}) collective-permute-start(bf16[256,768]{1,0:T(8,128)(2,1)S(1)} %collective-permute-done.1.x_far.x), channel_id=1, source_target_pairs={{0,1},{1,0},{2,3},{3,2},{4,5},{5,4},{6,7},{7,6},{8,9},{9,8},{10,11... | collective-permute-start | bytes 1179656 | tf_op jit(solution)/shard_map/ppermute | solution.py:232
  14.8 22.5 %collective-permute-start = (bf16[256,768]{1,0:T(8,128)(2,1)S(1)}, bf16[256,768]{1,0:T(8,128)(2,1)S(1)}, u32[]{:S(2)}, u32[]{:S(2)}) collective-permute-start(bf16[256,768]{1,0:T(8,128)(2,1)S(1)} %shard_map.56), channel_id=1, source_target_pairs={{0,2},{1,3},{2,0},{3,1},{4,6},{5,7},{6,4},{7,5},{8,10},{9,11},{10,... | collective-permute-start | bytes 1179656 | tf_op jit(solution)/shard_map/ppermute | solution.py:232
  19.0 4.5 %collective-permute-start.4 = (f32[144,128]{1,0:T(8,128)S(1)}, f32[144,128]{1,0:T(8,128)S(1)}, u32[]{:S(2)}, u32[]{:S(2)}) collective-permute-start(f32[144,128]{1,0:T(8,128)S(1)} %get-tuple-element.24), channel_id=1, source_target_pairs={{0,4},{4,0},{8,12},{12,8},{16,20},{20,16},{24,28},{28,24},{1,5},{5... | collective-permute-start | bytes 221192 | tf_op jit(solution)/shard_map/ppermute | solution.py:232
  20.6 4.9 %collective-permute-start.5 = (f32[144,128]{1,0:T(8,128)S(1)}, f32[144,128]{1,0:T(8,128)S(1)}, u32[]{:S(2)}, u32[]{:S(2)}) collective-permute-start(f32[144,128]{1,0:T(8,128)S(1)} %get-tuple-element.25), channel_id=1, source_target_pairs={{0,8},{4,12},{8,0},{12,4},{16,24},{20,28},{24,16},{28,20},{1,9},{5... | collective-permute-start | bytes 221192 | tf_op jit(solution)/shard_map/ppermute | solution.py:232
  22.1 5.3 %collective-permute-start.6 = (f32[144,128]{1,0:T(8,128)S(1)}, f32[144,128]{1,0:T(8,128)S(1)}, u32[]{:S(2)}, u32[]{:S(2)}) collective-permute-start(f32[144,128]{1,0:T(8,128)S(1)} %get-tuple-element.26), channel_id=1, source_target_pairs={{0,12},{4,8},{8,4},{12,0},{16,28},{20,24},{24,20},{28,16},{1,13},{... | collective-permute-start | bytes 221192 | tf_op jit(solution)/shard_map/ppermute | solution.py:232
  27.4 6.1 %collective-permute-start.9 = (f32[48,128]{1,0:T(8,128)S(1)}, f32[48,128]{1,0:T(8,128)S(1)}, u32[]{:S(2)}, u32[]{:S(2)}) collective-permute-start(f32[48,128]{1,0:T(8,128)S(1)} %get-tuple-element.28), channel_id=1, source_target_pairs={{0,18},{1,19},{2,16},{3,17},{4,22},{5,23},{6,20},{7,21},{8,26},{9,... | collective-permute-start | bytes 73736 | tf_op jit(solution)/shard_map/ppermute | solution.py:295
  30.1 3.8 %collective-permute-start.8 = (f32[48,128]{1,0:T(8,128)S(1)}, f32[48,128]{1,0:T(8,128)S(1)}, u32[]{:S(2)}, u32[]{:S(2)}) collective-permute-start(f32[48,128]{1,0:T(8,128)S(1)} %get-tuple-element.28), channel_id=1, source_target_pairs={{0,2},{1,3},{2,0},{3,1},{4,6},{5,7},{6,4},{7,5},{8,10},{9,11},{10,... | collective-permute-start | bytes 73736 | tf_op jit(solution)/shard_map/ppermute | solution.py:232
  31.5 5.5 %collective-permute-start.7 = (f32[96,128]{1,0:T(8,128)S(1)}, f32[96,128]{1,0:T(8,128)S(1)}, u32[]{:S(2)}, u32[]{:S(2)}) collective-permute-start(f32[96,128]{1,0:T(8,128)S(1)} %get-tuple-element.27.ahead), channel_id=1, source_target_pairs={{0,16},{4,20},{8,24},{12,28},{16,0},{20,4},{24,8},{28,12},{1,17},{... | collective-permute-start | bytes 147464 | tf_op jit(solution)/shard_map/ppermute | solution.py:232
  37.4 5.5 %copy-start = (bf16[768,768]{1,0:T(8,128)(2,1)S(1)}, bf16[768,768]{1,0:T(8,128)(2,1)}, u32[]{:S(2)}) copy-start(bf16[768,768]{1,0:T(8,128)(2,1)} %wo.1) | copy-start | bytes 3538948
  37.4 3.6 %collective-permute-start.13 = (bf16[256,768]{1,0:T(8,128)(2,1)S(1)}, bf16[256,768]{1,0:T(8,128)(2,1)S(1)}, u32[]{:S(2)}, u32[]{:S(2)}) collective-permute-start(bf16[256,768]{1,0:T(8,128)(2,1)S(1)} %collective-permute-done.x), channel_id=1, source_target_pairs={{0,1},{1,0},{2,3},{3,2},{4,5},{5,4},{6,7},{7,6},{8,9},{9,8},{10,11... | collective-permute-start | bytes 1179656 | tf_op jit(solution)/shard_map/ppermute | solution.py:232
  37.5 4.8 %collective-permute-start.12 = (bf16[96,128]{1,0:T(8,128)(2,1)S(1)}, bf16[96,128]{1,0:T(8,128)(2,1)S(1)}, u32[]{:S(2)}, u32[]{:S(2)}) collective-permute-start(bf16[96,128]{1,0:T(8,128)(2,1)S(1)} %shard_map.61.p0), channel_id=1, source_target_pairs={{0,12},{4,8},{8,4},{12,0},{16,28},{20,24},{24,20},{28,16},{1,13},{... | collective-permute-start | bytes 73736 | tf_op jit(solution)/shard_map/ppermute | solution.py:232
  38.3 3.9 %collective-permute-start.11 = (bf16[96,128]{1,0:T(8,128)(2,1)S(1)}, bf16[96,128]{1,0:T(8,128)(2,1)S(1)}, u32[]{:S(2)}, u32[]{:S(2)}) collective-permute-start(bf16[96,128]{1,0:T(8,128)(2,1)S(1)} %shard_map.61.p0), channel_id=1, source_target_pairs={{0,8},{4,12},{8,0},{12,4},{16,24},{20,28},{24,16},{28,20},{1,9},{5... | collective-permute-start | bytes 73736 | tf_op jit(solution)/shard_map/ppermute | solution.py:232
  39.0 3.8 %collective-permute-start.10 = (bf16[96,128]{1,0:T(8,128)(2,1)S(1)}, bf16[96,128]{1,0:T(8,128)(2,1)S(1)}, u32[]{:S(2)}, u32[]{:S(2)}) collective-permute-start(bf16[96,128]{1,0:T(8,128)(2,1)S(1)} %shard_map.61.p0), channel_id=1, source_target_pairs={{0,4},{4,0},{8,12},{12,8},{16,20},{20,16},{24,28},{28,24},{1,5},{5... | collective-permute-start | bytes 73736 | tf_op jit(solution)/shard_map/ppermute | solution.py:232

commit v3 on v2

--- a/solution.py
+++ b/solution.py
@@ -139,36 +139,46 @@
             kept[here, n * 2 * GROUP * sites : n * 2 * GROUP * sites + 2 * sites] = part
 
 
-def kernel_far(rows, sites, width, x_far, x_far_twin, kept, *refs):
-    parts, (far_k, far_q, ahead, back) = refs[:GROUP], refs[GROUP:]
+def kernel_back(rows, sites, width, x_far, kept, k_far, back, far_q):
     embed, half = x_far.shape[1], rows // 2
     at, _ = places(rows, sites, embed)
     came = (1 - lax.axis_index("res") // 2) * half
+    far_q[...] = matmul(x_far[...], kept[at["wq"] : at["wq"] + embed, :])
+    k_far[...] = matmul(x_far[...], kept[at["wk"] : at["wk"] + embed, :])
+    stack = GROUP * sites
+    for g in range(H // GROUP):
+        lanes = slice(g * width, (g + 1) * width)
+        two = jnp.zeros((stack, 2 * sites), F32)
+        for r in range(half):
+            other = far_q[r * sites : (r + 1) * sites, lanes]
+            k = kept[pl.ds(at["k"] + 2 * (came + r) * sites, 2 * sites), lanes]
+            two = two + against(by_head(other, width // GROUP), k)
+        back[g * stack : (g + 1) * stack, :] = two
+
+
+def kernel_ahead(rows, sites, width, x_far_twin, kept, k_far, back, *refs):
+    parts, (far_k, ahead) = refs[:GROUP], refs[GROUP:]
+    embed, half = x_far_twin.shape[1], rows // 2
+    at, _ = places(rows, sites, embed)
+    came = (1 - lax.axis_index("res") // 2) * half
     me = lax.rem(lax.axis_index("seq"), GROUP)
-    for t, x in enumerate((x_far, x_far_twin)):
-        k = matmul(x[...], kept[at["wk"] : at["wk"] + embed, :])
-        for r in range(half):
-            far_k[r, t * sites : (t + 1) * sites, :] = k[r * sites : (r + 1) * sites, :]
-    far_q[...] = matmul(x_far[...], kept[at["wq"] : at["wq"] + embed, :])
+    far_k[...] = matmul(x_far_twin[...], kept[at["wk"] : at["wk"] + embed, :])
     stack = GROUP * sites
     for g in range(H // GROUP):
         lanes = slice(g * width, (g + 1) * width)
         one = jnp.zeros((stack, 2 * sites), F32)
-        two = jnp.zeros((stack, 2 * sites), F32)
         for r in range(half):
             own = kept[pl.ds(at["q"] + (came + r) * sites, sites), lanes]
-            one = one + against(by_head(own, width // GROUP), far_k[r, :, lanes])
-            other = far_q[r * sites : (r + 1) * sites, lanes]
-            k = kept[pl.ds(at["k"] + 2 * (came + r) * sites, 2 * sites), lanes]
-            two = two + against(by_head(other, width // GROUP), k)
-        rows_g = slice(g * stack, (g + 1) * stack)
+            row = slice(r * sites, (r + 1) * sites)
+            k = jnp.concatenate([k_far[row, lanes], far_k[row, lanes]], axis=0)
+            one = one + against(by_head(own, width // GROUP), k)
         here = slice(at["near"] + g * stack, at["near"] + (g + 1) * stack)
         near = [
-            kept[here, n * 2 * GROUP * sites : n * 2 * GROUP * sites + 2 * sites].astype(F32)
-            for n in range(3)
+            kept[here, n * 2 * stack : n * 2 * stack + 2 * sites].astype(F32) for n in range(3)
         ]
-        ahead[rows_g, :] = jnp.concatenate([near[0] + near[1] + near[2], one], axis=1)
-        back[rows_g, :] = two
+        ahead[g * stack : (g + 1) * stack, :] = jnp.concatenate(
+            [near[0] + near[1] + near[2], one], axis=1
+        )
     size = H * sites // GROUP
     for k in range(GROUP):
         to = lax.bitwise_xor(me, k) * size
@@ -252,10 +262,8 @@
 
     sent_first = part(own, False)
     far_first = swap(sent_first, "res", 2)
-    later, sent_first = lax.optimization_barrier((own, sent_first))
-    sent_second = part(later, True)
-    far_second = swap(sent_second, "res", 2)
-    twin = swap(own, "res", 1)
+    mine, sent_first = lax.optimization_barrier((own, sent_first))
+    twin = swap(mine, "res", 1)
     at, total = places(rows, sites, embed)
     (kept,) = call(
         functools.partial(kernel_near, rows, sites, width),
@@ -265,23 +273,38 @@
         [pltpu.VMEM(flat, BF16), pltpu.VMEM(flat, BF16), pltpu.SemaphoreType.DMA((5,))],
         pltpu.HBM,
     )
-    far_first, kept = lax.optimization_barrier((far_first, kept))
+    later, kept = lax.optimization_barrier((own, kept))
+    sent_second = part(later, True)
+    far_second = swap(sent_second, "res", 2)
+    far_first, kept, sent_second = lax.optimization_barrier((far_first, kept, sent_second))
     far_first_twin = swap(far_first, "res", 1)
+    sums = ((H * sites, 2 * sites), F32)
+    k_far, back = call(
+        functools.partial(kernel_back, rows, sites, width),
+        [(half_flat, BF16), sums],
+        (far_first, kept),
+        cost,
+        [pltpu.VMEM(half_flat, BF16)],
+    )
+    far_first_twin, k_far = lax.optimization_barrier((far_first_twin, k_far))
     size = H * sites // GROUP
-    part = (size + size // 2, 4 * sites)
+    part_shape = (size + size // 2, 4 * sites)
     parts = call(
-        functools.partial(kernel_far, rows, sites, width),
-        [(part, F32)] * GROUP,
+        functools.partial(kernel_ahead, rows, sites, width),
+        [(part_shape, F32)] * GROUP,
+        (far_first_twin, kept, k_far, back),
+        cost,
+        [pltpu.VMEM(half_flat, BF16), pltpu.VMEM((H * sites, 4 * sites), F32)],
+    )
+    came = [swap(parts[k], "seq", k) for k in range(1, GROUP)]
+    came[0], kept = lax.optimization_barrier((came[0], kept))
+    (v_first,) = call(
+        functools.partial(kernel_values, sites, at["wv"]),
+        [((half, 2 * sites, embed), BF16)],
         (far_first, far_first_twin, kept),
-        2 * cost,
-        [
-            pltpu.VMEM((half, 2 * sites, embed), BF16),
-            pltpu.VMEM(half_flat, BF16),
-            pltpu.VMEM((H * sites, 4 * sites), F32),
-            pltpu.VMEM((H * sites, 2 * sites), F32),
-        ],
-    )
-    came = [swap(parts[k], "seq", k) for k in range(1, GROUP)]
+        cost,
+    )
+    came[1], v_first = lax.optimization_barrier((came[1], v_first))
     ahead, back = call(
         functools.partial(kernel_sum, size),
         [((size, 4 * sites), F32), ((size // 2, 4 * sites), F32)],
@@ -293,13 +316,6 @@
         (s * n_res + r, (s ^ GROUP) * n_res + (r ^ 2)) for s in range(n_seq) for r in range(n_res)
     ]
     back_xz = lax.ppermute(back, ("seq", "res"), cross)
-    (v_first,) = call(
-        functools.partial(kernel_values, sites, at["wv"]),
-        [((half, 2 * sites, embed), BF16)],
-        (far_first, far_first_twin, kept),
-        cost,
-    )
-    ahead_z, back_x, back_xz, v_first = lax.optimization_barrier((ahead_z, back_x, back_xz, v_first))
     (probs,) = call(
         functools.partial(kernel_softmax, scale),
         [((size, 4 * sites), BF16)],

time: 45.8 us -> 44 us (0.961)
  waiting for transfers between devices: 12.8 us -> 10.9 us
    ppermute x13, waiting for transfers between devices: 11.9 us -> 6.84 us  [swap(): return lax.ppermute(x, axis, [(i, i ^ bit) for i in range(count)])]
    ppermute x1, waiting for transfers between devices: 0.86 us -> 4.09 us  [body(): back_xz = lax.ppermute(back, ('seq', 'res'), cross)]
    ppermute x1, starting transfers between devices: 2.73 us -> 0.31 us  [body(): back_xz = lax.ppermute(back, ('seq', 'res'), cross)]
    ppermute x13, starting transfers between devices: 13.7 us -> 16 us  [swap(): return lax.ppermute(x, axis, [(i, i ^ bit) for i in range(count)])]
    unnamed x4 -> x6, local copies, waits for them, and re-layouts: 0.89 us -> 1.05 us
    pallas_call x9 -> x10, Pallas kernels: 15.4 us -> 15.4 us  [call(): pl.pallas_call(kernel, out_shape=shapes, in_specs=[pl.BlockSpec(memory_sp...]
  transfers between devices with their start and end apart: 14 -> 14, of which waited for: 9 -> 8; matrix products, arithmetic and copies ran while one was open for 0% -> 0% of each run, Pallas kernels for 28% -> 26%
where the time goes in v3:
time: 44 us; the launch traced here: 43.8 us
  starting transfers between devices  16.3 us (37%)
  Pallas kernels  15.4 us (35%)
  waiting for transfers between devices  10.9 us (25%)
  local copies, waits for them, and re-layouts  1.05 us (2%)
    ppermute x13, starting transfers between devices, swap(): return lax.ppermute(x, axis, [(i, i ^ bit) for i in range(count)])  16 us
    pallas_call x10, Pallas kernels, call(): pl.pallas_call(kernel, out_shape=shapes, in_specs=[pl.BlockSpec(memory_sp...  15.4 us
    ppermute x13, waiting for transfers between devices, swap(): return lax.ppermute(x, axis, [(i, i ^ bit) for i in range(count)])  6.84 us
    ppermute x1, waiting for transfers between devices, body(): back_xz = lax.ppermute(back, ('seq', 'res'), cross)  4.09 us
    unnamed x6, local copies, waits for them, and re-layouts  1.05 us
  transfers between devices with their start and end apart: 14, of which 8 were waited for; matrix products, arithmetic and copies ran while one was open for 0% of the time, Pallas kernels for 26%

profile of v3, /device:TPU:0, one launch (start us, length us, event | category | flops | bytes accessed | tf_op | source)
XLA Modules:
  0.0 43.8 jit_solution(5565718006262611083)
XLA Ops:
  0.0 1.1 %shard_map.55 = bf16[256,768]{1,0:T(8,128)(2,1)S(1)} custom-call(bf16[512,768]{1,0:T(8,128)(2,1)} %bitcast.2), custom_call_target="tpu_custom_call" | custom-call | bytes 1179648 | tf_op jit(solution)/shard_map/pallas_call | solution.py:52
  1.7 2.5 %collective-permute-start.2 = (bf16[256,768]{1,0:T(8,128)(2,1)S(1)}, bf16[256,768]{1,0:T(8,128)(2,1)S(1)}, u32[]{:S(2)}, u32[]{:S(2)}) collective-permute-start(bf16[256,768]{1,0:T(8,128)(2,1)S(1)} %shard_map.55), channel_id=1, source_target_pairs={{0,2},{1,3},{2,0},{3,1},{4,6},{5,7},{6,4},{7,5},{8,10},{9,11},{10,... | collective-permute-start | bytes 1179656 | tf_op jit(solution)/shard_map/ppermute | solution.py:242
  4.2 0.9 %copy-done.2 = bf16[512,768]{1,0:T(8,128)(2,1)} copy-done((bf16[512,768]{1,0:T(8,128)(2,1)}, bf16[512,768]{1,0:T(8,128)(2,1)S(1)}, u32[]{:S(2)}) %copy-start.2) | copy-done | bytes 786456
  5.1 6.4 %shard_map.56.kept = bf16[5248,768]{1,0:T(8,128)(2,1)S(1)} custom-call(bf16[512,768]{1,0:T(8,128)(2,1)} %bitcast.3, bf16[512,768]{1,0:T(8,128)(2,1)} %copy-done.2, bf16[768,768]{1,0:T(8,128)(2,1)} %wq.1, bf16[768,768]{1,0:T(8,128)(2,1)} %wk.1, bf16[768,768]{1,0:T(8,128)(2,1)} %wv.1), custom_call_target="tpu_custom_call" | custom-call | flops 3623878656 | bytes 13172736 | tf_op jit(solution)/shard_map/pallas_call | solution.py:52
  11.5 1.0 %shard_map.57 = bf16[256,768]{1,0:T(8,128)(2,1)S(1)} custom-call(bf16[512,768]{1,0:T(8,128)(2,1)} %bitcast.4), custom_call_target="tpu_custom_call" | custom-call | bytes 1179648 | tf_op jit(solution)/shard_map/pallas_call | solution.py:52
  12.5 1.4 %collective-permute-done.2.x_far.x = bf16[256,768]{1,0:T(8,128)(2,1)S(1)} collective-permute-done((bf16[256,768]{1,0:T(8,128)(2,1)S(1)}, bf16[256,768]{1,0:T(8,128)(2,1)S(1)}, u32[]{:S(2)}, u32[]{:S(2)}) %collective-permute-start.2) | collective-permute-done | bytes 393248 | tf_op jit(solution)/shard_map/ppermute | solution.py:242
  14.0 1.7 %collective-permute-start.1 = (bf16[256,768]{1,0:T(8,128)(2,1)S(1)}, bf16[256,768]{1,0:T(8,128)(2,1)S(1)}, u32[]{:S(2)}, u32[]{:S(2)}) collective-permute-start(bf16[256,768]{1,0:T(8,128)(2,1)S(1)} %shard_map.57), channel_id=1, source_target_pairs={{0,2},{1,3},{2,0},{3,1},{4,6},{5,7},{6,4},{7,5},{8,10},{9,11},{10,... | collective-permute-start | bytes 1179656 | tf_op jit(solution)/shard_map/ppermute | solution.py:242
  15.7 1.2 %shard_map.58 = (bf16[256,768]{1,0:T(8,128)(2,1)S(1)}, f32[384,64]{1,0:T(8,128)S(1)}) custom-call(bf16[256,768]{1,0:T(8,128)(2,1)S(1)} %collective-permute-done.2.x_far.x, bf16[5248,768]{1,0:T(8,128)(2,1)S(1)} %shard_map.56.kept), custom_call_target="tpu_custom_call" | custom-call | flops 603979776 | bytes 8945664 | tf_op jit(solution)/shard_map/pallas_call | solution.py:52
  16.9 1.1 %shard_map.59 = (f32[144,128]{1,0:T(8,128)S(1)}, f32[144,128]{1,0:T(8,128)S(1)}, f32[144,128]{1,0:T(8,128)S(1)}, f32[144,128]{1,0:T(8,128)S(1)}) custom-call(bf16[256,768]{1,0:T(8,128)(2,1)S(1)} %collective-permute-done.3.x_far_twin.x_twin, bf16[5248,768]{1,0:T(8,128)(2,1)S(1)} %shard_map.56.kept, bf16[256,768]{1,0:T(8,128)(2,1)S(1)} %get-tuple-element.33.k_far, ...), custom_call_target="tpu_custom_call" | custom-call | flops 603979776 | bytes 9240576 | tf_op jit(solution)/shard_map/pallas_call | solution.py:52
  18.0 1.6 %collective-permute-start.4 = (f32[144,128]{1,0:T(8,128)S(1)}, f32[144,128]{1,0:T(8,128)S(1)}, u32[]{:S(2)}, u32[]{:S(2)}) collective-permute-start(f32[144,128]{1,0:T(8,128)S(1)} %get-tuple-element.36), channel_id=1, source_target_pairs={{0,4},{4,0},{8,12},{12,8},{16,20},{20,16},{24,28},{28,24},{1,5},{5... | collective-permute-start | bytes 221192 | tf_op jit(solution)/shard_map/ppermute | solution.py:242
  19.6 1.6 %collective-permute-start.5 = (f32[144,128]{1,0:T(8,128)S(1)}, f32[144,128]{1,0:T(8,128)S(1)}, u32[]{:S(2)}, u32[]{:S(2)}) collective-permute-start(f32[144,128]{1,0:T(8,128)S(1)} %get-tuple-element.38), channel_id=1, source_target_pairs={{0,8},{4,12},{8,0},{12,4},{16,24},{20,28},{24,16},{28,20},{1,9},{5... | collective-permute-start | bytes 221192 | tf_op jit(solution)/shard_map/ppermute | solution.py:242
  21.6 0.9 %collective-permute-done.4.b = f32[144,128]{1,0:T(8,128)S(1)} collective-permute-done((f32[144,128]{1,0:T(8,128)S(1)}, f32[144,128]{1,0:T(8,128)S(1)}, u32[]{:S(2)}, u32[]{:S(2)}) %collective-permute-start.4) | collective-permute-done | bytes 73760 | tf_op jit(solution)/shard_map/ppermute | solution.py:242
  22.5 0.8 %shard_map.60.v_first = bf16[8,64,768]{2,1,0:T(8,128)(2,1)S(1)} custom-call(bf16[256,768]{1,0:T(8,128)(2,1)S(1)} %collective-permute-done.2.x_far.x, bf16[256,768]{1,0:T(8,128)(2,1)S(1)} %collective-permute-done.3.x_far_twin.x_twin, bf16[5248,768]{1,0:T(8,128)(2,1)S(1)} %shard_map.56.kept), custom_call_target="tpu_custom_call" | custom-call | flops 603979776 | bytes 9633792 | tf_op jit(solution)/shard_map/pallas_call | solution.py:52
  23.3 1.3 %collective-permute-done.5.c = f32[144,128]{1,0:T(8,128)S(1)} collective-permute-done((f32[144,128]{1,0:T(8,128)S(1)}, f32[144,128]{1,0:T(8,128)S(1)}, u32[]{:S(2)}, u32[]{:S(2)}) %collective-permute-start.5) | collective-permute-done | bytes 73760 | tf_op jit(solution)/shard_map/ppermute | solution.py:242
  24.5 1.9 %collective-permute-done.6.d = f32[144,128]{1,0:T(8,128)S(1)} collective-permute-done((f32[144,128]{1,0:T(8,128)S(1)}, f32[144,128]{1,0:T(8,128)S(1)}, u32[]{:S(2)}, u32[]{:S(2)}) %collective-permute-start.6) | collective-permute-done | bytes 73760 | tf_op jit(solution)/shard_map/ppermute | solution.py:242
  26.4 2.7 %collective-permute-start.7 = (f32[96,128]{1,0:T(8,128)S(1)}, f32[96,128]{1,0:T(8,128)S(1)}, u32[]{:S(2)}, u32[]{:S(2)}) collective-permute-start(f32[96,128]{1,0:T(8,128)S(1)} %get-tuple-element.42.ahead), channel_id=1, source_target_pairs={{0,16},{4,20},{8,24},{12,28},{16,0},{20,4},{24,8},{28,12},{1,17},{... | collective-permute-start | bytes 147464 | tf_op jit(solution)/shard_map/ppermute | solution.py:242
  29.4 1.5 %collective-permute-start.8 = (f32[48,128]{1,0:T(8,128)S(1)}, f32[48,128]{1,0:T(8,128)S(1)}, u32[]{:S(2)}, u32[]{:S(2)}) collective-permute-start(f32[48,128]{1,0:T(8,128)S(1)} %get-tuple-element.43), channel_id=1, source_target_pairs={{0,2},{1,3},{2,0},{3,1},{4,6},{5,7},{6,4},{7,5},{8,10},{9,11},{10,... | collective-permute-start | bytes 73736 | tf_op jit(solution)/shard_map/ppermute | solution.py:242
  30.9 4.1 %collective-permute-done.9.back_xz = f32[48,128]{1,0:T(8,128)S(1)} collective-permute-done((f32[48,128]{1,0:T(8,128)S(1)}, f32[48,128]{1,0:T(8,128)S(1)}, u32[]{:S(2)}, u32[]{:S(2)}) %collective-permute-start.9) | collective-permute-done | bytes 24608 | tf_op jit(solution)/shard_map/ppermute | solution.py:318
  35.4 1.1 %collective-permute-start.12 = (bf16[96,128]{1,0:T(8,128)(2,1)S(1)}, bf16[96,128]{1,0:T(8,128)(2,1)S(1)}, u32[]{:S(2)}, u32[]{:S(2)}) collective-permute-start(bf16[96,128]{1,0:T(8,128)(2,1)S(1)} %shard_map.62.p0), channel_id=1, source_target_pairs={{0,12},{4,8},{8,4},{12,0},{16,28},{20,24},{24,20},{28,16},{1,13},{... | collective-permute-start | bytes 73736 | tf_op jit(solution)/shard_map/ppermute | solution.py:242
  36.6 0.7 %collective-permute-start.11 = (bf16[96,128]{1,0:T(8,128)(2,1)S(1)}, bf16[96,128]{1,0:T(8,128)(2,1)S(1)}, u32[]{:S(2)}, u32[]{:S(2)}) collective-permute-start(bf16[96,128]{1,0:T(8,128)(2,1)S(1)} %shard_map.62.p0), channel_id=1, source_target_pairs={{0,8},{4,12},{8,0},{12,4},{16,24},{20,28},{24,16},{28,20},{1,9},{5... | collective-permute-start | bytes 73736 | tf_op jit(solution)/shard_map/ppermute | solution.py:242
  37.2 1.7 %collective-permute-start.10 = (bf16[96,128]{1,0:T(8,128)(2,1)S(1)}, bf16[96,128]{1,0:T(8,128)(2,1)S(1)}, u32[]{:S(2)}, u32[]{:S(2)}) collective-permute-start(bf16[96,128]{1,0:T(8,128)(2,1)S(1)} %shard_map.62.p0), channel_id=1, source_target_pairs={{0,4},{4,0},{8,12},{12,8},{16,20},{20,16},{24,28},{28,24},{1,5},{5... | collective-permute-start | bytes 73736 | tf_op jit(solution)/shard_map/ppermute | solution.py:242
  39.0 0.8 %shard_map.63.v_second = bf16[8,64,768]{2,1,0:T(8,128)(2,1)S(1)} custom-call(bf16[256,768]{1,0:T(8,128)(2,1)S(1)} %collective-permute-done.1.x, bf16[256,768]{1,0:T(8,128)(2,1)S(1)} %collective-permute-done.13.x_twin, bf16[5248,768]{1,0:T(8,128)(2,1)S(1)} %shard_map.56.kept), custom_call_target="tpu_custom_call" | custom-call | flops 603979776 | bytes 9633792 | tf_op jit(solution)/shard_map/pallas_call | solution.py:52
  40.4 0.7 %collective-permute-done.10.p1 = bf16[96,128]{1,0:T(8,128)(2,1)S(1)} collective-permute-done((bf16[96,128]{1,0:T(8,128)(2,1)S(1)}, bf16[96,128]{1,0:T(8,128)(2,1)S(1)}, u32[]{:S(2)}, u32[]{:S(2)}) %collective-permute-start.10) | collective-permute-done | bytes 24608 | tf_op jit(solution)/shard_map/ppermute | solution.py:242
  41.1 2.7 %shard_map.64 = bf16[512,768]{1,0:T(8,128)(2,1)} custom-call(bf16[96,128]{1,0:T(8,128)(2,1)S(1)} %shard_map.62.p0, bf16[96,128]{1,0:T(8,128)(2,1)S(1)} %collective-permute-done.10.p1, bf16[96,128]{1,0:T(8,128)(2,1)S(1)} %collective-permute-done.11.p2, bf16[96,128]{1,0:T(8,128)(2,1)S(1)} %collective-permute-done.12.p3, bf16[5248,768]{1,0:T(8,128)(2,1)S(1)} %shard_map.56.kept, ...), custom_call_target="tpu_custom_call" | custom-call | flops 1207959552 | bytes 11698176 | tf_op jit(solution)/shard_map/pallas_call | solution.py:52
  (20 shorter events, 2.4 us)
Async XLA Ops:
  0.0 1.3 %copy-start.1 = (bf16[16,32,768]{2,1,0:T(8,128)(2,1)S(1)}, bf16[16,32,768]{2,1,0:T(8,128)(2,1)}, u32[]{:S(2)}) copy-start(bf16[16,32,768]{2,1,0:T(8,128)(2,1)} %param.5) | copy-start | bytes 2359300
  1.3 2.9 %collective-permute-start = (bf16[512,768]{1,0:T(8,128)(2,1)S(1)}, bf16[512,768]{1,0:T(8,128)(2,1)S(1)}, u32[]{:S(2)}, u32[]{:S(2)}) collective-permute-start(bf16[512,768]{1,0:T(8,128)(2,1)S(1)} %bitcast.5), channel_id=1, source_target_pairs={{0,1},{1,0},{2,3},{3,2},{4,5},{5,4},{6,7},{7,6},{8,9},{9,8},{10,11... | collective-permute-start | bytes 2359304 | tf_op jit(solution)/shard_map/ppermute | solution.py:242
  1.7 12.3 %collective-permute-start.2 = (bf16[256,768]{1,0:T(8,128)(2,1)S(1)}, bf16[256,768]{1,0:T(8,128)(2,1)S(1)}, u32[]{:S(2)}, u32[]{:S(2)}) collective-permute-start(bf16[256,768]{1,0:T(8,128)(2,1)S(1)} %shard_map.55), channel_id=1, source_target_pairs={{0,2},{1,3},{2,0},{3,1},{4,6},{5,7},{6,4},{7,5},{8,10},{9,11},{10,... | collective-permute-start | bytes 1179656 | tf_op jit(solution)/shard_map/ppermute | solution.py:242
  4.2 0.9 %copy-start.2 = (bf16[512,768]{1,0:T(8,128)(2,1)}, bf16[512,768]{1,0:T(8,128)(2,1)S(1)}, u32[]{:S(2)}) copy-start(bf16[512,768]{1,0:T(8,128)(2,1)S(1)} %collective-permute-done.twin) | copy-start | bytes 2359300
  14.0 2.9 %collective-permute-start.3 = (bf16[256,768]{1,0:T(8,128)(2,1)S(1)}, bf16[256,768]{1,0:T(8,128)(2,1)S(1)}, u32[]{:S(2)}, u32[]{:S(2)}) collective-permute-start(bf16[256,768]{1,0:T(8,128)(2,1)S(1)} %collective-permute-done.2.x_far.x), channel_id=1, source_target_pairs={{0,1},{1,0},{2,3},{3,2},{4,5},{5,4},{6,7},{7,6},{8,9},{9,8},{10,11... | collective-permute-start | bytes 1179656 | tf_op jit(solution)/shard_map/ppermute | solution.py:242
  14.0 21.4 %collective-permute-start.1 = (bf16[256,768]{1,0:T(8,128)(2,1)S(1)}, bf16[256,768]{1,0:T(8,128)(2,1)S(1)}, u32[]{:S(2)}, u32[]{:S(2)}) collective-permute-start(bf16[256,768]{1,0:T(8,128)(2,1)S(1)} %shard_map.57), channel_id=1, source_target_pairs={{0,2},{1,3},{2,0},{3,1},{4,6},{5,7},{6,4},{7,5},{8,10},{9,11},{10,... | collective-permute-start | bytes 1179656 | tf_op jit(solution)/shard_map/ppermute | solution.py:242
  18.0 4.5 %collective-permute-start.4 = (f32[144,128]{1,0:T(8,128)S(1)}, f32[144,128]{1,0:T(8,128)S(1)}, u32[]{:S(2)}, u32[]{:S(2)}) collective-permute-start(f32[144,128]{1,0:T(8,128)S(1)} %get-tuple-element.36), channel_id=1, source_target_pairs={{0,4},{4,0},{8,12},{12,8},{16,20},{20,16},{24,28},{28,24},{1,5},{5... | collective-permute-start | bytes 221192 | tf_op jit(solution)/shard_map/ppermute | solution.py:242
  19.6 4.9 %collective-permute-start.5 = (f32[144,128]{1,0:T(8,128)S(1)}, f32[144,128]{1,0:T(8,128)S(1)}, u32[]{:S(2)}, u32[]{:S(2)}) collective-permute-start(f32[144,128]{1,0:T(8,128)S(1)} %get-tuple-element.38), channel_id=1, source_target_pairs={{0,8},{4,12},{8,0},{12,4},{16,24},{20,28},{24,16},{28,20},{1,9},{5... | collective-permute-start | bytes 221192 | tf_op jit(solution)/shard_map/ppermute | solution.py:242
  21.2 5.3 %collective-permute-start.6 = (f32[144,128]{1,0:T(8,128)S(1)}, f32[144,128]{1,0:T(8,128)S(1)}, u32[]{:S(2)}, u32[]{:S(2)}) collective-permute-start(f32[144,128]{1,0:T(8,128)S(1)} %get-tuple-element.41), channel_id=1, source_target_pairs={{0,12},{4,8},{8,4},{12,0},{16,28},{20,24},{24,20},{28,16},{1,13},{... | collective-permute-start | bytes 221192 | tf_op jit(solution)/shard_map/ppermute | solution.py:242
  26.4 8.6 %collective-permute-start.7 = (f32[96,128]{1,0:T(8,128)S(1)}, f32[96,128]{1,0:T(8,128)S(1)}, u32[]{:S(2)}, u32[]{:S(2)}) collective-permute-start(f32[96,128]{1,0:T(8,128)S(1)} %get-tuple-element.42.ahead), channel_id=1, source_target_pairs={{0,16},{4,20},{8,24},{12,28},{16,0},{20,4},{24,8},{28,12},{1,17},{... | collective-permute-start | bytes 147464 | tf_op jit(solution)/shard_map/ppermute | solution.py:242
  29.1 5.9 %collective-permute-start.9 = (f32[48,128]{1,0:T(8,128)S(1)}, f32[48,128]{1,0:T(8,128)S(1)}, u32[]{:S(2)}, u32[]{:S(2)}) collective-permute-start(f32[48,128]{1,0:T(8,128)S(1)} %get-tuple-element.43), channel_id=1, source_target_pairs={{0,18},{1,19},{2,16},{3,17},{4,22},{5,23},{6,20},{7,21},{8,26},{9,... | collective-permute-start | bytes 73736 | tf_op jit(solution)/shard_map/ppermute | solution.py:318
  29.4 5.6 %collective-permute-start.8 = (f32[48,128]{1,0:T(8,128)S(1)}, f32[48,128]{1,0:T(8,128)S(1)}, u32[]{:S(2)}, u32[]{:S(2)}) collective-permute-start(f32[48,128]{1,0:T(8,128)S(1)} %get-tuple-element.43), channel_id=1, source_target_pairs={{0,2},{1,3},{2,0},{3,1},{4,6},{5,7},{6,4},{7,5},{8,10},{9,11},{10,... | collective-permute-start | bytes 73736 | tf_op jit(solution)/shard_map/ppermute | solution.py:242
  35.3 5.8 %copy-start = (bf16[768,768]{1,0:T(8,128)(2,1)S(1)}, bf16[768,768]{1,0:T(8,128)(2,1)}, u32[]{:S(2)}) copy-start(bf16[768,768]{1,0:T(8,128)(2,1)} %wo.1) | copy-start | bytes 3538948
  35.3 3.6 %collective-permute-start.13 = (bf16[256,768]{1,0:T(8,128)(2,1)S(1)}, bf16[256,768]{1,0:T(8,128)(2,1)S(1)}, u32[]{:S(2)}, u32[]{:S(2)}) collective-permute-start(bf16[256,768]{1,0:T(8,128)(2,1)S(1)} %collective-permute-done.1.x), channel_id=1, source_target_pairs={{0,1},{1,0},{2,3},{3,2},{4,5},{5,4},{6,7},{7,6},{8,9},{9,8},{10,11... | collective-permute-start | bytes 1179656 | tf_op jit(solution)/shard_map/ppermute | solution.py:242
  35.4 4.8 %collective-permute-start.12 = (bf16[96,128]{1,0:T(8,128)(2,1)S(1)}, bf16[96,128]{1,0:T(8,128)(2,1)S(1)}, u32[]{:S(2)}, u32[]{:S(2)}) collective-permute-start(bf16[96,128]{1,0:T(8,128)(2,1)S(1)} %shard_map.62.p0), channel_id=1, source_target_pairs={{0,12},{4,8},{8,4},{12,0},{16,28},{20,24},{24,20},{28,16},{1,13},{... | collective-permute-start | bytes 73736 | tf_op jit(solution)/shard_map/ppermute | solution.py:242
  36.6 3.8 %collective-permute-start.11 = (bf16[96,128]{1,0:T(8,128)(2,1)S(1)}, bf16[96,128]{1,0:T(8,128)(2,1)S(1)}, u32[]{:S(2)}, u32[]{:S(2)}) collective-permute-start(bf16[96,128]{1,0:T(8,128)(2,1)S(1)} %shard_map.62.p0), channel_id=1, source_target_pairs={{0,8},{4,12},{8,0},{12,4},{16,24},{20,28},{24,16},{28,20},{1,9},{5... | collective-permute-start | bytes 73736 | tf_op jit(solution)/shard_map/ppermute | solution.py:242
  37.2 3.8 %collective-permute-start.10 = (bf16[96,128]{1,0:T(8,128)(2,1)S(1)}, bf16[96,128]{1,0:T(8,128)(2,1)S(1)}, u32[]{:S(2)}, u32[]{:S(2)}) collective-permute-start(bf16[96,128]{1,0:T(8,128)(2,1)S(1)} %shard_map.62.p0), channel_id=1, source_target_pairs={{0,4},{4,0},{8,12},{12,8},{16,20},{20,16},{24,28},{28,24},{1,5},{5... | collective-permute-start | bytes 73736 | tf_op jit(solution)/shard_map/ppermute | solution.py:242

commit v4 on v3

v4 whole, which is shorter than its diff:
```python
import functools
import math

import jax
import jax.numpy as jnp
from jax import lax
from jax.experimental import pallas as pl
from jax.experimental.pallas import tpu as pltpu
from jax.sharding import PartitionSpec as P

H = 12
GROUP = 4
F32, BF16 = jnp.float32, jnp.bfloat16


def reshape_by_group(inputs, weight, attention_groups):
    sequence_number, site_number, embed_size = inputs.shape
    out = jnp.dot(
        inputs.reshape(sequence_number * site_number, embed_size),
        weight,
        preferred_element_type=F32,
    )
    return out.astype(BF16).reshape(
        sequence_number, site_number, attention_groups, embed_size // attention_groups
    )


def plain_body(
    alignment_embedding, probe_projector, lookup_projector, content_projector, final_projector
):
    sequence_number, site_number, embed_size = alignment_embedding.shape
    head_size = embed_size // H
    scale = 1.0 / math.sqrt(head_size * sequence_number * lax.axis_size("seq"))
    probe_tensor = reshape_by_group(alignment_embedding, probe_projector, H)
    gathered = lax.all_gather(alignment_embedding, "res", axis=1, tiled=True)
    all_keys = reshape_by_group(gathered, lookup_projector, H)
    all_values = reshape_by_group(gathered, content_projector, H)
    logits = jnp.einsum("rihe,rjhe->hij", probe_tensor, all_keys, preferred_element_type=F32)
    summed = lax.psum(logits, "seq")
    probs = jax.nn.softmax(summed * scale, axis=-1).astype(BF16)
    attended = jnp.einsum("hij,rjhe->rihe", probs, all_values, preferred_element_type=F32)
    attended = attended.astype(BF16).reshape(sequence_number * site_number, embed_size)
    mixed = jnp.dot(attended, final_projector, preferred_element_type=F32).astype(BF16)
    return mixed.reshape(sequence_number, site_number, embed_size)


def call(kernel, outs, args, flops=0, scratch=(), space=pltpu.VMEM, to=pltpu.VMEM):
    shapes = [jax.ShapeDtypeStruct(s, d) for s, d in outs]
    if space == pltpu.HBM:
        args = [pltpu.with_memory_space_constraint(a, space) for a in args]
    moved = sum(a.size * a.dtype.itemsize for a in list(args) + shapes)
    return pl.pallas_call(
        kernel,
        out_shape=shapes,
        in_specs=[pl.BlockSpec(memory_space=space)] * len(args),
        out_specs=[pl.BlockSpec(memory_space=to)] * len(shapes),
        scratch_shapes=list(scratch),
        cost_estimate=pl.CostEstimate(flops=flops, bytes_accessed=moved, transcendentals=0),
        compiler_params=pltpu.CompilerParams(vmem_limit_bytes=4 * 1024 * 1024),
    )(*args)


def matmul(x, w):
    return jnp.dot(x, w, preferred_element_type=F32).astype(BF16)


def apart(x, sites, store):
    head = x.shape[1] // H
    rows = [x[r : r + sites, :] for r in range(0, x.shape[0], sites)]
    for r in range(0, len(rows), 2):
        for h in range(H):
            lanes = slice(h * head, (h + 1) * head)
            pair = [rows[r][:, lanes], rows[r + 1][:, lanes]]
            store(h, r * head, jnp.concatenate(pair, axis=1))


def keep_apart(x, sites, out, blocks=1, block=0):
    def store(h, lane, pair):
        at = (h * blocks + block) * sites
        out[at : at + sites, lane : lane + pair.shape[1]] = pair

    apart(x, sites, store)


def against(probe, keys):
    return lax.dot_general(probe, keys, (((1,), (1,)), ((), ())), preferred_element_type=F32)


def gray(n):
    return n ^ (n >> 1)


def ring_place():
    me = lax.rem(lax.axis_index("seq"), GROUP)
    return lax.bitwise_xor(me, lax.shift_right_logical(me, 1))


def kernel_part(count, other, x, out, sems):
    place = lax.axis_index("res") // 2
    start = (1 - place if other else place) * count
    piece = count // sems.shape[0]
    copies = [
        pltpu.make_async_copy(
            x.at[pl.ds(start + n * piece, piece)], out.at[pl.ds(n * piece, piece)], sems.at[n]
        )
        for n in range(sems.shape[0])
    ]
    for copy in copies:
        copy.start()
    for copy in copies:
        copy.wait()


def kernel_near(rows, sites, own, twin, wq, wk, wv, kept, q, k, v, near, x_own, x_twin, sems):
    embed = wq.shape[0]
    moves = [(own, x_own), (twin, x_twin)]
    moves += [(w, kept.at[pl.ds(n * embed, embed)]) for n, w in enumerate((wq, wk, wv))]
    own_in, twin_in, wq_in, wk_in, wv_in = copies = [
        pltpu.make_async_copy(source, target, sems.at[n])
        for n, (source, target) in enumerate(moves)
    ]
    for n in (2, 0, 3, 1, 4):
        copies[n].start()
    wq_in.wait()
    own_in.wait()
    keep_apart(matmul(x_own[...], kept[:embed, :]), sites, q)
    wk_in.wait()
    keep_apart(matmul(x_own[...], kept[embed : 2 * embed, :]), sites, k, 2, 0)
    twin_in.wait()
    keep_apart(matmul(x_twin[...], kept[embed : 2 * embed, :]), sites, k, 2, 1)
    for h in range(H):
        mine, both = slice(h * sites, (h + 1) * sites), slice(2 * h * sites, 2 * (h + 1) * sites)
        near[mine, :] = against(q[mine, :], k[both, :])
    wv_in.wait()
    keep_apart(matmul(x_own[...], kept[2 * embed :, :]), sites, v, 2, 0)
    keep_apart(matmul(x_twin[...], kept[2 * embed :, :]), sites, v, 2, 1)


def rows_that_came(half_width):
    came = (1 - lax.axis_index("res") // 2) * half_width
    return pl.ds(pl.multiple_of(came, half_width), half_width)


def kernel_back(sites, x_far, kept, k, k_far, back, q_far):
    embed, came = x_far.shape[1], rows_that_came(k_far.shape[1])
    keep_apart(matmul(x_far[...], kept[:embed, :]), sites, q_far)
    keep_apart(matmul(x_far[...], kept[embed : 2 * embed, :]), sites, k_far)
    for h in range(H):
        mine, both = slice(h * sites, (h + 1) * sites), slice(2 * h * sites, 2 * (h + 1) * sites)
        back[mine, :] = against(q_far[mine, :], k[both, came])


def kernel_ahead(sites, x_far_twin, kept, q, near, k_far, back, *refs):
    parts, (k_twin, ahead) = refs[:GROUP], refs[GROUP:]
    embed, came = x_far_twin.shape[1], rows_that_came(k_far.shape[1])
    me = ring_place()
    keep_apart(matmul(x_far_twin[...], kept[embed : 2 * embed, :]), sites, k_twin)
    for h in range(H):
        mine = slice(h * sites, (h + 1) * sites)
        keys = jnp.concatenate([k_far[mine, :], k_twin[mine, :]], axis=0)
        ahead[mine, :] = jnp.concatenate([near[mine, :], against(q[mine, came], keys)], axis=1)
    size = H * sites // GROUP
    for n in range(GROUP):
        to = lax.rem(me + n, GROUP) * size
        parts[n][:size, :] = ahead[pl.ds(to, size), :]
        parts[n][size:, :] = jnp.concatenate(
            [back[pl.ds(to, size // 2), :], back[pl.ds(to + size // 2, size // 2), :]], axis=1
        )


def kernel_sum(size, a, b, c, d, ahead, back):
    ahead[...] = (a[:size, :] + b[:size, :]) + (c[:size, :] + d[:size, :])
    back[...] = (a[size:, :] + b[size:, :]) + (c[size:, :] + d[size:, :])


def kernel_softmax(scale, ahead, ahead_z, back_x, back_xz, out):
    far = back_x[...] + back_xz[...]
    half = far.shape[1] // 2
    far = jnp.concatenate([far[:, :half], far[:, half:]], axis=0)
    far = jnp.concatenate([jnp.zeros_like(far), far], axis=1)
    logits = (ahead[...] + ahead_z[...] + far) * scale
    e = jnp.exp(logits - jnp.max(logits, axis=1, keepdims=True))
    out[...] = (e / jnp.sum(e, axis=1, keepdims=True)).astype(BF16)


def kernel_values(sites, x, x_twin, kept, out):
    w = kept[2 * x.shape[1] :, :]
    keep_apart(matmul(x[...], w), sites, out, 2, 0)
    keep_apart(matmul(x_twin[...], w), sites, out, 2, 1)


def kernel_last(sites, p0, p1, p2, p3, v_near, v_first, v_second, wo, out, probs, att, mixed, sems):
    place = lax.axis_index("res") // 2
    me = ring_place()
    size, width = H * sites // GROUP, v_first.shape[1]
    head = wo.shape[0] // H
    for n, p in enumerate((p0, p1, p2, p3)):
        probs[pl.ds(lax.rem(me + GROUP - n, GROUP) * size, size), :] = p[...]
    copies = []
    for far, half in ((v_first, 1 - place), (v_second, place)):
        came = pl.ds(pl.multiple_of(half * width, width), width)
        for h in range(0, H, 2):
            pair = []
            for one in (h, h + 1):
                both = slice(2 * one * sites, 2 * (one + 1) * sites)
                v = jnp.concatenate([v_near[both, came], far[both, :]], axis=0)
                p = probs[one * sites : (one + 1) * sites, :]
                pair.append(matmul(p, v))
            for r in range(width // head):
                lanes = slice(r * head, (r + 1) * head)
                att[r * sites : (r + 1) * sites, h * head : (h + 2) * head] = jnp.concatenate(
                    [pair[0][:, lanes], pair[1][:, lanes]], axis=1
                )
        rows = att.shape[0]
        piece = 2 * rows // sems.shape[0]
        for start in range(0, rows, piece):
            n = len(copies)
            mixed[n * piece : (n + 1) * piece, :] = matmul(att[start : start + piece, :], wo[...])
            target = out.at[pl.ds(half * rows + start, piece)]
            copies.append(
                pltpu.make_async_copy(mixed.at[pl.ds(n * piece, piece)], target, sems.at[n])
            )
            copies[n].start()
    for copy in copies:
        copy.wait()


def swap(x, axis, bit):
    count = lax.axis_size(axis)
    return lax.ppermute(x, axis, [(i, i ^ bit) for i in range(count)])


def turn(x, steps):
    count = lax.axis_size("seq")
    to = [s // GROUP * GROUP + gray((gray(s % GROUP) + steps) % GROUP) for s in range(count)]
    return lax.ppermute(x, "seq", list(enumerate(to)))


def body(x, wq, wk, wv, wo):
    rows, sites, embed = x.shape
    half, head = rows // 2, embed // H
    n_seq, n_res = lax.axis_size("seq"), lax.axis_size("res")
    scale = 1.0 / math.sqrt(head * rows * n_seq)
    flat, half_flat = (rows * sites, embed), (half * sites, embed)
    own = x.reshape(flat)
    cost = 2 * rows * sites * embed * embed

    def part(x, other):
        return call(
            functools.partial(kernel_part, half * sites, other),
            [(half_flat, BF16)],
            (x,),
            scratch=[pltpu.SemaphoreType.DMA((GROUP,))],
            space=pltpu.HBM,
        )[0]

    sent_first = part(own, False)
    far_first = swap(sent_first, "res", 2)
    mine, sent_first = lax.optimization_barrier((own, sent_first))
    twin = swap(mine, "res", 1)
    sums = ((H * sites, 2 * sites), F32)

    def heads(blocks, count):
        return ((H * blocks * sites, count * head), BF16)

    kept, q, k, v_near, near = call(
        functools.partial(kernel_near, rows, sites),
        [((3 * embed, embed), BF16), heads(1, rows), heads(2, rows), heads(2, rows), sums],
        (own, twin, wq, wk, wv),
        6 * cost,
        [pltpu.VMEM(flat, BF16), pltpu.VMEM(flat, BF16), pltpu.SemaphoreType.DMA((5,))],
        pltpu.HBM,
    )
    later, kept = lax.optimization_barrier((own, kept))
    sent_second = part(later, True)
    far_second = swap(sent_second, "res", 2)
    far_first, kept, sent_second = lax.optimization_barrier((far_first, kept, sent_second))
    far_first_twin = swap(far_first, "res", 1)
    k_far, back = call(
        functools.partial(kernel_back, sites),
        [heads(1, half), sums],
        (far_first, kept, k),
        cost,
        [pltpu.VMEM(*heads(1, half))],
    )
    far_first_twin, k_far = lax.optimization_barrier((far_first_twin, k_far))
    size = H * sites // GROUP
    part_shape = (size + size // 2, 4 * sites)
    parts = call(
        functools.partial(kernel_ahead, sites),
        [(part_shape, F32)] * GROUP,
        (far_first_twin, kept, q, near, k_far, back),
        cost,
        [pltpu.VMEM(*heads(1, half)), pltpu.VMEM((H * sites, 4 * sites), F32)],
    )
    came = [turn(parts[k], k) for k in range(1, GROUP)]
    came[0], kept = lax.optimization_barrier((came[0], kept))
    (v_first,) = call(
        functools.partial(kernel_values, sites),
        [heads(2, half)],
        (far_first, far_first_twin, kept),
        cost,
    )
    came[1], v_first = lax.optimization_barrier((came[1], v_first))
    ahead, back = call(
        functools.partial(kernel_sum, size),
        [((size, 4 * sites), F32), ((size // 2, 4 * sites), F32)],
        (parts[0], *came),
    )
    ahead_z = swap(ahead, "seq", GROUP)
    back_x = swap(back, "res", 2)
    cross = [
        (s * n_res + r, (s ^ GROUP) * n_res + (r ^ 2)) for s in range(n_seq) for r in range(n_res)
    ]
    back_xz = lax.ppermute(back, ("seq", "res"), cross)
    (probs,) = call(
        functools.partial(kernel_softmax, scale),
        [((size, 4 * sites), BF16)],
        (ahead, ahead_z, back_x, back_xz),
    )
    far_second, probs = lax.optimization_barrier((far_second, probs))
    far_second_twin = swap(far_second, "res", 1)
    others = [turn(probs, k) for k in range(1, GROUP)]

    (v_second,) = call(
        functools.partial(kernel_values, sites),
        [heads(2, half)],
        (far_second, far_second_twin, kept),
        cost,
    )
    (out,) = call(
        functools.partial(kernel_last, sites),
        [(flat, BF16)],
        (probs, *others, v_near, v_first, v_second, wo),
        2 * cost,
        [
            pltpu.VMEM((H * sites, 4 * sites), BF16),
            pltpu.VMEM(half_flat, BF16),
            pltpu.VMEM(flat, BF16),
            pltpu.SemaphoreType.DMA((4,)),
        ],
        to=pltpu.HBM,
    )
    return out.reshape(rows, sites, embed)


def solution(mesh):
    placed = (P("seq", "res", None), P(), P(), P(), P())
    fits = mesh.shape["res"] == 4 and mesh.shape["seq"] == 2 * GROUP
    return jax.shard_map(
        body if fits else plain_body,
        mesh=mesh,
        in_specs=placed,
        out_specs=P("seq", "res", None),
        check_vma=False,
    )
```

time: 44 us -> 43 us (0.977)
  waiting for transfers between devices: 10.9 us -> 9.22 us
  starting transfers between devices: 16.3 us -> 17.4 us
    ppermute x0 -> x6, starting transfers between devices: none -> 8.21 us  [turn(): return lax.ppermute(x, 'seq', list(enumerate(to)))]
    ppermute x13 -> x7, starting transfers between devices: 16 us -> 8.81 us  [swap(): return lax.ppermute(x, axis, [(i, i ^ bit) for i in range(count)])]
    ppermute x13 -> x7, waiting for transfers between devices: 6.84 us -> 1.28 us  [swap(): return lax.ppermute(x, axis, [(i, i ^ bit) for i in range(count)])]
    ppermute x0 -> x6, waiting for transfers between devices: none -> 4.12 us  [turn(): return lax.ppermute(x, 'seq', list(enumerate(to)))]
  transfers between devices with their start and end apart: 14 -> 14, of which waited for: 8 -> 6; matrix products, arithmetic and copies ran while one was open for 0% -> 0% of each run, Pallas kernels for 26% -> 27%
where the time goes in v4:
time: 43 us; the launch traced here: 42.8 us
  starting transfers between devices  17.4 us (40%)
  Pallas kernels  15 us (35%)
  waiting for transfers between devices  9.22 us (21%)
  local copies, waits for them, and re-layouts  1.06 us (2%)
    pallas_call x10, Pallas kernels, call(): pl.pallas_call(kernel, out_shape=shapes, in_specs=[pl.BlockSpec(memory_sp...  15 us
    ppermute x7, starting transfers between devices, swap(): return lax.ppermute(x, axis, [(i, i ^ bit) for i in range(count)])  8.81 us
    ppermute x6, starting transfers between devices, turn(): return lax.ppermute(x, 'seq', list(enumerate(to)))  8.21 us
    ppermute x6, waiting for transfers between devices, turn(): return lax.ppermute(x, 'seq', list(enumerate(to)))  4.12 us
    ppermute x1, waiting for transfers between devices, body(): back_xz = lax.ppermute(back, ('seq', 'res'), cross)  3.83 us
    ppermute x7, waiting for transfers between devices, swap(): return lax.ppermute(x, axis, [(i, i ^ bit) for i in range(count)])  1.28 us
    unnamed x6, local copies, waits for them, and re-layouts  1.06 us
  transfers between devices with their start and end apart: 14, of which 6 were waited for; matrix products, arithmetic and copies ran while one was open for 0% of the time, Pallas kernels for 27%

profile of v4, /device:TPU:0, one launch (start us, length us, event | category | flops | bytes accessed | tf_op | source)
XLA Modules:
  0.0 42.8 jit_solution(13872458043360121138)
XLA Ops:
  0.0 1.1 %shard_map.55 = bf16[256,768]{1,0:T(8,128)(2,1)S(1)} custom-call(bf16[512,768]{1,0:T(8,128)(2,1)} %bitcast.2), custom_call_target="tpu_custom_call" | custom-call | bytes 1179648 | tf_op jit(solution)/shard_map/pallas_call | solution.py:52
  1.8 2.5 %collective-permute-start.2 = (bf16[256,768]{1,0:T(8,128)(2,1)S(1)}, bf16[256,768]{1,0:T(8,128)(2,1)S(1)}, u32[]{:S(2)}, u32[]{:S(2)}) collective-permute-start(bf16[256,768]{1,0:T(8,128)(2,1)S(1)} %shard_map.55), channel_id=1, source_target_pairs={{0,2},{1,3},{2,0},{3,1},{4,6},{5,7},{6,4},{7,5},{8,10},{9,11},{10,... | collective-permute-start | bytes 1179656 | tf_op jit(solution)/shard_map/ppermute | solution.py:230
  4.3 0.9 %copy-done.2 = bf16[512,768]{1,0:T(8,128)(2,1)} copy-done((bf16[512,768]{1,0:T(8,128)(2,1)}, bf16[512,768]{1,0:T(8,128)(2,1)S(1)}, u32[]{:S(2)}) %copy-start.2) | copy-done | bytes 786456
  5.1 6.5 %shard_map.56 = (bf16[2304,768]{1,0:T(8,128)(2,1)S(1)}, bf16[384,1024]{1,0:T(8,128)(2,1)S(1)}, bf16[768,1024]{1,0:T(8,128)(2,1)S(1)}, bf16[768,1024]{1,0:T(8,128)(2,1)S(1)}, f32[384,64]{1,0:T(8,128)S(1)}) custom-call(bf16[512,768]{1,0:T(8,128)(2,1)} %bitcast.3, bf16[512,768]{1,0:T(8,128)(2,1)} %copy-done.2, bf16[768,768]{1,0:T(8,128)(2,1)} %wq.1, ...), custom_call_target="tpu_custom_call" | custom-call | flops 3623878656 | bytes 12681216 | tf_op jit(solution)/shard_map/pallas_call | solution.py:52
  11.7 1.1 %shard_map.57 = bf16[256,768]{1,0:T(8,128)(2,1)S(1)} custom-call(bf16[512,768]{1,0:T(8,128)(2,1)} %bitcast.4), custom_call_target="tpu_custom_call" | custom-call | bytes 1179648 | tf_op jit(solution)/shard_map/pallas_call | solution.py:52
  12.8 1.3 %collective-permute-done.2.x_far.x = bf16[256,768]{1,0:T(8,128)(2,1)S(1)} collective-permute-done((bf16[256,768]{1,0:T(8,128)(2,1)S(1)}, bf16[256,768]{1,0:T(8,128)(2,1)S(1)}, u32[]{:S(2)}, u32[]{:S(2)}) %collective-permute-start.2) | collective-permute-done | bytes 393248 | tf_op jit(solution)/shard_map/ppermute | solution.py:230
  14.1 1.7 %collective-permute-start.1 = (bf16[256,768]{1,0:T(8,128)(2,1)S(1)}, bf16[256,768]{1,0:T(8,128)(2,1)S(1)}, u32[]{:S(2)}, u32[]{:S(2)}) collective-permute-start(bf16[256,768]{1,0:T(8,128)(2,1)S(1)} %shard_map.57), channel_id=1, source_target_pairs={{0,2},{1,3},{2,0},{3,1},{4,6},{5,7},{6,4},{7,5},{8,10},{9,11},{10,... | collective-permute-start | bytes 1179656 | tf_op jit(solution)/shard_map/ppermute | solution.py:230
  15.8 1.0 %shard_map.58 = (bf16[384,512]{1,0:T(8,128)(2,1)S(1)}, f32[384,64]{1,0:T(8,128)S(1)}) custom-call(bf16[256,768]{1,0:T(8,128)(2,1)S(1)} %collective-permute-done.2.x_far.x, bf16[2304,768]{1,0:T(8,128)(2,1)S(1)} %get-tuple-element.48.kept, bf16[768,1024]{1,0:T(8,128)(2,1)S(1)} %get-tuple-element.37.k), custom_call_target="tpu_custom_call" | custom-call | flops 603979776 | bytes 5996544 | tf_op jit(solution)/shard_map/pallas_call | solution.py:52
  16.8 1.0 %shard_map.59 = (f32[144,128]{1,0:T(8,128)S(1)}, f32[144,128]{1,0:T(8,128)S(1)}, f32[144,128]{1,0:T(8,128)S(1)}, f32[144,128]{1,0:T(8,128)S(1)}) custom-call(bf16[256,768]{1,0:T(8,128)(2,1)S(1)} %collective-permute-done.3.x_far_twin.x_twin, bf16[2304,768]{1,0:T(8,128)(2,1)S(1)} %get-tuple-element.48.kept, bf16[384,1024]{1,0:T(8,128)(2,1)S(1)} %get-tuple-element.40.q, ...), custom_call_target="tpu_custom_call" | custom-call | flops 603979776 | bytes 5603328 | tf_op jit(solution)/shard_map/pallas_call | solution.py:52
  17.7 1.6 %collective-permute-start.4 = (f32[144,128]{1,0:T(8,128)S(1)}, f32[144,128]{1,0:T(8,128)S(1)}, u32[]{:S(2)}, u32[]{:S(2)}) collective-permute-start(f32[144,128]{1,0:T(8,128)S(1)} %get-tuple-element.45), channel_id=1, source_target_pairs={{0,4},{4,12},{8,0},{12,8},{16,20},{20,28},{24,16},{28,24},{1,5},{5... | collective-permute-start | bytes 221192 | tf_op jit(solution)/shard_map/ppermute | solution.py:236
  19.3 1.5 %collective-permute-start.5 = (f32[144,128]{1,0:T(8,128)S(1)}, f32[144,128]{1,0:T(8,128)S(1)}, u32[]{:S(2)}, u32[]{:S(2)}) collective-permute-start(f32[144,128]{1,0:T(8,128)S(1)} %get-tuple-element.47), channel_id=1, source_target_pairs={{0,12},{4,8},{8,4},{12,0},{16,28},{20,24},{24,20},{28,16},{1,13},{... | collective-permute-start | bytes 221192 | tf_op jit(solution)/shard_map/ppermute | solution.py:236
  20.8 1.5 %collective-permute-start.6 = (f32[144,128]{1,0:T(8,128)S(1)}, f32[144,128]{1,0:T(8,128)S(1)}, u32[]{:S(2)}, u32[]{:S(2)}) collective-permute-start(f32[144,128]{1,0:T(8,128)S(1)} %get-tuple-element.50), channel_id=1, source_target_pairs={{0,8},{4,0},{8,12},{12,4},{16,24},{20,16},{24,28},{28,20},{1,9},{5... | collective-permute-start | bytes 221192 | tf_op jit(solution)/shard_map/ppermute | solution.py:236
  22.4 0.9 %shard_map.60.v_first = bf16[768,512]{1,0:T(8,128)(2,1)S(1)} custom-call(bf16[256,768]{1,0:T(8,128)(2,1)S(1)} %collective-permute-done.2.x_far.x, bf16[256,768]{1,0:T(8,128)(2,1)S(1)} %collective-permute-done.3.x_far_twin.x_twin, bf16[2304,768]{1,0:T(8,128)(2,1)S(1)} %get-tuple-element.48.kept), custom_call_target="tpu_custom_call" | custom-call | flops 603979776 | bytes 5111808 | tf_op jit(solution)/shard_map/pallas_call | solution.py:52
  23.2 1.9 %collective-permute-done.5.c = f32[144,128]{1,0:T(8,128)S(1)} collective-permute-done((f32[144,128]{1,0:T(8,128)S(1)}, f32[144,128]{1,0:T(8,128)S(1)}, u32[]{:S(2)}, u32[]{:S(2)}) %collective-permute-start.5) | collective-permute-done | bytes 73760 | tf_op jit(solution)/shard_map/ppermute | solution.py:236
  25.1 0.8 %collective-permute-done.6.d = f32[144,128]{1,0:T(8,128)S(1)} collective-permute-done((f32[144,128]{1,0:T(8,128)S(1)}, f32[144,128]{1,0:T(8,128)S(1)}, u32[]{:S(2)}, u32[]{:S(2)}) %collective-permute-start.6) | collective-permute-done | bytes 73760 | tf_op jit(solution)/shard_map/ppermute | solution.py:236
  25.9 2.7 %collective-permute-start.7 = (f32[96,128]{1,0:T(8,128)S(1)}, f32[96,128]{1,0:T(8,128)S(1)}, u32[]{:S(2)}, u32[]{:S(2)}) collective-permute-start(f32[96,128]{1,0:T(8,128)S(1)} %get-tuple-element.51.ahead), channel_id=1, source_target_pairs={{0,16},{4,20},{8,24},{12,28},{16,0},{20,4},{24,8},{28,12},{1,17},{... | collective-permute-start | bytes 147464 | tf_op jit(solution)/shard_map/ppermute | solution.py:230
  29.0 1.4 %collective-permute-start.8 = (f32[48,128]{1,0:T(8,128)S(1)}, f32[48,128]{1,0:T(8,128)S(1)}, u32[]{:S(2)}, u32[]{:S(2)}) collective-permute-start(f32[48,128]{1,0:T(8,128)S(1)} %get-tuple-element.52), channel_id=1, source_target_pairs={{0,2},{1,3},{2,0},{3,1},{4,6},{5,7},{6,4},{7,5},{8,10},{9,11},{10,... | collective-permute-start | bytes 73736 | tf_op jit(solution)/shard_map/ppermute | solution.py:230
  30.4 3.8 %collective-permute-done.9.back_xz = f32[48,128]{1,0:T(8,128)S(1)} collective-permute-done((f32[48,128]{1,0:T(8,128)S(1)}, f32[48,128]{1,0:T(8,128)S(1)}, u32[]{:S(2)}, u32[]{:S(2)}) %collective-permute-start.9) | collective-permute-done | bytes 24608 | tf_op jit(solution)/shard_map/ppermute | solution.py:315
  34.6 0.9 %collective-permute-start.12 = (bf16[96,128]{1,0:T(8,128)(2,1)S(1)}, bf16[96,128]{1,0:T(8,128)(2,1)S(1)}, u32[]{:S(2)}, u32[]{:S(2)}) collective-permute-start(bf16[96,128]{1,0:T(8,128)(2,1)S(1)} %shard_map.62.p0), channel_id=1, source_target_pairs={{0,8},{4,0},{8,12},{12,4},{16,24},{20,16},{24,28},{28,20},{1,9},{5... | collective-permute-start | bytes 73736 | tf_op jit(solution)/shard_map/ppermute | solution.py:236
  35.5 1.2 %collective-permute-start.11 = (bf16[96,128]{1,0:T(8,128)(2,1)S(1)}, bf16[96,128]{1,0:T(8,128)(2,1)S(1)}, u32[]{:S(2)}, u32[]{:S(2)}) collective-permute-start(bf16[96,128]{1,0:T(8,128)(2,1)S(1)} %shard_map.62.p0), channel_id=1, source_target_pairs={{0,12},{4,8},{8,4},{12,0},{16,28},{20,24},{24,20},{28,16},{1,13},{... | collective-permute-start | bytes 73736 | tf_op jit(solution)/shard_map/ppermute | solution.py:236
  36.7 1.5 %collective-permute-start.10 = (bf16[96,128]{1,0:T(8,128)(2,1)S(1)}, bf16[96,128]{1,0:T(8,128)(2,1)S(1)}, u32[]{:S(2)}, u32[]{:S(2)}) collective-permute-start(bf16[96,128]{1,0:T(8,128)(2,1)S(1)} %shard_map.62.p0), channel_id=1, source_target_pairs={{0,4},{4,12},{8,0},{12,8},{16,20},{20,28},{24,16},{28,24},{1,5},{5... | collective-permute-start | bytes 73736 | tf_op jit(solution)/shard_map/ppermute | solution.py:236
  38.2 0.9 %shard_map.63.v_second = bf16[768,512]{1,0:T(8,128)(2,1)S(1)} custom-call(bf16[256,768]{1,0:T(8,128)(2,1)S(1)} %collective-permute-done.1.x, bf16[256,768]{1,0:T(8,128)(2,1)S(1)} %collective-permute-done.13.x_twin, bf16[2304,768]{1,0:T(8,128)(2,1)S(1)} %get-tuple-element.48.kept), custom_call_target="tpu_custom_call" | custom-call | flops 603979776 | bytes 5111808 | tf_op jit(solution)/shard_map/pallas_call | solution.py:52
  39.1 1.2 %collective-permute-done.11.p2 = bf16[96,128]{1,0:T(8,128)(2,1)S(1)} collective-permute-done((bf16[96,128]{1,0:T(8,128)(2,1)S(1)}, bf16[96,128]{1,0:T(8,128)(2,1)S(1)}, u32[]{:S(2)}, u32[]{:S(2)}) %collective-permute-start.11) | collective-permute-done | bytes 24608 | tf_op jit(solution)/shard_map/ppermute | solution.py:236
  40.5 2.3 %shard_map.64 = bf16[512,768]{1,0:T(8,128)(2,1)} custom-call(bf16[96,128]{1,0:T(8,128)(2,1)S(1)} %shard_map.62.p0, bf16[96,128]{1,0:T(8,128)(2,1)S(1)} %collective-permute-done.10.p1, bf16[96,128]{1,0:T(8,128)(2,1)S(1)} %collective-permute-done.11.p2, bf16[96,128]{1,0:T(8,128)(2,1)S(1)} %collective-permute-done.12.p3, ...), custom_call_target="tpu_custom_call" | custom-call | flops 1207959552 | bytes 5210112 | tf_op jit(solution)/shard_map/pallas_call | solution.py:52
  (20 shorter events, 1.7 us)
Async XLA Ops:
  0.0 1.3 %copy-start.1 = (bf16[16,32,768]{2,1,0:T(8,128)(2,1)S(1)}, bf16[16,32,768]{2,1,0:T(8,128)(2,1)}, u32[]{:S(2)}) copy-start(bf16[16,32,768]{2,1,0:T(8,128)(2,1)} %param.5) | copy-start | bytes 2359300
  1.3 2.9 %collective-permute-start = (bf16[512,768]{1,0:T(8,128)(2,1)S(1)}, bf16[512,768]{1,0:T(8,128)(2,1)S(1)}, u32[]{:S(2)}, u32[]{:S(2)}) collective-permute-start(bf16[512,768]{1,0:T(8,128)(2,1)S(1)} %bitcast.5), channel_id=1, source_target_pairs={{0,1},{1,0},{2,3},{3,2},{4,5},{5,4},{6,7},{7,6},{8,9},{9,8},{10,11... | collective-permute-start | bytes 2359304 | tf_op jit(solution)/shard_map/ppermute | solution.py:230
  1.8 12.3 %collective-permute-start.2 = (bf16[256,768]{1,0:T(8,128)(2,1)S(1)}, bf16[256,768]{1,0:T(8,128)(2,1)S(1)}, u32[]{:S(2)}, u32[]{:S(2)}) collective-permute-start(bf16[256,768]{1,0:T(8,128)(2,1)S(1)} %shard_map.55), channel_id=1, source_target_pairs={{0,2},{1,3},{2,0},{3,1},{4,6},{5,7},{6,4},{7,5},{8,10},{9,11},{10,... | collective-permute-start | bytes 1179656 | tf_op jit(solution)/shard_map/ppermute | solution.py:230
  4.3 0.9 %copy-start.2 = (bf16[512,768]{1,0:T(8,128)(2,1)}, bf16[512,768]{1,0:T(8,128)(2,1)S(1)}, u32[]{:S(2)}) copy-start(bf16[512,768]{1,0:T(8,128)(2,1)S(1)} %collective-permute-done.twin) | copy-start | bytes 2359300
  14.0 2.7 %collective-permute-start.3 = (bf16[256,768]{1,0:T(8,128)(2,1)S(1)}, bf16[256,768]{1,0:T(8,128)(2,1)S(1)}, u32[]{:S(2)}, u32[]{:S(2)}) collective-permute-start(bf16[256,768]{1,0:T(8,128)(2,1)S(1)} %collective-permute-done.2.x_far.x), channel_id=1, source_target_pairs={{0,1},{1,0},{2,3},{3,2},{4,5},{5,4},{6,7},{7,6},{8,9},{9,8},{10,11... | collective-permute-start | bytes 1179656 | tf_op jit(solution)/shard_map/ppermute | solution.py:230
  14.1 20.5 %collective-permute-start.1 = (bf16[256,768]{1,0:T(8,128)(2,1)S(1)}, bf16[256,768]{1,0:T(8,128)(2,1)S(1)}, u32[]{:S(2)}, u32[]{:S(2)}) collective-permute-start(bf16[256,768]{1,0:T(8,128)(2,1)S(1)} %shard_map.57), channel_id=1, source_target_pairs={{0,2},{1,3},{2,0},{3,1},{4,6},{5,7},{6,4},{7,5},{8,10},{9,11},{10,... | collective-permute-start | bytes 1179656 | tf_op jit(solution)/shard_map/ppermute | solution.py:230
  17.7 4.6 %collective-permute-start.4 = (f32[144,128]{1,0:T(8,128)S(1)}, f32[144,128]{1,0:T(8,128)S(1)}, u32[]{:S(2)}, u32[]{:S(2)}) collective-permute-start(f32[144,128]{1,0:T(8,128)S(1)} %get-tuple-element.45), channel_id=1, source_target_pairs={{0,4},{4,12},{8,0},{12,8},{16,20},{20,28},{24,16},{28,24},{1,5},{5... | collective-permute-start | bytes 221192 | tf_op jit(solution)/shard_map/ppermute | solution.py:236
  19.3 5.8 %collective-permute-start.5 = (f32[144,128]{1,0:T(8,128)S(1)}, f32[144,128]{1,0:T(8,128)S(1)}, u32[]{:S(2)}, u32[]{:S(2)}) collective-permute-start(f32[144,128]{1,0:T(8,128)S(1)} %get-tuple-element.47), channel_id=1, source_target_pairs={{0,12},{4,8},{8,4},{12,0},{16,28},{20,24},{24,20},{28,16},{1,13},{... | collective-permute-start | bytes 221192 | tf_op jit(solution)/shard_map/ppermute | solution.py:236
  20.8 5.1 %collective-permute-start.6 = (f32[144,128]{1,0:T(8,128)S(1)}, f32[144,128]{1,0:T(8,128)S(1)}, u32[]{:S(2)}, u32[]{:S(2)}) collective-permute-start(f32[144,128]{1,0:T(8,128)S(1)} %get-tuple-element.50), channel_id=1, source_target_pairs={{0,8},{4,0},{8,12},{12,4},{16,24},{20,16},{24,28},{28,20},{1,9},{5... | collective-permute-start | bytes 221192 | tf_op jit(solution)/shard_map/ppermute | solution.py:236
  25.9 8.3 %collective-permute-start.7 = (f32[96,128]{1,0:T(8,128)S(1)}, f32[96,128]{1,0:T(8,128)S(1)}, u32[]{:S(2)}, u32[]{:S(2)}) collective-permute-start(f32[96,128]{1,0:T(8,128)S(1)} %get-tuple-element.51.ahead), channel_id=1, source_target_pairs={{0,16},{4,20},{8,24},{12,28},{16,0},{20,4},{24,8},{28,12},{1,17},{... | collective-permute-start | bytes 147464 | tf_op jit(solution)/shard_map/ppermute | solution.py:230
  28.6 5.6 %collective-permute-start.9 = (f32[48,128]{1,0:T(8,128)S(1)}, f32[48,128]{1,0:T(8,128)S(1)}, u32[]{:S(2)}, u32[]{:S(2)}) collective-permute-start(f32[48,128]{1,0:T(8,128)S(1)} %get-tuple-element.52), channel_id=1, source_target_pairs={{0,18},{1,19},{2,16},{3,17},{4,22},{5,23},{6,20},{7,21},{8,26},{9,... | collective-permute-start | bytes 73736 | tf_op jit(solution)/shard_map/ppermute | solution.py:315
  29.0 5.2 %collective-permute-start.8 = (f32[48,128]{1,0:T(8,128)S(1)}, f32[48,128]{1,0:T(8,128)S(1)}, u32[]{:S(2)}, u32[]{:S(2)}) collective-permute-start(f32[48,128]{1,0:T(8,128)S(1)} %get-tuple-element.52), channel_id=1, source_target_pairs={{0,2},{1,3},{2,0},{3,1},{4,6},{5,7},{6,4},{7,5},{8,10},{9,11},{10,... | collective-permute-start | bytes 73736 | tf_op jit(solution)/shard_map/ppermute | solution.py:230
  34.5 6.0 %copy-start = (bf16[768,768]{1,0:T(8,128)(2,1)S(1)}, bf16[768,768]{1,0:T(8,128)(2,1)}, u32[]{:S(2)}) copy-start(bf16[768,768]{1,0:T(8,128)(2,1)} %wo.1) | copy-start | bytes 3538948
  34.6 3.7 %collective-permute-start.13 = (bf16[256,768]{1,0:T(8,128)(2,1)S(1)}, bf16[256,768]{1,0:T(8,128)(2,1)S(1)}, u32[]{:S(2)}, u32[]{:S(2)}) collective-permute-start(bf16[256,768]{1,0:T(8,128)(2,1)S(1)} %collective-permute-done.1.x), channel_id=1, source_target_pairs={{0,1},{1,0},{2,3},{3,2},{4,5},{5,4},{6,7},{7,6},{8,9},{9,8},{10,11... | collective-permute-start | bytes 1179656 | tf_op jit(solution)/shard_map/ppermute | solution.py:230
  34.6 4.5 %collective-permute-start.12 = (bf16[96,128]{1,0:T(8,128)(2,1)S(1)}, bf16[96,128]{1,0:T(8,128)(2,1)S(1)}, u32[]{:S(2)}, u32[]{:S(2)}) collective-permute-start(bf16[96,128]{1,0:T(8,128)(2,1)S(1)} %shard_map.62.p0), channel_id=1, source_target_pairs={{0,8},{4,0},{8,12},{12,4},{16,24},{20,16},{24,28},{28,20},{1,9},{5... | collective-permute-start | bytes 73736 | tf_op jit(solution)/shard_map/ppermute | solution.py:236
  35.5 4.7 %collective-permute-start.11 = (bf16[96,128]{1,0:T(8,128)(2,1)S(1)}, bf16[96,128]{1,0:T(8,128)(2,1)S(1)}, u32[]{:S(2)}, u32[]{:S(2)}) collective-permute-start(bf16[96,128]{1,0:T(8,128)(2,1)S(1)} %shard_map.62.p0), channel_id=1, source_target_pairs={{0,12},{4,8},{8,4},{12,0},{16,28},{20,24},{24,20},{28,16},{1,13},{... | collective-permute-start | bytes 73736 | tf_op jit(solution)/shard_map/ppermute | solution.py:236
  36.7 3.8 %collective-permute-start.10 = (bf16[96,128]{1,0:T(8,128)(2,1)S(1)}, bf16[96,128]{1,0:T(8,128)(2,1)S(1)}, u32[]{:S(2)}, u32[]{:S(2)}) collective-permute-start(bf16[96,128]{1,0:T(8,128)(2,1)S(1)} %shard_map.62.p0), channel_id=1, source_target_pairs={{0,4},{4,12},{8,0},{12,8},{16,20},{20,28},{24,16},{28,24},{1,5},{5... | collective-permute-start | bytes 73736 | tf_op jit(solution)/shard_map/ppermute | solution.py:236

commit v5 on v4

--- a/solution.py
+++ b/solution.py
@@ -90,9 +90,9 @@
     return n ^ (n >> 1)
 
 
-def ring_place():
-    me = lax.rem(lax.axis_index("seq"), GROUP)
-    return lax.bitwise_xor(me, lax.shift_right_logical(me, 1))
+def ring_place(other=0):
+    place = lax.bitwise_xor(lax.rem(lax.axis_index("seq"), GROUP), other)
+    return lax.bitwise_xor(place, lax.shift_right_logical(place, 1))
 
 
 def kernel_part(count, other, x, out, sems):
@@ -141,44 +141,46 @@
     return pl.ds(pl.multiple_of(came, half_width), half_width)
 
 
-def kernel_back(sites, x_far, kept, k, k_far, back, q_far):
+def kernel_back(sites, x_far, kept, k, k_far, back, q_far, total):
     embed, came = x_far.shape[1], rows_that_came(k_far.shape[1])
     keep_apart(matmul(x_far[...], kept[:embed, :]), sites, q_far)
     keep_apart(matmul(x_far[...], kept[embed : 2 * embed, :]), sites, k_far)
     for h in range(H):
         mine, both = slice(h * sites, (h + 1) * sites), slice(2 * h * sites, 2 * (h + 1) * sites)
-        back[mine, :] = against(q_far[mine, :], k[both, came])
-
-
-def kernel_ahead(sites, x_far_twin, kept, q, near, k_far, back, *refs):
-    parts, (k_twin, ahead) = refs[:GROUP], refs[GROUP:]
+        total[mine, :] = against(q_far[mine, :], k[both, came])
+    half = total.shape[0] // 2
+    back[...] = jnp.concatenate([total[:half, :], total[half:, :]], axis=1)
+
+
+def kernel_ahead(sites, x_far_twin, kept, q, k_far, ahead, k_twin):
     embed, came = x_far_twin.shape[1], rows_that_came(k_far.shape[1])
-    me = ring_place()
     keep_apart(matmul(x_far_twin[...], kept[embed : 2 * embed, :]), sites, k_twin)
     for h in range(H):
         mine = slice(h * sites, (h + 1) * sites)
         keys = jnp.concatenate([k_far[mine, :], k_twin[mine, :]], axis=0)
-        ahead[mine, :] = jnp.concatenate([near[mine, :], against(q[mine, came], keys)], axis=1)
-    size = H * sites // GROUP
-    for n in range(GROUP):
-        to = lax.rem(me + n, GROUP) * size
-        parts[n][:size, :] = ahead[pl.ds(to, size), :]
-        parts[n][size:, :] = jnp.concatenate(
-            [back[pl.ds(to, size // 2), :], back[pl.ds(to + size // 2, size // 2), :]], axis=1
-        )
-
-
-def kernel_sum(size, a, b, c, d, ahead, back):
-    ahead[...] = (a[:size, :] + b[:size, :]) + (c[:size, :] + d[:size, :])
-    back[...] = (a[size:, :] + b[size:, :]) + (c[size:, :] + d[size:, :])
-
-
-def kernel_softmax(scale, ahead, ahead_z, back_x, back_xz, out):
-    far = back_x[...] + back_xz[...]
-    half = far.shape[1] // 2
-    far = jnp.concatenate([far[:, :half], far[:, half:]], axis=0)
-    far = jnp.concatenate([jnp.zeros_like(far), far], axis=1)
-    logits = (ahead[...] + ahead_z[...] + far) * scale
+        ahead[mine, :] = against(q[mine, came], keys)
+
+
+def kernel_mix(near, ahead, back, *refs):
+    *parts, total = refs
+    half = near.shape[0] // 2
+    for rows, lanes in (
+        (slice(0, half), slice(0, near.shape[1])),
+        (slice(half, 2 * half), slice(near.shape[1], 2 * near.shape[1])),
+    ):
+        far = ahead[rows, :] + back[:, lanes]
+        total[rows, :] = jnp.concatenate([near[rows, :], far], axis=1)
+    me, size = ring_place(), total.shape[0] // GROUP
+    for n, part in enumerate(parts):
+        part[...] = total[pl.ds(lax.rem(me + n, GROUP) * size, size), :]
+
+
+def kernel_sum(a, b, c, d, out):
+    out[...] = (a[...] + b[...]) + (c[...] + d[...])
+
+
+def kernel_softmax(scale, mine, other, out):
+    logits = (mine[...] + other[...]) * scale
     e = jnp.exp(logits - jnp.max(logits, axis=1, keepdims=True))
     out[...] = (e / jnp.sum(e, axis=1, keepdims=True)).astype(BF16)
 
@@ -191,11 +193,10 @@
 
 def kernel_last(sites, p0, p1, p2, p3, v_near, v_first, v_second, wo, out, probs, att, mixed, sems):
     place = lax.axis_index("res") // 2
-    me = ring_place()
     size, width = H * sites // GROUP, v_first.shape[1]
     head = wo.shape[0] // H
     for n, p in enumerate((p0, p1, p2, p3)):
-        probs[pl.ds(lax.rem(me + GROUP - n, GROUP) * size, size), :] = p[...]
+        probs[pl.ds(ring_place(n) * size, size), :] = p[...]
     copies = []
     for far, half in ((v_first, 1 - place), (v_second, place)):
         came = pl.ds(pl.multiple_of(half * width, width), width)
@@ -239,7 +240,7 @@
 def body(x, wq, wk, wv, wo):
     rows, sites, embed = x.shape
     half, head = rows // 2, embed // H
-    n_seq, n_res = lax.axis_size("seq"), lax.axis_size("res")
+    n_seq = lax.axis_size("seq")
     scale = 1.0 / math.sqrt(head * rows * n_seq)
     flat, half_flat = (rows * sites, embed), (half * sites, embed)
     own = x.reshape(flat)
@@ -263,6 +264,8 @@
     def heads(blocks, count):
         return ((H * blocks * sites, count * head), BF16)
 
+    size = H * sites // GROUP
+    share = ((size, 4 * sites), F32)
     kept, q, k, v_near, near = call(
         functools.partial(kernel_near, rows, sites),
         [((3 * embed, embed), BF16), heads(1, rows), heads(2, rows), heads(2, rows), sums],
@@ -273,54 +276,48 @@
     )
     later, kept = lax.optimization_barrier((own, kept))
     sent_second = part(later, True)
-    far_second = swap(sent_second, "res", 2)
     far_first, kept, sent_second = lax.optimization_barrier((far_first, kept, sent_second))
     far_first_twin = swap(far_first, "res", 1)
     k_far, back = call(
         functools.partial(kernel_back, sites),
-        [heads(1, half), sums],
+        [heads(1, half), ((H * sites // 2, 4 * sites), F32)],
         (far_first, kept, k),
         cost,
+        [pltpu.VMEM(*heads(1, half)), pltpu.VMEM(*sums)],
+    )
+    back = swap(back, "res", 2)
+    far_first_twin, k_far, sent_second = lax.optimization_barrier(
+        (far_first_twin, k_far, sent_second)
+    )
+    far_second = swap(sent_second, "res", 2)
+    (ahead,) = call(
+        functools.partial(kernel_ahead, sites),
+        [sums],
+        (far_first_twin, kept, q, k_far),
+        cost,
         [pltpu.VMEM(*heads(1, half))],
     )
-    far_first_twin, k_far = lax.optimization_barrier((far_first_twin, k_far))
-    size = H * sites // GROUP
-    part_shape = (size + size // 2, 4 * sites)
-    parts = call(
-        functools.partial(kernel_ahead, sites),
-        [(part_shape, F32)] * GROUP,
-        (far_first_twin, kept, q, near, k_far, back),
-        cost,
-        [pltpu.VMEM(*heads(1, half)), pltpu.VMEM((H * sites, 4 * sites), F32)],
-    )
-    came = [turn(parts[k], k) for k in range(1, GROUP)]
-    came[0], kept = lax.optimization_barrier((came[0], kept))
+    wide = ((H * sites, 4 * sites), F32)
+    far = call(kernel_mix, [share] * GROUP, (near, ahead, back), 0, [pltpu.VMEM(*wide)])
+    far = [far[0]] + [turn(far[n], n) for n in range(1, GROUP)]
+    far[1], kept = lax.optimization_barrier((far[1], kept))
     (v_first,) = call(
         functools.partial(kernel_values, sites),
         [heads(2, half)],
         (far_first, far_first_twin, kept),
         cost,
     )
-    came[1], v_first = lax.optimization_barrier((came[1], v_first))
-    ahead, back = call(
-        functools.partial(kernel_sum, size),
-        [((size, 4 * sites), F32), ((size // 2, 4 * sites), F32)],
-        (parts[0], *came),
-    )
-    ahead_z = swap(ahead, "seq", GROUP)
-    back_x = swap(back, "res", 2)
-    cross = [
-        (s * n_res + r, (s ^ GROUP) * n_res + (r ^ 2)) for s in range(n_seq) for r in range(n_res)
-    ]
-    back_xz = lax.ppermute(back, ("seq", "res"), cross)
+    far[2], v_first = lax.optimization_barrier((far[2], v_first))
+    (mine,) = call(kernel_sum, [share], far)
     (probs,) = call(
         functools.partial(kernel_softmax, scale),
         [((size, 4 * sites), BF16)],
-        (ahead, ahead_z, back_x, back_xz),
+        (mine, swap(mine, "seq", GROUP)),
+        2000000000,
     )
     far_second, probs = lax.optimization_barrier((far_second, probs))
     far_second_twin = swap(far_second, "res", 1)
-    others = [turn(probs, k) for k in range(1, GROUP)]
+    others = [swap(probs, "seq", k) for k in range(1, GROUP)]
 
     (v_second,) = call(
         functools.partial(kernel_values, sites),

time: 43 us -> 42.5 us (0.988)
  starting transfers between devices: 17.4 us -> 16.5 us
  waiting for transfers between devices: 9.22 us -> 9.66 us
    ppermute x7 -> x10, waiting for transfers between devices: 1.28 us -> 7.96 us  [swap(): return lax.ppermute(x, axis, [(i, i ^ bit) for i in range(count)])]
    ppermute x1 -> x0, waiting for transfers between devices: 3.83 us -> none  [body(): back_xz = lax.ppermute(back, ('seq', 'res'), cross)]
    ppermute x6 -> x3, starting transfers between devices: 8.21 us -> 4.86 us  [turn(): return lax.ppermute(x, 'seq', list(enumerate(to)))]
    ppermute x7 -> x10, starting transfers between devices: 8.81 us -> 11.6 us  [swap(): return lax.ppermute(x, axis, [(i, i ^ bit) for i in range(count)])]
    ppermute x6 -> x3, waiting for transfers between devices: 4.12 us -> 1.7 us  [turn(): return lax.ppermute(x, 'seq', list(enumerate(to)))]
    pallas_call x10 -> x11, Pallas kernels: 15 us -> 15.1 us  [call(): pl.pallas_call(kernel, out_shape=shapes, in_specs=[pl.BlockSpec(memory_sp...]
  transfers between devices with their start and end apart: 14 -> 13, of which waited for: 6 -> 8; matrix products, arithmetic and copies ran while one was open for 0% -> 0% of each run, Pallas kernels for 27% -> 28%
where the time goes in v5:
time: 42.5 us; the launch traced here: 42.3 us
  starting transfers between devices  16.5 us (39%)
  Pallas kernels  15.1 us (36%)
  waiting for transfers between devices  9.66 us (23%)
  local copies, waits for them, and re-layouts  1.06 us (2%)
    pallas_call x11, Pallas kernels, call(): pl.pallas_call(kernel, out_shape=shapes, in_specs=[pl.BlockSpec(memory_sp...  15.1 us
    ppermute x10, starting transfers between devices, swap(): return lax.ppermute(x, axis, [(i, i ^ bit) for i in range(count)])  11.6 us
    ppermute x10, waiting for transfers between devices, swap(): return lax.ppermute(x, axis, [(i, i ^ bit) for i in range(count)])  7.96 us
    ppermute x3, starting transfers between devices, turn(): return lax.ppermute(x, 'seq', list(enumerate(to)))  4.86 us
    ppermute x3, waiting for transfers between devices, turn(): return lax.ppermute(x, 'seq', list(enumerate(to)))  1.7 us
    unnamed x6, local copies, waits for them, and re-layouts  1.06 us
  transfers between devices with their start and end apart: 13, of which 8 were waited for; matrix products, arithmetic and copies ran while one was open for 0% of the time, Pallas kernels for 28%

profile of v5, /device:TPU:0, one launch (start us, length us, event | category | flops | bytes accessed | tf_op | source)
XLA Modules:
  0.0 42.3 jit_solution(4806891253055069266)
XLA Ops:
  0.0 1.1 %shard_map.55 = bf16[256,768]{1,0:T(8,128)(2,1)S(1)} custom-call(bf16[512,768]{1,0:T(8,128)(2,1)} %bitcast.2), custom_call_target="tpu_custom_call" | custom-call | bytes 1179648 | tf_op jit(solution)/shard_map/pallas_call | solution.py:52
  1.8 2.5 %collective-permute-start = (bf16[256,768]{1,0:T(8,128)(2,1)S(1)}, bf16[256,768]{1,0:T(8,128)(2,1)S(1)}, u32[]{:S(2)}, u32[]{:S(2)}) collective-permute-start(bf16[256,768]{1,0:T(8,128)(2,1)S(1)} %shard_map.55), channel_id=1, source_target_pairs={{0,2},{1,3},{2,0},{3,1},{4,6},{5,7},{6,4},{7,5},{8,10},{9,11},{10,... | collective-permute-start | bytes 1179656 | tf_op jit(solution)/shard_map/ppermute | solution.py:231
  4.3 0.9 %copy-done.2 = bf16[512,768]{1,0:T(8,128)(2,1)} copy-done((bf16[512,768]{1,0:T(8,128)(2,1)}, bf16[512,768]{1,0:T(8,128)(2,1)S(1)}, u32[]{:S(2)}) %copy-start.2) | copy-done | bytes 786456
  5.1 6.5 %shard_map.56 = (bf16[2304,768]{1,0:T(8,128)(2,1)S(1)}, bf16[384,1024]{1,0:T(8,128)(2,1)S(1)}, bf16[768,1024]{1,0:T(8,128)(2,1)S(1)}, bf16[768,1024]{1,0:T(8,128)(2,1)S(1)}, f32[384,64]{1,0:T(8,128)S(1)}) custom-call(bf16[512,768]{1,0:T(8,128)(2,1)} %bitcast.3, bf16[512,768]{1,0:T(8,128)(2,1)} %copy-done.2, bf16[768,768]{1,0:T(8,128)(2,1)} %wq.1, ...), custom_call_target="tpu_custom_call" | custom-call | flops 3623878656 | bytes 12681216 | tf_op jit(solution)/shard_map/pallas_call | solution.py:52
  11.7 1.1 %shard_map.57 = bf16[256,768]{1,0:T(8,128)(2,1)S(1)} custom-call(bf16[512,768]{1,0:T(8,128)(2,1)} %bitcast.4), custom_call_target="tpu_custom_call" | custom-call | bytes 1179648 | tf_op jit(solution)/shard_map/pallas_call | solution.py:52
  12.8 1.3 %collective-permute-done.x_far.x = bf16[256,768]{1,0:T(8,128)(2,1)S(1)} collective-permute-done((bf16[256,768]{1,0:T(8,128)(2,1)S(1)}, bf16[256,768]{1,0:T(8,128)(2,1)S(1)}, u32[]{:S(2)}, u32[]{:S(2)}) %collective-permute-start) | collective-permute-done | bytes 393248 | tf_op jit(solution)/shard_map/ppermute | solution.py:231
  14.1 1.1 %shard_map.58 = (bf16[384,512]{1,0:T(8,128)(2,1)S(1)}, f32[192,128]{1,0:T(8,128)S(1)}) custom-call(bf16[256,768]{1,0:T(8,128)(2,1)S(1)} %collective-permute-done.x_far.x, bf16[2304,768]{1,0:T(8,128)(2,1)S(1)} %get-tuple-element.50.kept, bf16[768,1024]{1,0:T(8,128)(2,1)S(1)} %get-tuple-element.37.k), custom_call_target="tpu_custom_call" | custom-call | flops 603979776 | bytes 5996544 | tf_op jit(solution)/shard_map/pallas_call | solution.py:52
  15.1 1.8 %collective-permute-start.4 = (f32[192,128]{1,0:T(8,128)S(1)}, f32[192,128]{1,0:T(8,128)S(1)}, u32[]{:S(2)}, u32[]{:S(2)}) collective-permute-start(f32[192,128]{1,0:T(8,128)S(1)} %get-tuple-element.45), channel_id=1, source_target_pairs={{0,2},{1,3},{2,0},{3,1},{4,6},{5,7},{6,4},{7,5},{8,10},{9,11},{10,... | collective-permute-start | bytes 294920 | tf_op jit(solution)/shard_map/ppermute | solution.py:231
  17.5 0.9 %shard_map.59.ahead = f32[384,64]{1,0:T(8,128)S(1)} custom-call(bf16[256,768]{1,0:T(8,128)(2,1)S(1)} %collective-permute-done.2.x_far_twin.x_twin, bf16[2304,768]{1,0:T(8,128)(2,1)S(1)} %get-tuple-element.50.kept, bf16[384,1024]{1,0:T(8,128)(2,1)S(1)} %get-tuple-element.43.q, bf16[384,512]{1,0:T(8,128)(2,1)S(1)} %get-tuple-element.44.k_far), custom_call_target="tpu_custom_call" | custom-call | flops 603979776 | bytes 5210112 | tf_op jit(solution)/shard_map/pallas_call | solution.py:52
  18.4 2.4 %collective-permute-done.4.back = f32[192,128]{1,0:T(8,128)S(1)} collective-permute-done((f32[192,128]{1,0:T(8,128)S(1)}, f32[192,128]{1,0:T(8,128)S(1)}, u32[]{:S(2)}, u32[]{:S(2)}) %collective-permute-start.4) | collective-permute-done | bytes 98336 | tf_op jit(solution)/shard_map/ppermute | solution.py:231
  21.0 1.8 %collective-permute-start.5 = (f32[96,128]{1,0:T(8,128)S(1)}, f32[96,128]{1,0:T(8,128)S(1)}, u32[]{:S(2)}, u32[]{:S(2)}) collective-permute-start(f32[96,128]{1,0:T(8,128)S(1)} %get-tuple-element.47), channel_id=1, source_target_pairs={{0,4},{4,12},{8,0},{12,8},{16,20},{20,28},{24,16},{28,24},{1,5},{5... | collective-permute-start | bytes 147464 | tf_op jit(solution)/shard_map/ppermute | solution.py:237
  22.8 1.5 %collective-permute-start.6 = (f32[96,128]{1,0:T(8,128)S(1)}, f32[96,128]{1,0:T(8,128)S(1)}, u32[]{:S(2)}, u32[]{:S(2)}) collective-permute-start(f32[96,128]{1,0:T(8,128)S(1)} %get-tuple-element.49), channel_id=1, source_target_pairs={{0,12},{4,8},{8,4},{12,0},{16,28},{20,24},{24,20},{28,16},{1,13},{... | collective-permute-start | bytes 147464 | tf_op jit(solution)/shard_map/ppermute | solution.py:237
  24.3 1.5 %collective-permute-start.7 = (f32[96,128]{1,0:T(8,128)S(1)}, f32[96,128]{1,0:T(8,128)S(1)}, u32[]{:S(2)}, u32[]{:S(2)}) collective-permute-start(f32[96,128]{1,0:T(8,128)S(1)} %get-tuple-element.52), channel_id=1, source_target_pairs={{0,8},{4,0},{8,12},{12,4},{16,24},{20,16},{24,28},{28,20},{1,9},{5... | collective-permute-start | bytes 147464 | tf_op jit(solution)/shard_map/ppermute | solution.py:237
  25.8 0.9 %shard_map.61.v_first = bf16[768,512]{1,0:T(8,128)(2,1)S(1)} custom-call(bf16[256,768]{1,0:T(8,128)(2,1)S(1)} %collective-permute-done.x_far.x, bf16[256,768]{1,0:T(8,128)(2,1)S(1)} %collective-permute-done.2.x_far_twin.x_twin, bf16[2304,768]{1,0:T(8,128)(2,1)S(1)} %get-tuple-element.50.kept), custom_call_target="tpu_custom_call" | custom-call | flops 603979776 | bytes 5111808 | tf_op jit(solution)/shard_map/pallas_call | solution.py:52
  26.7 1.1 %collective-permute-done.6.c = f32[96,128]{1,0:T(8,128)S(1)} collective-permute-done((f32[96,128]{1,0:T(8,128)S(1)}, f32[96,128]{1,0:T(8,128)S(1)}, u32[]{:S(2)}, u32[]{:S(2)}) %collective-permute-start.6) | collective-permute-done | bytes 49184 | tf_op jit(solution)/shard_map/ppermute | solution.py:237
  27.8 0.6 %collective-permute-done.7.d = f32[96,128]{1,0:T(8,128)S(1)} collective-permute-done((f32[96,128]{1,0:T(8,128)S(1)}, f32[96,128]{1,0:T(8,128)S(1)}, u32[]{:S(2)}, u32[]{:S(2)}) %collective-permute-start.7) | collective-permute-done | bytes 49184 | tf_op jit(solution)/shard_map/ppermute | solution.py:237
  28.4 2.7 %collective-permute-start.8 = (f32[96,128]{1,0:T(8,128)S(1)}, f32[96,128]{1,0:T(8,128)S(1)}, u32[]{:S(2)}, u32[]{:S(2)}) collective-permute-start(f32[96,128]{1,0:T(8,128)S(1)} %shard_map.62.mine), channel_id=1, source_target_pairs={{0,16},{4,20},{8,24},{12,28},{16,0},{20,4},{24,8},{28,12},{1,17},{... | collective-permute-start | bytes 147464 | tf_op jit(solution)/shard_map/ppermute | solution.py:231
  31.1 2.4 %collective-permute-done.8.other = f32[96,128]{1,0:T(8,128)S(1)} collective-permute-done((f32[96,128]{1,0:T(8,128)S(1)}, f32[96,128]{1,0:T(8,128)S(1)}, u32[]{:S(2)}, u32[]{:S(2)}) %collective-permute-start.8) | collective-permute-done | bytes 49184 | tf_op jit(solution)/shard_map/ppermute | solution.py:231
  33.7 1.6 %collective-permute-start.11 = (bf16[96,128]{1,0:T(8,128)(2,1)S(1)}, bf16[96,128]{1,0:T(8,128)(2,1)S(1)}, u32[]{:S(2)}, u32[]{:S(2)}) collective-permute-start(bf16[96,128]{1,0:T(8,128)(2,1)S(1)} %shard_map.63.p0), channel_id=1, source_target_pairs={{0,12},{4,8},{8,4},{12,0},{16,28},{20,24},{24,20},{28,16},{1,13},{... | collective-permute-start | bytes 73736 | tf_op jit(solution)/shard_map/ppermute | solution.py:231
  35.3 0.9 %collective-permute-start.10 = (bf16[96,128]{1,0:T(8,128)(2,1)S(1)}, bf16[96,128]{1,0:T(8,128)(2,1)S(1)}, u32[]{:S(2)}, u32[]{:S(2)}) collective-permute-start(bf16[96,128]{1,0:T(8,128)(2,1)S(1)} %shard_map.63.p0), channel_id=1, source_target_pairs={{0,8},{4,12},{8,0},{12,4},{16,24},{20,28},{24,16},{28,20},{1,9},{5... | collective-permute-start | bytes 73736 | tf_op jit(solution)/shard_map/ppermute | solution.py:231
  36.2 1.1 %collective-permute-start.9 = (bf16[96,128]{1,0:T(8,128)(2,1)S(1)}, bf16[96,128]{1,0:T(8,128)(2,1)S(1)}, u32[]{:S(2)}, u32[]{:S(2)}) collective-permute-start(bf16[96,128]{1,0:T(8,128)(2,1)S(1)} %shard_map.63.p0), channel_id=1, source_target_pairs={{0,4},{4,0},{8,12},{12,8},{16,20},{20,16},{24,28},{28,24},{1,5},{5... | collective-permute-start | bytes 73736 | tf_op jit(solution)/shard_map/ppermute | solution.py:231
  37.3 0.9 %shard_map.64.v_second = bf16[768,512]{1,0:T(8,128)(2,1)S(1)} custom-call(bf16[256,768]{1,0:T(8,128)(2,1)S(1)} %collective-permute-done.3.x, bf16[256,768]{1,0:T(8,128)(2,1)S(1)} %collective-permute-done.12.x_twin, bf16[2304,768]{1,0:T(8,128)(2,1)S(1)} %get-tuple-element.50.kept), custom_call_target="tpu_custom_call" | custom-call | flops 603979776 | bytes 5111808 | tf_op jit(solution)/shard_map/pallas_call | solution.py:52
  39.1 0.9 %collective-permute-done.9.p1 = bf16[96,128]{1,0:T(8,128)(2,1)S(1)} collective-permute-done((bf16[96,128]{1,0:T(8,128)(2,1)S(1)}, bf16[96,128]{1,0:T(8,128)(2,1)S(1)}, u32[]{:S(2)}, u32[]{:S(2)}) %collective-permute-start.9) | collective-permute-done | bytes 24608 | tf_op jit(solution)/shard_map/ppermute | solution.py:231
  40.1 2.3 %shard_map.65 = bf16[512,768]{1,0:T(8,128)(2,1)} custom-call(bf16[96,128]{1,0:T(8,128)(2,1)S(1)} %shard_map.63.p0, bf16[96,128]{1,0:T(8,128)(2,1)S(1)} %collective-permute-done.9.p1, bf16[96,128]{1,0:T(8,128)(2,1)S(1)} %collective-permute-done.10.p2, bf16[96,128]{1,0:T(8,128)(2,1)S(1)} %collective-permute-done.11.p3, ...), custom_call_target="tpu_custom_call" | custom-call | flops 1207959552 | bytes 5210112 | tf_op jit(solution)/shard_map/pallas_call | solution.py:52
  (19 shorter events, 2.6 us)
Async XLA Ops:
  0.0 1.3 %copy-start.1 = (bf16[16,32,768]{2,1,0:T(8,128)(2,1)S(1)}, bf16[16,32,768]{2,1,0:T(8,128)(2,1)}, u32[]{:S(2)}) copy-start(bf16[16,32,768]{2,1,0:T(8,128)(2,1)} %param.5) | copy-start | bytes 2359300
  1.3 2.9 %collective-permute-start.1 = (bf16[512,768]{1,0:T(8,128)(2,1)S(1)}, bf16[512,768]{1,0:T(8,128)(2,1)S(1)}, u32[]{:S(2)}, u32[]{:S(2)}) collective-permute-start(bf16[512,768]{1,0:T(8,128)(2,1)S(1)} %bitcast.5), channel_id=1, source_target_pairs={{0,1},{1,0},{2,3},{3,2},{4,5},{5,4},{6,7},{7,6},{8,9},{9,8},{10,11... | collective-permute-start | bytes 2359304 | tf_op jit(solution)/shard_map/ppermute | solution.py:231
  1.8 12.3 %collective-permute-start = (bf16[256,768]{1,0:T(8,128)(2,1)S(1)}, bf16[256,768]{1,0:T(8,128)(2,1)S(1)}, u32[]{:S(2)}, u32[]{:S(2)}) collective-permute-start(bf16[256,768]{1,0:T(8,128)(2,1)S(1)} %shard_map.55), channel_id=1, source_target_pairs={{0,2},{1,3},{2,0},{3,1},{4,6},{5,7},{6,4},{7,5},{8,10},{9,11},{10,... | collective-permute-start | bytes 1179656 | tf_op jit(solution)/shard_map/ppermute | solution.py:231
  4.3 0.9 %copy-start.2 = (bf16[512,768]{1,0:T(8,128)(2,1)}, bf16[512,768]{1,0:T(8,128)(2,1)S(1)}, u32[]{:S(2)}) copy-start(bf16[512,768]{1,0:T(8,128)(2,1)S(1)} %collective-permute-done.1.twin) | copy-start | bytes 2359300
  14.0 2.9 %collective-permute-start.2 = (bf16[256,768]{1,0:T(8,128)(2,1)S(1)}, bf16[256,768]{1,0:T(8,128)(2,1)S(1)}, u32[]{:S(2)}, u32[]{:S(2)}) collective-permute-start(bf16[256,768]{1,0:T(8,128)(2,1)S(1)} %collective-permute-done.x_far.x), channel_id=1, source_target_pairs={{0,1},{1,0},{2,3},{3,2},{4,5},{5,4},{6,7},{7,6},{8,9},{9,8},{10,11... | collective-permute-start | bytes 1179656 | tf_op jit(solution)/shard_map/ppermute | solution.py:231
  15.1 5.7 %collective-permute-start.4 = (f32[192,128]{1,0:T(8,128)S(1)}, f32[192,128]{1,0:T(8,128)S(1)}, u32[]{:S(2)}, u32[]{:S(2)}) collective-permute-start(f32[192,128]{1,0:T(8,128)S(1)} %get-tuple-element.45), channel_id=1, source_target_pairs={{0,2},{1,3},{2,0},{3,1},{4,6},{5,7},{6,4},{7,5},{8,10},{9,11},{10,... | collective-permute-start | bytes 294920 | tf_op jit(solution)/shard_map/ppermute | solution.py:231
  16.9 16.7 %collective-permute-start.3 = (bf16[256,768]{1,0:T(8,128)(2,1)S(1)}, bf16[256,768]{1,0:T(8,128)(2,1)S(1)}, u32[]{:S(2)}, u32[]{:S(2)}) collective-permute-start(bf16[256,768]{1,0:T(8,128)(2,1)S(1)} %shard_map.57), channel_id=1, source_target_pairs={{0,2},{1,3},{2,0},{3,1},{4,6},{5,7},{6,4},{7,5},{8,10},{9,11},{10,... | collective-permute-start | bytes 1179656 | tf_op jit(solution)/shard_map/ppermute | solution.py:231
  21.0 4.9 %collective-permute-start.5 = (f32[96,128]{1,0:T(8,128)S(1)}, f32[96,128]{1,0:T(8,128)S(1)}, u32[]{:S(2)}, u32[]{:S(2)}) collective-permute-start(f32[96,128]{1,0:T(8,128)S(1)} %get-tuple-element.47), channel_id=1, source_target_pairs={{0,4},{4,12},{8,0},{12,8},{16,20},{20,28},{24,16},{28,24},{1,5},{5... | collective-permute-start | bytes 147464 | tf_op jit(solution)/shard_map/ppermute | solution.py:237
  22.8 5.0 %collective-permute-start.6 = (f32[96,128]{1,0:T(8,128)S(1)}, f32[96,128]{1,0:T(8,128)S(1)}, u32[]{:S(2)}, u32[]{:S(2)}) collective-permute-start(f32[96,128]{1,0:T(8,128)S(1)} %get-tuple-element.49), channel_id=1, source_target_pairs={{0,12},{4,8},{8,4},{12,0},{16,28},{20,24},{24,20},{28,16},{1,13},{... | collective-permute-start | bytes 147464 | tf_op jit(solution)/shard_map/ppermute | solution.py:237
  24.3 4.1 %collective-permute-start.7 = (f32[96,128]{1,0:T(8,128)S(1)}, f32[96,128]{1,0:T(8,128)S(1)}, u32[]{:S(2)}, u32[]{:S(2)}) collective-permute-start(f32[96,128]{1,0:T(8,128)S(1)} %get-tuple-element.52), channel_id=1, source_target_pairs={{0,8},{4,0},{8,12},{12,4},{16,24},{20,16},{24,28},{28,20},{1,9},{5... | collective-permute-start | bytes 147464 | tf_op jit(solution)/shard_map/ppermute | solution.py:237
  28.4 5.1 %collective-permute-start.8 = (f32[96,128]{1,0:T(8,128)S(1)}, f32[96,128]{1,0:T(8,128)S(1)}, u32[]{:S(2)}, u32[]{:S(2)}) collective-permute-start(f32[96,128]{1,0:T(8,128)S(1)} %shard_map.62.mine), channel_id=1, source_target_pairs={{0,16},{4,20},{8,24},{12,28},{16,0},{20,4},{24,8},{28,12},{1,17},{... | collective-permute-start | bytes 147464 | tf_op jit(solution)/shard_map/ppermute | solution.py:231
  33.6 6.4 %copy-start = (bf16[768,768]{1,0:T(8,128)(2,1)S(1)}, bf16[768,768]{1,0:T(8,128)(2,1)}, u32[]{:S(2)}) copy-start(bf16[768,768]{1,0:T(8,128)(2,1)} %wo.1) | copy-start | bytes 3538948
  33.7 3.6 %collective-permute-start.12 = (bf16[256,768]{1,0:T(8,128)(2,1)S(1)}, bf16[256,768]{1,0:T(8,128)(2,1)S(1)}, u32[]{:S(2)}, u32[]{:S(2)}) collective-permute-start(bf16[256,768]{1,0:T(8,128)(2,1)S(1)} %collective-permute-done.3.x), channel_id=1, source_target_pairs={{0,1},{1,0},{2,3},{3,2},{4,5},{5,4},{6,7},{7,6},{8,9},{9,8},{10,11... | collective-permute-start | bytes 1179656 | tf_op jit(solution)/shard_map/ppermute | solution.py:231
  33.7 4.8 %collective-permute-start.11 = (bf16[96,128]{1,0:T(8,128)(2,1)S(1)}, bf16[96,128]{1,0:T(8,128)(2,1)S(1)}, u32[]{:S(2)}, u32[]{:S(2)}) collective-permute-start(bf16[96,128]{1,0:T(8,128)(2,1)S(1)} %shard_map.63.p0), channel_id=1, source_target_pairs={{0,12},{4,8},{8,4},{12,0},{16,28},{20,24},{24,20},{28,16},{1,13},{... | collective-permute-start | bytes 73736 | tf_op jit(solution)/shard_map/ppermute | solution.py:231
  35.3 3.8 %collective-permute-start.10 = (bf16[96,128]{1,0:T(8,128)(2,1)S(1)}, bf16[96,128]{1,0:T(8,128)(2,1)S(1)}, u32[]{:S(2)}, u32[]{:S(2)}) collective-permute-start(bf16[96,128]{1,0:T(8,128)(2,1)S(1)} %shard_map.63.p0), channel_id=1, source_target_pairs={{0,8},{4,12},{8,0},{12,4},{16,24},{20,28},{24,16},{28,20},{1,9},{5... | collective-permute-start | bytes 73736 | tf_op jit(solution)/shard_map/ppermute | solution.py:231
  36.2 3.8 %collective-permute-start.9 = (bf16[96,128]{1,0:T(8,128)(2,1)S(1)}, bf16[96,128]{1,0:T(8,128)(2,1)S(1)}, u32[]{:S(2)}, u32[]{:S(2)}) collective-permute-start(bf16[96,128]{1,0:T(8,128)(2,1)S(1)} %shard_map.63.p0), channel_id=1, source_target_pairs={{0,4},{4,0},{8,12},{12,8},{16,20},{20,16},{24,28},{28,24},{1,5},{5... | collective-permute-start | bytes 73736 | tf_op jit(solution)/shard_map/ppermute | solution.py:231

commit v6 on v5

--- a/solution.py
+++ b/solution.py
@@ -141,10 +141,9 @@
     return pl.ds(pl.multiple_of(came, half_width), half_width)
 
 
-def kernel_back(sites, x_far, kept, k, k_far, back, q_far, total):
-    embed, came = x_far.shape[1], rows_that_came(k_far.shape[1])
+def kernel_back(sites, x_far, kept, k, back, q_far, total):
+    embed, came = x_far.shape[1], rows_that_came(q_far.shape[1])
     keep_apart(matmul(x_far[...], kept[:embed, :]), sites, q_far)
-    keep_apart(matmul(x_far[...], kept[embed : 2 * embed, :]), sites, k_far)
     for h in range(H):
         mine, both = slice(h * sites, (h + 1) * sites), slice(2 * h * sites, 2 * (h + 1) * sites)
         total[mine, :] = against(q_far[mine, :], k[both, came])
@@ -152,8 +151,9 @@
     back[...] = jnp.concatenate([total[:half, :], total[half:, :]], axis=1)
 
 
-def kernel_ahead(sites, x_far_twin, kept, q, k_far, ahead, k_twin):
+def kernel_ahead(sites, x_far, x_far_twin, kept, q, ahead, k_far, k_twin):
     embed, came = x_far_twin.shape[1], rows_that_came(k_far.shape[1])
+    keep_apart(matmul(x_far[...], kept[embed : 2 * embed, :]), sites, k_far)
     keep_apart(matmul(x_far_twin[...], kept[embed : 2 * embed, :]), sites, k_twin)
     for h in range(H):
         mine = slice(h * sites, (h + 1) * sites)
@@ -197,9 +197,9 @@
     head = wo.shape[0] // H
     for n, p in enumerate((p0, p1, p2, p3)):
         probs[pl.ds(ring_place(n) * size, size), :] = p[...]
-    copies = []
-    for far, half in ((v_first, 1 - place), (v_second, place)):
-        came = pl.ds(pl.multiple_of(half * width, width), width)
+    rows, halves = out.shape[0] // 2, (1 - place, place)
+    for n, far in enumerate((v_first, v_second)):
+        came = pl.ds(pl.multiple_of(halves[n] * width, width), width)
         for h in range(0, H, 2):
             pair = []
             for one in (h, h + 1):
@@ -208,20 +208,20 @@
                 p = probs[one * sites : (one + 1) * sites, :]
                 pair.append(matmul(p, v))
             for r in range(width // head):
-                lanes = slice(r * head, (r + 1) * head)
-                att[r * sites : (r + 1) * sites, h * head : (h + 2) * head] = jnp.concatenate(
+                lanes, to = slice(r * head, (r + 1) * head), n * rows + r * sites
+                att[to : to + sites, h * head : (h + 2) * head] = jnp.concatenate(
                     [pair[0][:, lanes], pair[1][:, lanes]], axis=1
                 )
-        rows = att.shape[0]
-        piece = 2 * rows // sems.shape[0]
-        for start in range(0, rows, piece):
-            n = len(copies)
-            mixed[n * piece : (n + 1) * piece, :] = matmul(att[start : start + piece, :], wo[...])
-            target = out.at[pl.ds(half * rows + start, piece)]
-            copies.append(
-                pltpu.make_async_copy(mixed.at[pl.ds(n * piece, piece)], target, sems.at[n])
-            )
-            copies[n].start()
+    copies = []
+    piece = 2 * wo.shape[1] // sems.shape[0]
+    for start in range(0, wo.shape[1], piece):
+        lanes = slice(start, start + piece)
+        mixed[:, lanes] = matmul(att[...], wo[:, lanes])
+        for n, half in enumerate(halves):
+            source = mixed.at[n * rows : (n + 1) * rows, lanes]
+            target = out.at[pl.ds(half * rows, rows), lanes]
+            copies.append(pltpu.make_async_copy(source, target, sems.at[len(copies)]))
+            copies[-1].start()
     for copy in copies:
         copy.wait()
 
@@ -278,24 +278,24 @@
     sent_second = part(later, True)
     far_first, kept, sent_second = lax.optimization_barrier((far_first, kept, sent_second))
     far_first_twin = swap(far_first, "res", 1)
-    k_far, back = call(
+    (sent_back,) = call(
         functools.partial(kernel_back, sites),
-        [heads(1, half), ((H * sites // 2, 4 * sites), F32)],
+        [((H * sites // 2, 4 * sites), F32)],
         (far_first, kept, k),
         cost,
         [pltpu.VMEM(*heads(1, half)), pltpu.VMEM(*sums)],
     )
-    back = swap(back, "res", 2)
-    far_first_twin, k_far, sent_second = lax.optimization_barrier(
-        (far_first_twin, k_far, sent_second)
+    back = swap(sent_back, "res", 2)
+    far_first_twin, sent_back, sent_second = lax.optimization_barrier(
+        (far_first_twin, sent_back, sent_second)
     )
     far_second = swap(sent_second, "res", 2)
     (ahead,) = call(
         functools.partial(kernel_ahead, sites),
         [sums],
-        (far_first_twin, kept, q, k_far),
+        (far_first, far_first_twin, kept, q),
         cost,
-        [pltpu.VMEM(*heads(1, half))],
+        [pltpu.VMEM(*heads(1, half)), pltpu.VMEM(*heads(1, half))],
     )
     wide = ((H * sites, 4 * sites), F32)
     far = call(kernel_mix, [share] * GROUP, (near, ahead, back), 0, [pltpu.VMEM(*wide)])
@@ -332,9 +332,9 @@
         2 * cost,
         [
             pltpu.VMEM((H * sites, 4 * sites), BF16),
-            pltpu.VMEM(half_flat, BF16),
             pltpu.VMEM(flat, BF16),
-            pltpu.SemaphoreType.DMA((4,)),
+            pltpu.VMEM(flat, BF16),
+            pltpu.SemaphoreType.DMA((2 * H // GROUP,)),
         ],
         to=pltpu.HBM,
     )

time: 42.5 us -> 42.2 us (level)
  no operation moved by 1% of the time
where the time goes in v6:
time: 42.2 us; the launch traced here: 42 us
  starting transfers between devices  16.6 us (39%)
  Pallas kernels  15 us (36%)
  waiting for transfers between devices  9.26 us (22%)
  local copies, waits for them, and re-layouts  1.06 us (3%)
    pallas_call x11, Pallas kernels, call(): pl.pallas_call(kernel, out_shape=shapes, in_specs=[pl.BlockSpec(memory_sp...  15 us
    ppermute x10, starting transfers between devices, swap(): return lax.ppermute(x, axis, [(i, i ^ bit) for i in range(count)])  11.8 us
    ppermute x10, waiting for transfers between devices, swap(): return lax.ppermute(x, axis, [(i, i ^ bit) for i in range(count)])  7.55 us
    ppermute x3, starting transfers between devices, turn(): return lax.ppermute(x, 'seq', list(enumerate(to)))  4.86 us
    ppermute x3, waiting for transfers between devices, turn(): return lax.ppermute(x, 'seq', list(enumerate(to)))  1.71 us
    unnamed x6, local copies, waits for them, and re-layouts  1.06 us
  transfers between devices with their start and end apart: 13, of which 8 were waited for; matrix products, arithmetic and copies ran while one was open for 0% of the time, Pallas kernels for 28%

profile of v6, /device:TPU:0, one launch (start us, length us, event | category | flops | bytes accessed | tf_op | source)
XLA Modules:
  0.0 42.0 jit_solution(16824974904506123943)
XLA Ops:
  0.0 1.1 %shard_map.55 = bf16[256,768]{1,0:T(8,128)(2,1)S(1)} custom-call(bf16[512,768]{1,0:T(8,128)(2,1)} %bitcast.2), custom_call_target="tpu_custom_call" | custom-call | bytes 1179648 | tf_op jit(solution)/shard_map/pallas_call | solution.py:52
  1.8 2.5 %collective-permute-start = (bf16[256,768]{1,0:T(8,128)(2,1)S(1)}, bf16[256,768]{1,0:T(8,128)(2,1)S(1)}, u32[]{:S(2)}, u32[]{:S(2)}) collective-permute-start(bf16[256,768]{1,0:T(8,128)(2,1)S(1)} %shard_map.55), channel_id=1, source_target_pairs={{0,2},{1,3},{2,0},{3,1},{4,6},{5,7},{6,4},{7,5},{8,10},{9,11},{10,... | collective-permute-start | bytes 1179656 | tf_op jit(solution)/shard_map/ppermute | solution.py:231
  4.3 0.9 %copy-done.2 = bf16[512,768]{1,0:T(8,128)(2,1)} copy-done((bf16[512,768]{1,0:T(8,128)(2,1)}, bf16[512,768]{1,0:T(8,128)(2,1)S(1)}, u32[]{:S(2)}) %copy-start.2) | copy-done | bytes 786456
  5.1 6.5 %shard_map.56 = (bf16[2304,768]{1,0:T(8,128)(2,1)S(1)}, bf16[384,1024]{1,0:T(8,128)(2,1)S(1)}, bf16[768,1024]{1,0:T(8,128)(2,1)S(1)}, bf16[768,1024]{1,0:T(8,128)(2,1)S(1)}, f32[384,64]{1,0:T(8,128)S(1)}) custom-call(bf16[512,768]{1,0:T(8,128)(2,1)} %bitcast.3, bf16[512,768]{1,0:T(8,128)(2,1)} %copy-done.2, bf16[768,768]{1,0:T(8,128)(2,1)} %wq.1, ...), custom_call_target="tpu_custom_call" | custom-call | flops 3623878656 | bytes 12681216 | tf_op jit(solution)/shard_map/pallas_call | solution.py:52
  11.7 1.1 %shard_map.57 = bf16[256,768]{1,0:T(8,128)(2,1)S(1)} custom-call(bf16[512,768]{1,0:T(8,128)(2,1)} %bitcast.4), custom_call_target="tpu_custom_call" | custom-call | bytes 1179648 | tf_op jit(solution)/shard_map/pallas_call | solution.py:52
  12.8 1.3 %collective-permute-done.x_far.x = bf16[256,768]{1,0:T(8,128)(2,1)S(1)} collective-permute-done((bf16[256,768]{1,0:T(8,128)(2,1)S(1)}, bf16[256,768]{1,0:T(8,128)(2,1)S(1)}, u32[]{:S(2)}, u32[]{:S(2)}) %collective-permute-start) | collective-permute-done | bytes 393248 | tf_op jit(solution)/shard_map/ppermute | solution.py:231
  14.1 0.9 %shard_map.58 = f32[192,128]{1,0:T(8,128)S(1)} custom-call(bf16[256,768]{1,0:T(8,128)(2,1)S(1)} %collective-permute-done.x_far.x, bf16[2304,768]{1,0:T(8,128)(2,1)S(1)} %get-tuple-element.44.kept, bf16[768,1024]{1,0:T(8,128)(2,1)S(1)} %get-tuple-element.34.k), custom_call_target="tpu_custom_call" | custom-call | flops 603979776 | bytes 5603328 | tf_op jit(solution)/shard_map/pallas_call | solution.py:52
  15.0 1.8 %collective-permute-start.4 = (f32[192,128]{1,0:T(8,128)S(1)}, f32[192,128]{1,0:T(8,128)S(1)}, u32[]{:S(2)}, u32[]{:S(2)}) collective-permute-start(f32[192,128]{1,0:T(8,128)S(1)} %shard_map.58), channel_id=1, source_target_pairs={{0,2},{1,3},{2,0},{3,1},{4,6},{5,7},{6,4},{7,5},{8,10},{9,11},{10,... | collective-permute-start | bytes 294920 | tf_op jit(solution)/shard_map/ppermute | solution.py:231
  16.8 0.7 %collective-permute-start.3 = (bf16[256,768]{1,0:T(8,128)(2,1)S(1)}, bf16[256,768]{1,0:T(8,128)(2,1)S(1)}, u32[]{:S(2)}, u32[]{:S(2)}) collective-permute-start(bf16[256,768]{1,0:T(8,128)(2,1)S(1)} %shard_map.57), channel_id=1, source_target_pairs={{0,2},{1,3},{2,0},{3,1},{4,6},{5,7},{6,4},{7,5},{8,10},{9,11},{10,... | collective-permute-start | bytes 1179656 | tf_op jit(solution)/shard_map/ppermute | solution.py:231
  17.5 1.1 %shard_map.59.ahead = f32[384,64]{1,0:T(8,128)S(1)} custom-call(bf16[256,768]{1,0:T(8,128)(2,1)S(1)} %collective-permute-done.x_far.x, bf16[256,768]{1,0:T(8,128)(2,1)S(1)} %collective-permute-done.2.x_far_twin.x_twin, bf16[2304,768]{1,0:T(8,128)(2,1)S(1)} %get-tuple-element.44.kept, bf16[384,1024]{1,0:T(8,128)(2,1)S(1)} %get-tuple-element.39.q), custom_call_target="tpu_custom_call" | custom-call | flops 603979776 | bytes 5210112 | tf_op jit(solution)/shard_map/pallas_call | solution.py:52
  18.6 2.0 %collective-permute-done.4.back = f32[192,128]{1,0:T(8,128)S(1)} collective-permute-done((f32[192,128]{1,0:T(8,128)S(1)}, f32[192,128]{1,0:T(8,128)S(1)}, u32[]{:S(2)}, u32[]{:S(2)}) %collective-permute-start.4) | collective-permute-done | bytes 98336 | tf_op jit(solution)/shard_map/ppermute | solution.py:231
  20.8 1.8 %collective-permute-start.5 = (f32[96,128]{1,0:T(8,128)S(1)}, f32[96,128]{1,0:T(8,128)S(1)}, u32[]{:S(2)}, u32[]{:S(2)}) collective-permute-start(f32[96,128]{1,0:T(8,128)S(1)} %get-tuple-element.41), channel_id=1, source_target_pairs={{0,4},{4,12},{8,0},{12,8},{16,20},{20,28},{24,16},{28,24},{1,5},{5... | collective-permute-start | bytes 147464 | tf_op jit(solution)/shard_map/ppermute | solution.py:237
  22.6 1.5 %collective-permute-start.6 = (f32[96,128]{1,0:T(8,128)S(1)}, f32[96,128]{1,0:T(8,128)S(1)}, u32[]{:S(2)}, u32[]{:S(2)}) collective-permute-start(f32[96,128]{1,0:T(8,128)S(1)} %get-tuple-element.43), channel_id=1, source_target_pairs={{0,12},{4,8},{8,4},{12,0},{16,28},{20,24},{24,20},{28,16},{1,13},{... | collective-permute-start | bytes 147464 | tf_op jit(solution)/shard_map/ppermute | solution.py:237
  24.2 1.5 %collective-permute-start.7 = (f32[96,128]{1,0:T(8,128)S(1)}, f32[96,128]{1,0:T(8,128)S(1)}, u32[]{:S(2)}, u32[]{:S(2)}) collective-permute-start(f32[96,128]{1,0:T(8,128)S(1)} %get-tuple-element.46), channel_id=1, source_target_pairs={{0,8},{4,0},{8,12},{12,4},{16,24},{20,16},{24,28},{28,20},{1,9},{5... | collective-permute-start | bytes 147464 | tf_op jit(solution)/shard_map/ppermute | solution.py:237
  25.7 0.8 %shard_map.61.v_first = bf16[768,512]{1,0:T(8,128)(2,1)S(1)} custom-call(bf16[256,768]{1,0:T(8,128)(2,1)S(1)} %collective-permute-done.x_far.x, bf16[256,768]{1,0:T(8,128)(2,1)S(1)} %collective-permute-done.2.x_far_twin.x_twin, bf16[2304,768]{1,0:T(8,128)(2,1)S(1)} %get-tuple-element.44.kept), custom_call_target="tpu_custom_call" | custom-call | flops 603979776 | bytes 5111808 | tf_op jit(solution)/shard_map/pallas_call | solution.py:52
  26.5 1.1 %collective-permute-done.6.c = f32[96,128]{1,0:T(8,128)S(1)} collective-permute-done((f32[96,128]{1,0:T(8,128)S(1)}, f32[96,128]{1,0:T(8,128)S(1)}, u32[]{:S(2)}, u32[]{:S(2)}) %collective-permute-start.6) | collective-permute-done | bytes 49184 | tf_op jit(solution)/shard_map/ppermute | solution.py:237
  28.3 2.7 %collective-permute-start.8 = (f32[96,128]{1,0:T(8,128)S(1)}, f32[96,128]{1,0:T(8,128)S(1)}, u32[]{:S(2)}, u32[]{:S(2)}) collective-permute-start(f32[96,128]{1,0:T(8,128)S(1)} %shard_map.62.mine), channel_id=1, source_target_pairs={{0,16},{4,20},{8,24},{12,28},{16,0},{20,4},{24,8},{28,12},{1,17},{... | collective-permute-start | bytes 147464 | tf_op jit(solution)/shard_map/ppermute | solution.py:231
  30.9 2.4 %collective-permute-done.8.other = f32[96,128]{1,0:T(8,128)S(1)} collective-permute-done((f32[96,128]{1,0:T(8,128)S(1)}, f32[96,128]{1,0:T(8,128)S(1)}, u32[]{:S(2)}, u32[]{:S(2)}) %collective-permute-start.8) | collective-permute-done | bytes 49184 | tf_op jit(solution)/shard_map/ppermute | solution.py:231
  33.6 1.6 %collective-permute-start.11 = (bf16[96,128]{1,0:T(8,128)(2,1)S(1)}, bf16[96,128]{1,0:T(8,128)(2,1)S(1)}, u32[]{:S(2)}, u32[]{:S(2)}) collective-permute-start(bf16[96,128]{1,0:T(8,128)(2,1)S(1)} %shard_map.63.p0), channel_id=1, source_target_pairs={{0,12},{4,8},{8,4},{12,0},{16,28},{20,24},{24,20},{28,16},{1,13},{... | collective-permute-start | bytes 73736 | tf_op jit(solution)/shard_map/ppermute | solution.py:231
  35.2 0.9 %collective-permute-start.10 = (bf16[96,128]{1,0:T(8,128)(2,1)S(1)}, bf16[96,128]{1,0:T(8,128)(2,1)S(1)}, u32[]{:S(2)}, u32[]{:S(2)}) collective-permute-start(bf16[96,128]{1,0:T(8,128)(2,1)S(1)} %shard_map.63.p0), channel_id=1, source_target_pairs={{0,8},{4,12},{8,0},{12,4},{16,24},{20,28},{24,16},{28,20},{1,9},{5... | collective-permute-start | bytes 73736 | tf_op jit(solution)/shard_map/ppermute | solution.py:231
  36.1 1.1 %collective-permute-start.9 = (bf16[96,128]{1,0:T(8,128)(2,1)S(1)}, bf16[96,128]{1,0:T(8,128)(2,1)S(1)}, u32[]{:S(2)}, u32[]{:S(2)}) collective-permute-start(bf16[96,128]{1,0:T(8,128)(2,1)S(1)} %shard_map.63.p0), channel_id=1, source_target_pairs={{0,4},{4,0},{8,12},{12,8},{16,20},{20,16},{24,28},{28,24},{1,5},{5... | collective-permute-start | bytes 73736 | tf_op jit(solution)/shard_map/ppermute | solution.py:231
  37.2 0.9 %shard_map.64.v_second = bf16[768,512]{1,0:T(8,128)(2,1)S(1)} custom-call(bf16[256,768]{1,0:T(8,128)(2,1)S(1)} %collective-permute-done.3.x, bf16[256,768]{1,0:T(8,128)(2,1)S(1)} %collective-permute-done.12.x_twin, bf16[2304,768]{1,0:T(8,128)(2,1)S(1)} %get-tuple-element.44.kept), custom_call_target="tpu_custom_call" | custom-call | flops 603979776 | bytes 5111808 | tf_op jit(solution)/shard_map/pallas_call | solution.py:52
  39.0 0.9 %collective-permute-done.9.p1 = bf16[96,128]{1,0:T(8,128)(2,1)S(1)} collective-permute-done((bf16[96,128]{1,0:T(8,128)(2,1)S(1)}, bf16[96,128]{1,0:T(8,128)(2,1)S(1)}, u32[]{:S(2)}, u32[]{:S(2)}) %collective-permute-start.9) | collective-permute-done | bytes 24608 | tf_op jit(solution)/shard_map/ppermute | solution.py:231
  39.9 2.1 %shard_map.65 = bf16[512,768]{1,0:T(8,128)(2,1)} custom-call(bf16[96,128]{1,0:T(8,128)(2,1)S(1)} %shard_map.63.p0, bf16[96,128]{1,0:T(8,128)(2,1)S(1)} %collective-permute-done.9.p1, bf16[96,128]{1,0:T(8,128)(2,1)S(1)} %collective-permute-done.10.p2, bf16[96,128]{1,0:T(8,128)(2,1)S(1)} %collective-permute-done.11.p3, ...), custom_call_target="tpu_custom_call" | custom-call | flops 1207959552 | bytes 5210112 | tf_op jit(solution)/shard_map/pallas_call | solution.py:52
  (19 shorter events, 2.7 us)
Async XLA Ops:
  0.0 1.3 %copy-start.1 = (bf16[16,32,768]{2,1,0:T(8,128)(2,1)S(1)}, bf16[16,32,768]{2,1,0:T(8,128)(2,1)}, u32[]{:S(2)}) copy-start(bf16[16,32,768]{2,1,0:T(8,128)(2,1)} %param.5) | copy-start | bytes 2359300
  1.3 2.9 %collective-permute-start.1 = (bf16[512,768]{1,0:T(8,128)(2,1)S(1)}, bf16[512,768]{1,0:T(8,128)(2,1)S(1)}, u32[]{:S(2)}, u32[]{:S(2)}) collective-permute-start(bf16[512,768]{1,0:T(8,128)(2,1)S(1)} %bitcast.5), channel_id=1, source_target_pairs={{0,1},{1,0},{2,3},{3,2},{4,5},{5,4},{6,7},{7,6},{8,9},{9,8},{10,11... | collective-permute-start | bytes 2359304 | tf_op jit(solution)/shard_map/ppermute | solution.py:231
  1.8 12.3 %collective-permute-start = (bf16[256,768]{1,0:T(8,128)(2,1)S(1)}, bf16[256,768]{1,0:T(8,128)(2,1)S(1)}, u32[]{:S(2)}, u32[]{:S(2)}) collective-permute-start(bf16[256,768]{1,0:T(8,128)(2,1)S(1)} %shard_map.55), channel_id=1, source_target_pairs={{0,2},{1,3},{2,0},{3,1},{4,6},{5,7},{6,4},{7,5},{8,10},{9,11},{10,... | collective-permute-start | bytes 1179656 | tf_op jit(solution)/shard_map/ppermute | solution.py:231
  4.3 0.9 %copy-start.2 = (bf16[512,768]{1,0:T(8,128)(2,1)}, bf16[512,768]{1,0:T(8,128)(2,1)S(1)}, u32[]{:S(2)}) copy-start(bf16[512,768]{1,0:T(8,128)(2,1)S(1)} %collective-permute-done.1.twin) | copy-start | bytes 2359300
  14.0 2.7 %collective-permute-start.2 = (bf16[256,768]{1,0:T(8,128)(2,1)S(1)}, bf16[256,768]{1,0:T(8,128)(2,1)S(1)}, u32[]{:S(2)}, u32[]{:S(2)}) collective-permute-start(bf16[256,768]{1,0:T(8,128)(2,1)S(1)} %collective-permute-done.x_far.x), channel_id=1, source_target_pairs={{0,1},{1,0},{2,3},{3,2},{4,5},{5,4},{6,7},{7,6},{8,9},{9,8},{10,11... | collective-permute-start | bytes 1179656 | tf_op jit(solution)/shard_map/ppermute | solution.py:231
  15.0 5.6 %collective-permute-start.4 = (f32[192,128]{1,0:T(8,128)S(1)}, f32[192,128]{1,0:T(8,128)S(1)}, u32[]{:S(2)}, u32[]{:S(2)}) collective-permute-start(f32[192,128]{1,0:T(8,128)S(1)} %shard_map.58), channel_id=1, source_target_pairs={{0,2},{1,3},{2,0},{3,1},{4,6},{5,7},{6,4},{7,5},{8,10},{9,11},{10,... | collective-permute-start | bytes 294920 | tf_op jit(solution)/shard_map/ppermute | solution.py:231
  16.8 16.7 %collective-permute-start.3 = (bf16[256,768]{1,0:T(8,128)(2,1)S(1)}, bf16[256,768]{1,0:T(8,128)(2,1)S(1)}, u32[]{:S(2)}, u32[]{:S(2)}) collective-permute-start(bf16[256,768]{1,0:T(8,128)(2,1)S(1)} %shard_map.57), channel_id=1, source_target_pairs={{0,2},{1,3},{2,0},{3,1},{4,6},{5,7},{6,4},{7,5},{8,10},{9,11},{10,... | collective-permute-start | bytes 1179656 | tf_op jit(solution)/shard_map/ppermute | solution.py:231
  20.8 4.9 %collective-permute-start.5 = (f32[96,128]{1,0:T(8,128)S(1)}, f32[96,128]{1,0:T(8,128)S(1)}, u32[]{:S(2)}, u32[]{:S(2)}) collective-permute-start(f32[96,128]{1,0:T(8,128)S(1)} %get-tuple-element.41), channel_id=1, source_target_pairs={{0,4},{4,12},{8,0},{12,8},{16,20},{20,28},{24,16},{28,24},{1,5},{5... | collective-permute-start | bytes 147464 | tf_op jit(solution)/shard_map/ppermute | solution.py:237
  22.6 5.0 %collective-permute-start.6 = (f32[96,128]{1,0:T(8,128)S(1)}, f32[96,128]{1,0:T(8,128)S(1)}, u32[]{:S(2)}, u32[]{:S(2)}) collective-permute-start(f32[96,128]{1,0:T(8,128)S(1)} %get-tuple-element.43), channel_id=1, source_target_pairs={{0,12},{4,8},{8,4},{12,0},{16,28},{20,24},{24,20},{28,16},{1,13},{... | collective-permute-start | bytes 147464 | tf_op jit(solution)/shard_map/ppermute | solution.py:237
  24.2 4.1 %collective-permute-start.7 = (f32[96,128]{1,0:T(8,128)S(1)}, f32[96,128]{1,0:T(8,128)S(1)}, u32[]{:S(2)}, u32[]{:S(2)}) collective-permute-start(f32[96,128]{1,0:T(8,128)S(1)} %get-tuple-element.46), channel_id=1, source_target_pairs={{0,8},{4,0},{8,12},{12,4},{16,24},{20,16},{24,28},{28,20},{1,9},{5... | collective-permute-start | bytes 147464 | tf_op jit(solution)/shard_map/ppermute | solution.py:237
  28.3 5.1 %collective-permute-start.8 = (f32[96,128]{1,0:T(8,128)S(1)}, f32[96,128]{1,0:T(8,128)S(1)}, u32[]{:S(2)}, u32[]{:S(2)}) collective-permute-start(f32[96,128]{1,0:T(8,128)S(1)} %shard_map.62.mine), channel_id=1, source_target_pairs={{0,16},{4,20},{8,24},{12,28},{16,0},{20,4},{24,8},{28,12},{1,17},{... | collective-permute-start | bytes 147464 | tf_op jit(solution)/shard_map/ppermute | solution.py:231
  33.5 6.4 %copy-start = (bf16[768,768]{1,0:T(8,128)(2,1)S(1)}, bf16[768,768]{1,0:T(8,128)(2,1)}, u32[]{:S(2)}) copy-start(bf16[768,768]{1,0:T(8,128)(2,1)} %wo.1) | copy-start | bytes 3538948
  33.5 3.6 %collective-permute-start.12 = (bf16[256,768]{1,0:T(8,128)(2,1)S(1)}, bf16[256,768]{1,0:T(8,128)(2,1)S(1)}, u32[]{:S(2)}, u32[]{:S(2)}) collective-permute-start(bf16[256,768]{1,0:T(8,128)(2,1)S(1)} %collective-permute-done.3.x), channel_id=1, source_target_pairs={{0,1},{1,0},{2,3},{3,2},{4,5},{5,4},{6,7},{7,6},{8,9},{9,8},{10,11... | collective-permute-start | bytes 1179656 | tf_op jit(solution)/shard_map/ppermute | solution.py:231
  33.6 4.8 %collective-permute-start.11 = (bf16[96,128]{1,0:T(8,128)(2,1)S(1)}, bf16[96,128]{1,0:T(8,128)(2,1)S(1)}, u32[]{:S(2)}, u32[]{:S(2)}) collective-permute-start(bf16[96,128]{1,0:T(8,128)(2,1)S(1)} %shard_map.63.p0), channel_id=1, source_target_pairs={{0,12},{4,8},{8,4},{12,0},{16,28},{20,24},{24,20},{28,16},{1,13},{... | collective-permute-start | bytes 73736 | tf_op jit(solution)/shard_map/ppermute | solution.py:231
  35.2 3.8 %collective-permute-start.10 = (bf16[96,128]{1,0:T(8,128)(2,1)S(1)}, bf16[96,128]{1,0:T(8,128)(2,1)S(1)}, u32[]{:S(2)}, u32[]{:S(2)}) collective-permute-start(bf16[96,128]{1,0:T(8,128)(2,1)S(1)} %shard_map.63.p0), channel_id=1, source_target_pairs={{0,8},{4,12},{8,0},{12,4},{16,24},{20,28},{24,16},{28,20},{1,9},{5... | collective-permute-start | bytes 73736 | tf_op jit(solution)/shard_map/ppermute | solution.py:231
  36.1 3.8 %collective-permute-start.9 = (bf16[96,128]{1,0:T(8,128)(2,1)S(1)}, bf16[96,128]{1,0:T(8,128)(2,1)S(1)}, u32[]{:S(2)}, u32[]{:S(2)}) collective-permute-start(bf16[96,128]{1,0:T(8,128)(2,1)S(1)} %shard_map.63.p0), channel_id=1, source_target_pairs={{0,4},{4,0},{8,12},{12,8},{16,20},{20,16},{24,28},{28,24},{1,5},{5... | collective-permute-start | bytes 73736 | tf_op jit(solution)/shard_map/ppermute | solution.py:231

commit v7 on v6

--- a/solution.py
+++ b/solution.py
@@ -299,7 +299,7 @@
     )
     wide = ((H * sites, 4 * sites), F32)
     far = call(kernel_mix, [share] * GROUP, (near, ahead, back), 0, [pltpu.VMEM(*wide)])
-    far = [far[0]] + [turn(far[n], n) for n in range(1, GROUP)]
+    far = [far[0]] + [turn(far[n], n) for n in (2, 1, 3)]
     far[1], kept = lax.optimization_barrier((far[1], kept))
     (v_first,) = call(
         functools.partial(kernel_values, sites),

time: 42.2 us -> 41.7 us (0.988)
  waiting for transfers between devices: 9.26 us -> 8.76 us
    ppermute x10, waiting for transfers between devices: 7.55 us -> 7.05 us  [swap(): return lax.ppermute(x, axis, [(i, i ^ bit) for i in range(count)])]
  transfers between devices with their start and end apart: 13 -> 13, of which waited for: 8 -> 9; matrix products, arithmetic and copies ran while one was open for 0% -> 0% of each run, Pallas kernels for 28% -> 28%
where the time goes in v7:
time: 41.7 us; the launch traced here: 41.6 us
  starting transfers between devices  16.6 us (40%)
  Pallas kernels  15 us (36%)
  waiting for transfers between devices  8.76 us (21%)
  local copies, waits for them, and re-layouts  1.06 us (3%)
    pallas_call x11, Pallas kernels, call(): pl.pallas_call(kernel, out_shape=shapes, in_specs=[pl.BlockSpec(memory_sp...  15 us
    ppermute x10, starting transfers between devices, swap(): return lax.ppermute(x, axis, [(i, i ^ bit) for i in range(count)])  11.8 us
    ppermute x10, waiting for transfers between devices, swap(): return lax.ppermute(x, axis, [(i, i ^ bit) for i in range(count)])  7.05 us
    ppermute x3, starting transfers between devices, turn(): return lax.ppermute(x, 'seq', list(enumerate(to)))  4.87 us
    ppermute x3, waiting for transfers between devices, turn(): return lax.ppermute(x, 'seq', list(enumerate(to)))  1.71 us
    unnamed x6, local copies, waits for them, and re-layouts  1.06 us
  transfers between devices with their start and end apart: 13, of which 9 were waited for; matrix products, arithmetic and copies ran while one was open for 0% of the time, Pallas kernels for 28%

profile of v7, /device:TPU:0, one launch (start us, length us, event | category | flops | bytes accessed | tf_op | source)
XLA Modules:
  0.0 41.6 jit_solution(10294545064315545419)
XLA Ops:
  0.0 1.1 %shard_map.55 = bf16[256,768]{1,0:T(8,128)(2,1)S(1)} custom-call(bf16[512,768]{1,0:T(8,128)(2,1)} %bitcast.2), custom_call_target="tpu_custom_call" | custom-call | bytes 1179648 | tf_op jit(solution)/shard_map/pallas_call | solution.py:52
  1.8 2.5 %collective-permute-start = (bf16[256,768]{1,0:T(8,128)(2,1)S(1)}, bf16[256,768]{1,0:T(8,128)(2,1)S(1)}, u32[]{:S(2)}, u32[]{:S(2)}) collective-permute-start(bf16[256,768]{1,0:T(8,128)(2,1)S(1)} %shard_map.55), channel_id=1, source_target_pairs={{0,2},{1,3},{2,0},{3,1},{4,6},{5,7},{6,4},{7,5},{8,10},{9,11},{10,... | collective-permute-start | bytes 1179656 | tf_op jit(solution)/shard_map/ppermute | solution.py:231
  4.3 0.9 %copy-done.2 = bf16[512,768]{1,0:T(8,128)(2,1)} copy-done((bf16[512,768]{1,0:T(8,128)(2,1)}, bf16[512,768]{1,0:T(8,128)(2,1)S(1)}, u32[]{:S(2)}) %copy-start.2) | copy-done | bytes 786456
  5.1 6.5 %shard_map.56 = (bf16[2304,768]{1,0:T(8,128)(2,1)S(1)}, bf16[384,1024]{1,0:T(8,128)(2,1)S(1)}, bf16[768,1024]{1,0:T(8,128)(2,1)S(1)}, bf16[768,1024]{1,0:T(8,128)(2,1)S(1)}, f32[384,64]{1,0:T(8,128)S(1)}) custom-call(bf16[512,768]{1,0:T(8,128)(2,1)} %bitcast.3, bf16[512,768]{1,0:T(8,128)(2,1)} %copy-done.2, bf16[768,768]{1,0:T(8,128)(2,1)} %wq.1, ...), custom_call_target="tpu_custom_call" | custom-call | flops 3623878656 | bytes 12681216 | tf_op jit(solution)/shard_map/pallas_call | solution.py:52
  11.7 1.1 %shard_map.57 = bf16[256,768]{1,0:T(8,128)(2,1)S(1)} custom-call(bf16[512,768]{1,0:T(8,128)(2,1)} %bitcast.4), custom_call_target="tpu_custom_call" | custom-call | bytes 1179648 | tf_op jit(solution)/shard_map/pallas_call | solution.py:52
  12.8 1.3 %collective-permute-done.x_far.x = bf16[256,768]{1,0:T(8,128)(2,1)S(1)} collective-permute-done((bf16[256,768]{1,0:T(8,128)(2,1)S(1)}, bf16[256,768]{1,0:T(8,128)(2,1)S(1)}, u32[]{:S(2)}, u32[]{:S(2)}) %collective-permute-start) | collective-permute-done | bytes 393248 | tf_op jit(solution)/shard_map/ppermute | solution.py:231
  14.1 0.9 %shard_map.58 = f32[192,128]{1,0:T(8,128)S(1)} custom-call(bf16[256,768]{1,0:T(8,128)(2,1)S(1)} %collective-permute-done.x_far.x, bf16[2304,768]{1,0:T(8,128)(2,1)S(1)} %get-tuple-element.44.kept, bf16[768,1024]{1,0:T(8,128)(2,1)S(1)} %get-tuple-element.34.k), custom_call_target="tpu_custom_call" | custom-call | flops 603979776 | bytes 5603328 | tf_op jit(solution)/shard_map/pallas_call | solution.py:52
  15.0 1.8 %collective-permute-start.4 = (f32[192,128]{1,0:T(8,128)S(1)}, f32[192,128]{1,0:T(8,128)S(1)}, u32[]{:S(2)}, u32[]{:S(2)}) collective-permute-start(f32[192,128]{1,0:T(8,128)S(1)} %shard_map.58), channel_id=1, source_target_pairs={{0,2},{1,3},{2,0},{3,1},{4,6},{5,7},{6,4},{7,5},{8,10},{9,11},{10,... | collective-permute-start | bytes 294920 | tf_op jit(solution)/shard_map/ppermute | solution.py:231
  16.8 0.7 %collective-permute-start.3 = (bf16[256,768]{1,0:T(8,128)(2,1)S(1)}, bf16[256,768]{1,0:T(8,128)(2,1)S(1)}, u32[]{:S(2)}, u32[]{:S(2)}) collective-permute-start(bf16[256,768]{1,0:T(8,128)(2,1)S(1)} %shard_map.57), channel_id=1, source_target_pairs={{0,2},{1,3},{2,0},{3,1},{4,6},{5,7},{6,4},{7,5},{8,10},{9,11},{10,... | collective-permute-start | bytes 1179656 | tf_op jit(solution)/shard_map/ppermute | solution.py:231
  17.5 1.1 %shard_map.59.ahead = f32[384,64]{1,0:T(8,128)S(1)} custom-call(bf16[256,768]{1,0:T(8,128)(2,1)S(1)} %collective-permute-done.x_far.x, bf16[256,768]{1,0:T(8,128)(2,1)S(1)} %collective-permute-done.2.x_far_twin.x_twin, bf16[2304,768]{1,0:T(8,128)(2,1)S(1)} %get-tuple-element.44.kept, bf16[384,1024]{1,0:T(8,128)(2,1)S(1)} %get-tuple-element.39.q), custom_call_target="tpu_custom_call" | custom-call | flops 603979776 | bytes 5210112 | tf_op jit(solution)/shard_map/pallas_call | solution.py:52
  18.6 2.0 %collective-permute-done.4.back = f32[192,128]{1,0:T(8,128)S(1)} collective-permute-done((f32[192,128]{1,0:T(8,128)S(1)}, f32[192,128]{1,0:T(8,128)S(1)}, u32[]{:S(2)}, u32[]{:S(2)}) %collective-permute-start.4) | collective-permute-done | bytes 98336 | tf_op jit(solution)/shard_map/ppermute | solution.py:231
  20.8 2.8 %collective-permute-start.5 = (f32[96,128]{1,0:T(8,128)S(1)}, f32[96,128]{1,0:T(8,128)S(1)}, u32[]{:S(2)}, u32[]{:S(2)}) collective-permute-start(f32[96,128]{1,0:T(8,128)S(1)} %get-tuple-element.41), channel_id=1, source_target_pairs={{0,12},{4,8},{8,4},{12,0},{16,28},{20,24},{24,20},{28,16},{1,13},{... | collective-permute-start | bytes 147464 | tf_op jit(solution)/shard_map/ppermute | solution.py:237
  24.2 1.5 %collective-permute-start.7 = (f32[96,128]{1,0:T(8,128)S(1)}, f32[96,128]{1,0:T(8,128)S(1)}, u32[]{:S(2)}, u32[]{:S(2)}) collective-permute-start(f32[96,128]{1,0:T(8,128)S(1)} %get-tuple-element.46), channel_id=1, source_target_pairs={{0,8},{4,0},{8,12},{12,4},{16,24},{20,16},{24,28},{28,20},{1,9},{5... | collective-permute-start | bytes 147464 | tf_op jit(solution)/shard_map/ppermute | solution.py:237
  25.7 0.7 %collective-permute-done.5.b = f32[96,128]{1,0:T(8,128)S(1)} collective-permute-done((f32[96,128]{1,0:T(8,128)S(1)}, f32[96,128]{1,0:T(8,128)S(1)}, u32[]{:S(2)}, u32[]{:S(2)}) %collective-permute-start.5) | collective-permute-done | bytes 49184 | tf_op jit(solution)/shard_map/ppermute | solution.py:237
  26.4 0.8 %shard_map.61.v_first = bf16[768,512]{1,0:T(8,128)(2,1)S(1)} custom-call(bf16[256,768]{1,0:T(8,128)(2,1)S(1)} %collective-permute-done.x_far.x, bf16[256,768]{1,0:T(8,128)(2,1)S(1)} %collective-permute-done.2.x_far_twin.x_twin, bf16[2304,768]{1,0:T(8,128)(2,1)S(1)} %get-tuple-element.44.kept), custom_call_target="tpu_custom_call" | custom-call | flops 603979776 | bytes 5111808 | tf_op jit(solution)/shard_map/pallas_call | solution.py:52
  27.2 0.5 %collective-permute-done.6.c = f32[96,128]{1,0:T(8,128)S(1)} collective-permute-done((f32[96,128]{1,0:T(8,128)S(1)}, f32[96,128]{1,0:T(8,128)S(1)}, u32[]{:S(2)}, u32[]{:S(2)}) %collective-permute-start.6) | collective-permute-done | bytes 49184 | tf_op jit(solution)/shard_map/ppermute | solution.py:237
  27.8 0.5 %collective-permute-done.7.d = f32[96,128]{1,0:T(8,128)S(1)} collective-permute-done((f32[96,128]{1,0:T(8,128)S(1)}, f32[96,128]{1,0:T(8,128)S(1)}, u32[]{:S(2)}, u32[]{:S(2)}) %collective-permute-start.7) | collective-permute-done | bytes 49184 | tf_op jit(solution)/shard_map/ppermute | solution.py:237
  28.3 2.7 %collective-permute-start.8 = (f32[96,128]{1,0:T(8,128)S(1)}, f32[96,128]{1,0:T(8,128)S(1)}, u32[]{:S(2)}, u32[]{:S(2)}) collective-permute-start(f32[96,128]{1,0:T(8,128)S(1)} %shard_map.62.mine), channel_id=1, source_target_pairs={{0,16},{4,20},{8,24},{12,28},{16,0},{20,4},{24,8},{28,12},{1,17},{... | collective-permute-start | bytes 147464 | tf_op jit(solution)/shard_map/ppermute | solution.py:231
  30.9 2.4 %collective-permute-done.8.other = f32[96,128]{1,0:T(8,128)S(1)} collective-permute-done((f32[96,128]{1,0:T(8,128)S(1)}, f32[96,128]{1,0:T(8,128)S(1)}, u32[]{:S(2)}, u32[]{:S(2)}) %collective-permute-start.8) | collective-permute-done | bytes 49184 | tf_op jit(solution)/shard_map/ppermute | solution.py:231
  33.6 1.7 %collective-permute-start.11 = (bf16[96,128]{1,0:T(8,128)(2,1)S(1)}, bf16[96,128]{1,0:T(8,128)(2,1)S(1)}, u32[]{:S(2)}, u32[]{:S(2)}) collective-permute-start(bf16[96,128]{1,0:T(8,128)(2,1)S(1)} %shard_map.63.p0), channel_id=1, source_target_pairs={{0,12},{4,8},{8,4},{12,0},{16,28},{20,24},{24,20},{28,16},{1,13},{... | collective-permute-start | bytes 73736 | tf_op jit(solution)/shard_map/ppermute | solution.py:231
  35.6 1.6 %collective-permute-start.9 = (bf16[96,128]{1,0:T(8,128)(2,1)S(1)}, bf16[96,128]{1,0:T(8,128)(2,1)S(1)}, u32[]{:S(2)}, u32[]{:S(2)}) collective-permute-start(bf16[96,128]{1,0:T(8,128)(2,1)S(1)} %shard_map.63.p0), channel_id=1, source_target_pairs={{0,4},{4,0},{8,12},{12,8},{16,20},{20,16},{24,28},{28,24},{1,5},{5... | collective-permute-start | bytes 73736 | tf_op jit(solution)/shard_map/ppermute | solution.py:231
  37.2 0.9 %shard_map.64.v_second = bf16[768,512]{1,0:T(8,128)(2,1)S(1)} custom-call(bf16[256,768]{1,0:T(8,128)(2,1)S(1)} %collective-permute-done.3.x, bf16[256,768]{1,0:T(8,128)(2,1)S(1)} %collective-permute-done.12.x_twin, bf16[2304,768]{1,0:T(8,128)(2,1)S(1)} %get-tuple-element.44.kept), custom_call_target="tpu_custom_call" | custom-call | flops 603979776 | bytes 5111808 | tf_op jit(solution)/shard_map/pallas_call | solution.py:52
  38.5 0.6 %collective-permute-done.10.p2 = bf16[96,128]{1,0:T(8,128)(2,1)S(1)} collective-permute-done((bf16[96,128]{1,0:T(8,128)(2,1)S(1)}, bf16[96,128]{1,0:T(8,128)(2,1)S(1)}, u32[]{:S(2)}, u32[]{:S(2)}) %collective-permute-start.10) | collective-permute-done | bytes 24608 | tf_op jit(solution)/shard_map/ppermute | solution.py:231
  39.4 2.1 %shard_map.65 = bf16[512,768]{1,0:T(8,128)(2,1)} custom-call(bf16[96,128]{1,0:T(8,128)(2,1)S(1)} %shard_map.63.p0, bf16[96,128]{1,0:T(8,128)(2,1)S(1)} %collective-permute-done.9.p1, bf16[96,128]{1,0:T(8,128)(2,1)S(1)} %collective-permute-done.10.p2, bf16[96,128]{1,0:T(8,128)(2,1)S(1)} %collective-permute-done.11.p3, ...), custom_call_target="tpu_custom_call" | custom-call | flops 1207959552 | bytes 5210112 | tf_op jit(solution)/shard_map/pallas_call | solution.py:52
  (19 shorter events, 2.6 us)
Async XLA Ops:
  0.0 1.3 %copy-start.1 = (bf16[16,32,768]{2,1,0:T(8,128)(2,1)S(1)}, bf16[16,32,768]{2,1,0:T(8,128)(2,1)}, u32[]{:S(2)}) copy-start(bf16[16,32,768]{2,1,0:T(8,128)(2,1)} %param.5) | copy-start | bytes 2359300
  1.3 2.9 %collective-permute-start.1 = (bf16[512,768]{1,0:T(8,128)(2,1)S(1)}, bf16[512,768]{1,0:T(8,128)(2,1)S(1)}, u32[]{:S(2)}, u32[]{:S(2)}) collective-permute-start(bf16[512,768]{1,0:T(8,128)(2,1)S(1)} %bitcast.5), channel_id=1, source_target_pairs={{0,1},{1,0},{2,3},{3,2},{4,5},{5,4},{6,7},{7,6},{8,9},{9,8},{10,11... | collective-permute-start | bytes 2359304 | tf_op jit(solution)/shard_map/ppermute | solution.py:231
  1.8 12.3 %collective-permute-start = (bf16[256,768]{1,0:T(8,128)(2,1)S(1)}, bf16[256,768]{1,0:T(8,128)(2,1)S(1)}, u32[]{:S(2)}, u32[]{:S(2)}) collective-permute-start(bf16[256,768]{1,0:T(8,128)(2,1)S(1)} %shard_map.55), channel_id=1, source_target_pairs={{0,2},{1,3},{2,0},{3,1},{4,6},{5,7},{6,4},{7,5},{8,10},{9,11},{10,... | collective-permute-start | bytes 1179656 | tf_op jit(solution)/shard_map/ppermute | solution.py:231
  4.3 0.9 %copy-start.2 = (bf16[512,768]{1,0:T(8,128)(2,1)}, bf16[512,768]{1,0:T(8,128)(2,1)S(1)}, u32[]{:S(2)}) copy-start(bf16[512,768]{1,0:T(8,128)(2,1)S(1)} %collective-permute-done.1.twin) | copy-start | bytes 2359300
  14.0 2.7 %collective-permute-start.2 = (bf16[256,768]{1,0:T(8,128)(2,1)S(1)}, bf16[256,768]{1,0:T(8,128)(2,1)S(1)}, u32[]{:S(2)}, u32[]{:S(2)}) collective-permute-start(bf16[256,768]{1,0:T(8,128)(2,1)S(1)} %collective-permute-done.x_far.x), channel_id=1, source_target_pairs={{0,1},{1,0},{2,3},{3,2},{4,5},{5,4},{6,7},{7,6},{8,9},{9,8},{10,11... | collective-permute-start | bytes 1179656 | tf_op jit(solution)/shard_map/ppermute | solution.py:231
  15.0 5.6 %collective-permute-start.4 = (f32[192,128]{1,0:T(8,128)S(1)}, f32[192,128]{1,0:T(8,128)S(1)}, u32[]{:S(2)}, u32[]{:S(2)}) collective-permute-start(f32[192,128]{1,0:T(8,128)S(1)} %shard_map.58), channel_id=1, source_target_pairs={{0,2},{1,3},{2,0},{3,1},{4,6},{5,7},{6,4},{7,5},{8,10},{9,11},{10,... | collective-permute-start | bytes 294920 | tf_op jit(solution)/shard_map/ppermute | solution.py:231
  16.8 16.8 %collective-permute-start.3 = (bf16[256,768]{1,0:T(8,128)(2,1)S(1)}, bf16[256,768]{1,0:T(8,128)(2,1)S(1)}, u32[]{:S(2)}, u32[]{:S(2)}) collective-permute-start(bf16[256,768]{1,0:T(8,128)(2,1)S(1)} %shard_map.57), channel_id=1, source_target_pairs={{0,2},{1,3},{2,0},{3,1},{4,6},{5,7},{6,4},{7,5},{8,10},{9,11},{10,... | collective-permute-start | bytes 1179656 | tf_op jit(solution)/shard_map/ppermute | solution.py:231
  20.8 5.5 %collective-permute-start.5 = (f32[96,128]{1,0:T(8,128)S(1)}, f32[96,128]{1,0:T(8,128)S(1)}, u32[]{:S(2)}, u32[]{:S(2)}) collective-permute-start(f32[96,128]{1,0:T(8,128)S(1)} %get-tuple-element.41), channel_id=1, source_target_pairs={{0,12},{4,8},{8,4},{12,0},{16,28},{20,24},{24,20},{28,16},{1,13},{... | collective-permute-start | bytes 147464 | tf_op jit(solution)/shard_map/ppermute | solution.py:237
  23.7 4.1 %collective-permute-start.6 = (f32[96,128]{1,0:T(8,128)S(1)}, f32[96,128]{1,0:T(8,128)S(1)}, u32[]{:S(2)}, u32[]{:S(2)}) collective-permute-start(f32[96,128]{1,0:T(8,128)S(1)} %get-tuple-element.43), channel_id=1, source_target_pairs={{0,4},{4,12},{8,0},{12,8},{16,20},{20,28},{24,16},{28,24},{1,5},{5... | collective-permute-start | bytes 147464 | tf_op jit(solution)/shard_map/ppermute | solution.py:237
  24.2 4.1 %collective-permute-start.7 = (f32[96,128]{1,0:T(8,128)S(1)}, f32[96,128]{1,0:T(8,128)S(1)}, u32[]{:S(2)}, u32[]{:S(2)}) collective-permute-start(f32[96,128]{1,0:T(8,128)S(1)} %get-tuple-element.46), channel_id=1, source_target_pairs={{0,8},{4,0},{8,12},{12,4},{16,24},{20,16},{24,28},{28,20},{1,9},{5... | collective-permute-start | bytes 147464 | tf_op jit(solution)/shard_map/ppermute | solution.py:237
  28.3 5.1 %collective-permute-start.8 = (f32[96,128]{1,0:T(8,128)S(1)}, f32[96,128]{1,0:T(8,128)S(1)}, u32[]{:S(2)}, u32[]{:S(2)}) collective-permute-start(f32[96,128]{1,0:T(8,128)S(1)} %shard_map.62.mine), channel_id=1, source_target_pairs={{0,16},{4,20},{8,24},{12,28},{16,0},{20,4},{24,8},{28,12},{1,17},{... | collective-permute-start | bytes 147464 | tf_op jit(solution)/shard_map/ppermute | solution.py:231
  33.5 5.9 %copy-start = (bf16[768,768]{1,0:T(8,128)(2,1)S(1)}, bf16[768,768]{1,0:T(8,128)(2,1)}, u32[]{:S(2)}) copy-start(bf16[768,768]{1,0:T(8,128)(2,1)} %wo.1) | copy-start | bytes 3538948
  33.5 3.6 %collective-permute-start.12 = (bf16[256,768]{1,0:T(8,128)(2,1)S(1)}, bf16[256,768]{1,0:T(8,128)(2,1)S(1)}, u32[]{:S(2)}, u32[]{:S(2)}) collective-permute-start(bf16[256,768]{1,0:T(8,128)(2,1)S(1)} %collective-permute-done.3.x), channel_id=1, source_target_pairs={{0,1},{1,0},{2,3},{3,2},{4,5},{5,4},{6,7},{7,6},{8,9},{9,8},{10,11... | collective-permute-start | bytes 1179656 | tf_op jit(solution)/shard_map/ppermute | solution.py:231
  33.6 4.9 %collective-permute-start.11 = (bf16[96,128]{1,0:T(8,128)(2,1)S(1)}, bf16[96,128]{1,0:T(8,128)(2,1)S(1)}, u32[]{:S(2)}, u32[]{:S(2)}) collective-permute-start(bf16[96,128]{1,0:T(8,128)(2,1)S(1)} %shard_map.63.p0), channel_id=1, source_target_pairs={{0,12},{4,8},{8,4},{12,0},{16,28},{20,24},{24,20},{28,16},{1,13},{... | collective-permute-start | bytes 73736 | tf_op jit(solution)/shard_map/ppermute | solution.py:231
  35.3 3.8 %collective-permute-start.10 = (bf16[96,128]{1,0:T(8,128)(2,1)S(1)}, bf16[96,128]{1,0:T(8,128)(2,1)S(1)}, u32[]{:S(2)}, u32[]{:S(2)}) collective-permute-start(bf16[96,128]{1,0:T(8,128)(2,1)S(1)} %shard_map.63.p0), channel_id=1, source_target_pairs={{0,8},{4,12},{8,0},{12,4},{16,24},{20,28},{24,16},{28,20},{1,9},{5... | collective-permute-start | bytes 73736 | tf_op jit(solution)/shard_map/ppermute | solution.py:231
  35.6 3.8 %collective-permute-start.9 = (bf16[96,128]{1,0:T(8,128)(2,1)S(1)}, bf16[96,128]{1,0:T(8,128)(2,1)S(1)}, u32[]{:S(2)}, u32[]{:S(2)}) collective-permute-start(bf16[96,128]{1,0:T(8,128)(2,1)S(1)} %shard_map.63.p0), channel_id=1, source_target_pairs={{0,4},{4,0},{8,12},{12,8},{16,20},{20,16},{24,28},{28,24},{1,5},{5... | collective-permute-start | bytes 73736 | tf_op jit(solution)/shard_map/ppermute | solution.py:231

commit v8 on v7

--- a/solution.py
+++ b/solution.py
@@ -251,7 +251,7 @@
             functools.partial(kernel_part, half * sites, other),
             [(half_flat, BF16)],
             (x,),
-            scratch=[pltpu.SemaphoreType.DMA((GROUP,))],
+            scratch=[pltpu.SemaphoreType.DMA((1,))],
             space=pltpu.HBM,
         )[0]
 

time: 41.7 us -> 41.7 us (level)
  no operation moved by 1% of the time
where the time goes in v8:
time: 41.7 us; the launch traced here: 41.5 us
  starting transfers between devices  16.6 us (40%)
  Pallas kernels  14.9 us (36%)
  waiting for transfers between devices  8.83 us (21%)
  local copies, waits for them, and re-layouts  1.05 us (3%)
    pallas_call x11, Pallas kernels, call(): pl.pallas_call(kernel, out_shape=shapes, in_specs=[pl.BlockSpec(memory_sp...  14.9 us
    ppermute x10, starting transfers between devices, swap(): return lax.ppermute(x, axis, [(i, i ^ bit) for i in range(count)])  11.8 us
    ppermute x10, waiting for transfers between devices, swap(): return lax.ppermute(x, axis, [(i, i ^ bit) for i in range(count)])  7.11 us
    ppermute x3, starting transfers between devices, turn(): return lax.ppermute(x, 'seq', list(enumerate(to)))  4.88 us
    ppermute x3, waiting for transfers between devices, turn(): return lax.ppermute(x, 'seq', list(enumerate(to)))  1.71 us
    unnamed x6, local copies, waits for them, and re-layouts  1.05 us
  transfers between devices with their start and end apart: 13, of which 9 were waited for; matrix products, arithmetic and copies ran while one was open for 0% of the time, Pallas kernels for 28%

profile of v8, /device:TPU:0, one launch (start us, length us, event | category | flops | bytes accessed | tf_op | source)
XLA Modules:
  0.0 41.5 jit_solution(8197524425797764789)
XLA Ops:
  0.0 1.1 %shard_map.55 = bf16[256,768]{1,0:T(8,128)(2,1)S(1)} custom-call(bf16[512,768]{1,0:T(8,128)(2,1)} %bitcast.2), custom_call_target="tpu_custom_call" | custom-call | bytes 1179648 | tf_op jit(solution)/shard_map/pallas_call | solution.py:52
  1.7 2.5 %collective-permute-start = (bf16[256,768]{1,0:T(8,128)(2,1)S(1)}, bf16[256,768]{1,0:T(8,128)(2,1)S(1)}, u32[]{:S(2)}, u32[]{:S(2)}) collective-permute-start(bf16[256,768]{1,0:T(8,128)(2,1)S(1)} %shard_map.55), channel_id=1, source_target_pairs={{0,2},{1,3},{2,0},{3,1},{4,6},{5,7},{6,4},{7,5},{8,10},{9,11},{10,... | collective-permute-start | bytes 1179656 | tf_op jit(solution)/shard_map/ppermute | solution.py:231
  4.2 0.9 %copy-done.2 = bf16[512,768]{1,0:T(8,128)(2,1)} copy-done((bf16[512,768]{1,0:T(8,128)(2,1)}, bf16[512,768]{1,0:T(8,128)(2,1)S(1)}, u32[]{:S(2)}) %copy-start.2) | copy-done | bytes 786456
  5.1 6.5 %shard_map.56 = (bf16[2304,768]{1,0:T(8,128)(2,1)S(1)}, bf16[384,1024]{1,0:T(8,128)(2,1)S(1)}, bf16[768,1024]{1,0:T(8,128)(2,1)S(1)}, bf16[768,1024]{1,0:T(8,128)(2,1)S(1)}, f32[384,64]{1,0:T(8,128)S(1)}) custom-call(bf16[512,768]{1,0:T(8,128)(2,1)} %bitcast.3, bf16[512,768]{1,0:T(8,128)(2,1)} %copy-done.2, bf16[768,768]{1,0:T(8,128)(2,1)} %wq.1, ...), custom_call_target="tpu_custom_call" | custom-call | flops 3623878656 | bytes 12681216 | tf_op jit(solution)/shard_map/pallas_call | solution.py:52
  11.6 1.0 %shard_map.57 = bf16[256,768]{1,0:T(8,128)(2,1)S(1)} custom-call(bf16[512,768]{1,0:T(8,128)(2,1)} %bitcast.4), custom_call_target="tpu_custom_call" | custom-call | bytes 1179648 | tf_op jit(solution)/shard_map/pallas_call | solution.py:52
  12.6 1.3 %collective-permute-done.x_far.x = bf16[256,768]{1,0:T(8,128)(2,1)S(1)} collective-permute-done((bf16[256,768]{1,0:T(8,128)(2,1)S(1)}, bf16[256,768]{1,0:T(8,128)(2,1)S(1)}, u32[]{:S(2)}, u32[]{:S(2)}) %collective-permute-start) | collective-permute-done | bytes 393248 | tf_op jit(solution)/shard_map/ppermute | solution.py:231
  14.0 0.9 %shard_map.58 = f32[192,128]{1,0:T(8,128)S(1)} custom-call(bf16[256,768]{1,0:T(8,128)(2,1)S(1)} %collective-permute-done.x_far.x, bf16[2304,768]{1,0:T(8,128)(2,1)S(1)} %get-tuple-element.44.kept, bf16[768,1024]{1,0:T(8,128)(2,1)S(1)} %get-tuple-element.34.k), custom_call_target="tpu_custom_call" | custom-call | flops 603979776 | bytes 5603328 | tf_op jit(solution)/shard_map/pallas_call | solution.py:52
  14.9 1.8 %collective-permute-start.4 = (f32[192,128]{1,0:T(8,128)S(1)}, f32[192,128]{1,0:T(8,128)S(1)}, u32[]{:S(2)}, u32[]{:S(2)}) collective-permute-start(f32[192,128]{1,0:T(8,128)S(1)} %shard_map.58), channel_id=1, source_target_pairs={{0,2},{1,3},{2,0},{3,1},{4,6},{5,7},{6,4},{7,5},{8,10},{9,11},{10,... | collective-permute-start | bytes 294920 | tf_op jit(solution)/shard_map/ppermute | solution.py:231
  16.7 0.7 %collective-permute-start.3 = (bf16[256,768]{1,0:T(8,128)(2,1)S(1)}, bf16[256,768]{1,0:T(8,128)(2,1)S(1)}, u32[]{:S(2)}, u32[]{:S(2)}) collective-permute-start(bf16[256,768]{1,0:T(8,128)(2,1)S(1)} %shard_map.57), channel_id=1, source_target_pairs={{0,2},{1,3},{2,0},{3,1},{4,6},{5,7},{6,4},{7,5},{8,10},{9,11},{10,... | collective-permute-start | bytes 1179656 | tf_op jit(solution)/shard_map/ppermute | solution.py:231
  17.4 1.1 %shard_map.59.ahead = f32[384,64]{1,0:T(8,128)S(1)} custom-call(bf16[256,768]{1,0:T(8,128)(2,1)S(1)} %collective-permute-done.x_far.x, bf16[256,768]{1,0:T(8,128)(2,1)S(1)} %collective-permute-done.2.x_far_twin.x_twin, bf16[2304,768]{1,0:T(8,128)(2,1)S(1)} %get-tuple-element.44.kept, bf16[384,1024]{1,0:T(8,128)(2,1)S(1)} %get-tuple-element.39.q), custom_call_target="tpu_custom_call" | custom-call | flops 603979776 | bytes 5210112 | tf_op jit(solution)/shard_map/pallas_call | solution.py:52
  18.6 2.0 %collective-permute-done.4.back = f32[192,128]{1,0:T(8,128)S(1)} collective-permute-done((f32[192,128]{1,0:T(8,128)S(1)}, f32[192,128]{1,0:T(8,128)S(1)}, u32[]{:S(2)}, u32[]{:S(2)}) %collective-permute-start.4) | collective-permute-done | bytes 98336 | tf_op jit(solution)/shard_map/ppermute | solution.py:231
  20.7 2.8 %collective-permute-start.5 = (f32[96,128]{1,0:T(8,128)S(1)}, f32[96,128]{1,0:T(8,128)S(1)}, u32[]{:S(2)}, u32[]{:S(2)}) collective-permute-start(f32[96,128]{1,0:T(8,128)S(1)} %get-tuple-element.41), channel_id=1, source_target_pairs={{0,12},{4,8},{8,4},{12,0},{16,28},{20,24},{24,20},{28,16},{1,13},{... | collective-permute-start | bytes 147464 | tf_op jit(solution)/shard_map/ppermute | solution.py:237
  23.6 0.5 %collective-permute-start.6 = (f32[96,128]{1,0:T(8,128)S(1)}, f32[96,128]{1,0:T(8,128)S(1)}, u32[]{:S(2)}, u32[]{:S(2)}) collective-permute-start(f32[96,128]{1,0:T(8,128)S(1)} %get-tuple-element.43), channel_id=1, source_target_pairs={{0,4},{4,12},{8,0},{12,8},{16,20},{20,28},{24,16},{28,24},{1,5},{5... | collective-permute-start | bytes 147464 | tf_op jit(solution)/shard_map/ppermute | solution.py:237
  24.1 1.5 %collective-permute-start.7 = (f32[96,128]{1,0:T(8,128)S(1)}, f32[96,128]{1,0:T(8,128)S(1)}, u32[]{:S(2)}, u32[]{:S(2)}) collective-permute-start(f32[96,128]{1,0:T(8,128)S(1)} %get-tuple-element.46), channel_id=1, source_target_pairs={{0,8},{4,0},{8,12},{12,4},{16,24},{20,16},{24,28},{28,20},{1,9},{5... | collective-permute-start | bytes 147464 | tf_op jit(solution)/shard_map/ppermute | solution.py:237
  25.6 0.7 %collective-permute-done.5.b = f32[96,128]{1,0:T(8,128)S(1)} collective-permute-done((f32[96,128]{1,0:T(8,128)S(1)}, f32[96,128]{1,0:T(8,128)S(1)}, u32[]{:S(2)}, u32[]{:S(2)}) %collective-permute-start.5) | collective-permute-done | bytes 49184 | tf_op jit(solution)/shard_map/ppermute | solution.py:237
  26.3 0.8 %shard_map.61.v_first = bf16[768,512]{1,0:T(8,128)(2,1)S(1)} custom-call(bf16[256,768]{1,0:T(8,128)(2,1)S(1)} %collective-permute-done.x_far.x, bf16[256,768]{1,0:T(8,128)(2,1)S(1)} %collective-permute-done.2.x_far_twin.x_twin, bf16[2304,768]{1,0:T(8,128)(2,1)S(1)} %get-tuple-element.44.kept), custom_call_target="tpu_custom_call" | custom-call | flops 603979776 | bytes 5111808 | tf_op jit(solution)/shard_map/pallas_call | solution.py:52
  27.1 0.5 %collective-permute-done.6.c = f32[96,128]{1,0:T(8,128)S(1)} collective-permute-done((f32[96,128]{1,0:T(8,128)S(1)}, f32[96,128]{1,0:T(8,128)S(1)}, u32[]{:S(2)}, u32[]{:S(2)}) %collective-permute-start.6) | collective-permute-done | bytes 49184 | tf_op jit(solution)/shard_map/ppermute | solution.py:237
  28.2 2.7 %collective-permute-start.8 = (f32[96,128]{1,0:T(8,128)S(1)}, f32[96,128]{1,0:T(8,128)S(1)}, u32[]{:S(2)}, u32[]{:S(2)}) collective-permute-start(f32[96,128]{1,0:T(8,128)S(1)} %shard_map.62.mine), channel_id=1, source_target_pairs={{0,16},{4,20},{8,24},{12,28},{16,0},{20,4},{24,8},{28,12},{1,17},{... | collective-permute-start | bytes 147464 | tf_op jit(solution)/shard_map/ppermute | solution.py:231
  30.9 2.4 %collective-permute-done.8.other = f32[96,128]{1,0:T(8,128)S(1)} collective-permute-done((f32[96,128]{1,0:T(8,128)S(1)}, f32[96,128]{1,0:T(8,128)S(1)}, u32[]{:S(2)}, u32[]{:S(2)}) %collective-permute-start.8) | collective-permute-done | bytes 49184 | tf_op jit(solution)/shard_map/ppermute | solution.py:231
  33.5 1.7 %collective-permute-start.11 = (bf16[96,128]{1,0:T(8,128)(2,1)S(1)}, bf16[96,128]{1,0:T(8,128)(2,1)S(1)}, u32[]{:S(2)}, u32[]{:S(2)}) collective-permute-start(bf16[96,128]{1,0:T(8,128)(2,1)S(1)} %shard_map.63.p0), channel_id=1, source_target_pairs={{0,12},{4,8},{8,4},{12,0},{16,28},{20,24},{24,20},{28,16},{1,13},{... | collective-permute-start | bytes 73736 | tf_op jit(solution)/shard_map/ppermute | solution.py:231
  35.5 1.6 %collective-permute-start.9 = (bf16[96,128]{1,0:T(8,128)(2,1)S(1)}, bf16[96,128]{1,0:T(8,128)(2,1)S(1)}, u32[]{:S(2)}, u32[]{:S(2)}) collective-permute-start(bf16[96,128]{1,0:T(8,128)(2,1)S(1)} %shard_map.63.p0), channel_id=1, source_target_pairs={{0,4},{4,0},{8,12},{12,8},{16,20},{20,16},{24,28},{28,24},{1,5},{5... | collective-permute-start | bytes 73736 | tf_op jit(solution)/shard_map/ppermute | solution.py:231
  37.1 0.9 %shard_map.64.v_second = bf16[768,512]{1,0:T(8,128)(2,1)S(1)} custom-call(bf16[256,768]{1,0:T(8,128)(2,1)S(1)} %collective-permute-done.3.x, bf16[256,768]{1,0:T(8,128)(2,1)S(1)} %collective-permute-done.12.x_twin, bf16[2304,768]{1,0:T(8,128)(2,1)S(1)} %get-tuple-element.44.kept), custom_call_target="tpu_custom_call" | custom-call | flops 603979776 | bytes 5111808 | tf_op jit(solution)/shard_map/pallas_call | solution.py:52
  38.4 0.6 %collective-permute-done.10.p2 = bf16[96,128]{1,0:T(8,128)(2,1)S(1)} collective-permute-done((bf16[96,128]{1,0:T(8,128)(2,1)S(1)}, bf16[96,128]{1,0:T(8,128)(2,1)S(1)}, u32[]{:S(2)}, u32[]{:S(2)}) %collective-permute-start.10) | collective-permute-done | bytes 24608 | tf_op jit(solution)/shard_map/ppermute | solution.py:231
  39.4 2.1 %shard_map.65 = bf16[512,768]{1,0:T(8,128)(2,1)} custom-call(bf16[96,128]{1,0:T(8,128)(2,1)S(1)} %shard_map.63.p0, bf16[96,128]{1,0:T(8,128)(2,1)S(1)} %collective-permute-done.9.p1, bf16[96,128]{1,0:T(8,128)(2,1)S(1)} %collective-permute-done.10.p2, bf16[96,128]{1,0:T(8,128)(2,1)S(1)} %collective-permute-done.11.p3, ...), custom_call_target="tpu_custom_call" | custom-call | flops 1207959552 | bytes 5210112 | tf_op jit(solution)/shard_map/pallas_call | solution.py:52
  (19 shorter events, 2.6 us)
Async XLA Ops:
  0.0 1.3 %copy-start.1 = (bf16[16,32,768]{2,1,0:T(8,128)(2,1)S(1)}, bf16[16,32,768]{2,1,0:T(8,128)(2,1)}, u32[]{:S(2)}) copy-start(bf16[16,32,768]{2,1,0:T(8,128)(2,1)} %param.5) | copy-start | bytes 2359300
  1.3 2.9 %collective-permute-start.1 = (bf16[512,768]{1,0:T(8,128)(2,1)S(1)}, bf16[512,768]{1,0:T(8,128)(2,1)S(1)}, u32[]{:S(2)}, u32[]{:S(2)}) collective-permute-start(bf16[512,768]{1,0:T(8,128)(2,1)S(1)} %bitcast.5), channel_id=1, source_target_pairs={{0,1},{1,0},{2,3},{3,2},{4,5},{5,4},{6,7},{7,6},{8,9},{9,8},{10,11... | collective-permute-start | bytes 2359304 | tf_op jit(solution)/shard_map/ppermute | solution.py:231
  1.7 12.3 %collective-permute-start = (bf16[256,768]{1,0:T(8,128)(2,1)S(1)}, bf16[256,768]{1,0:T(8,128)(2,1)S(1)}, u32[]{:S(2)}, u32[]{:S(2)}) collective-permute-start(bf16[256,768]{1,0:T(8,128)(2,1)S(1)} %shard_map.55), channel_id=1, source_target_pairs={{0,2},{1,3},{2,0},{3,1},{4,6},{5,7},{6,4},{7,5},{8,10},{9,11},{10,... | collective-permute-start | bytes 1179656 | tf_op jit(solution)/shard_map/ppermute | solution.py:231
  4.2 0.9 %copy-start.2 = (bf16[512,768]{1,0:T(8,128)(2,1)}, bf16[512,768]{1,0:T(8,128)(2,1)S(1)}, u32[]{:S(2)}) copy-start(bf16[512,768]{1,0:T(8,128)(2,1)S(1)} %collective-permute-done.1.twin) | copy-start | bytes 2359300
  14.0 2.7 %collective-permute-start.2 = (bf16[256,768]{1,0:T(8,128)(2,1)S(1)}, bf16[256,768]{1,0:T(8,128)(2,1)S(1)}, u32[]{:S(2)}, u32[]{:S(2)}) collective-permute-start(bf16[256,768]{1,0:T(8,128)(2,1)S(1)} %collective-permute-done.x_far.x), channel_id=1, source_target_pairs={{0,1},{1,0},{2,3},{3,2},{4,5},{5,4},{6,7},{7,6},{8,9},{9,8},{10,11... | collective-permute-start | bytes 1179656 | tf_op jit(solution)/shard_map/ppermute | solution.py:231
  14.9 5.6 %collective-permute-start.4 = (f32[192,128]{1,0:T(8,128)S(1)}, f32[192,128]{1,0:T(8,128)S(1)}, u32[]{:S(2)}, u32[]{:S(2)}) collective-permute-start(f32[192,128]{1,0:T(8,128)S(1)} %shard_map.58), channel_id=1, source_target_pairs={{0,2},{1,3},{2,0},{3,1},{4,6},{5,7},{6,4},{7,5},{8,10},{9,11},{10,... | collective-permute-start | bytes 294920 | tf_op jit(solution)/shard_map/ppermute | solution.py:231
  16.7 16.8 %collective-permute-start.3 = (bf16[256,768]{1,0:T(8,128)(2,1)S(1)}, bf16[256,768]{1,0:T(8,128)(2,1)S(1)}, u32[]{:S(2)}, u32[]{:S(2)}) collective-permute-start(bf16[256,768]{1,0:T(8,128)(2,1)S(1)} %shard_map.57), channel_id=1, source_target_pairs={{0,2},{1,3},{2,0},{3,1},{4,6},{5,7},{6,4},{7,5},{8,10},{9,11},{10,... | collective-permute-start | bytes 1179656 | tf_op jit(solution)/shard_map/ppermute | solution.py:231
  20.7 5.5 %collective-permute-start.5 = (f32[96,128]{1,0:T(8,128)S(1)}, f32[96,128]{1,0:T(8,128)S(1)}, u32[]{:S(2)}, u32[]{:S(2)}) collective-permute-start(f32[96,128]{1,0:T(8,128)S(1)} %get-tuple-element.41), channel_id=1, source_target_pairs={{0,12},{4,8},{8,4},{12,0},{16,28},{20,24},{24,20},{28,16},{1,13},{... | collective-permute-start | bytes 147464 | tf_op jit(solution)/shard_map/ppermute | solution.py:237
  23.6 4.1 %collective-permute-start.6 = (f32[96,128]{1,0:T(8,128)S(1)}, f32[96,128]{1,0:T(8,128)S(1)}, u32[]{:S(2)}, u32[]{:S(2)}) collective-permute-start(f32[96,128]{1,0:T(8,128)S(1)} %get-tuple-element.43), channel_id=1, source_target_pairs={{0,4},{4,12},{8,0},{12,8},{16,20},{20,28},{24,16},{28,24},{1,5},{5... | collective-permute-start | bytes 147464 | tf_op jit(solution)/shard_map/ppermute | solution.py:237
  24.1 4.1 %collective-permute-start.7 = (f32[96,128]{1,0:T(8,128)S(1)}, f32[96,128]{1,0:T(8,128)S(1)}, u32[]{:S(2)}, u32[]{:S(2)}) collective-permute-start(f32[96,128]{1,0:T(8,128)S(1)} %get-tuple-element.46), channel_id=1, source_target_pairs={{0,8},{4,0},{8,12},{12,4},{16,24},{20,16},{24,28},{28,20},{1,9},{5... | collective-permute-start | bytes 147464 | tf_op jit(solution)/shard_map/ppermute | solution.py:237
  28.2 5.1 %collective-permute-start.8 = (f32[96,128]{1,0:T(8,128)S(1)}, f32[96,128]{1,0:T(8,128)S(1)}, u32[]{:S(2)}, u32[]{:S(2)}) collective-permute-start(f32[96,128]{1,0:T(8,128)S(1)} %shard_map.62.mine), channel_id=1, source_target_pairs={{0,16},{4,20},{8,24},{12,28},{16,0},{20,4},{24,8},{28,12},{1,17},{... | collective-permute-start | bytes 147464 | tf_op jit(solution)/shard_map/ppermute | solution.py:231
  33.4 5.9 %copy-start = (bf16[768,768]{1,0:T(8,128)(2,1)S(1)}, bf16[768,768]{1,0:T(8,128)(2,1)}, u32[]{:S(2)}) copy-start(bf16[768,768]{1,0:T(8,128)(2,1)} %wo.1) | copy-start | bytes 3538948
  33.5 3.6 %collective-permute-start.12 = (bf16[256,768]{1,0:T(8,128)(2,1)S(1)}, bf16[256,768]{1,0:T(8,128)(2,1)S(1)}, u32[]{:S(2)}, u32[]{:S(2)}) collective-permute-start(bf16[256,768]{1,0:T(8,128)(2,1)S(1)} %collective-permute-done.3.x), channel_id=1, source_target_pairs={{0,1},{1,0},{2,3},{3,2},{4,5},{5,4},{6,7},{7,6},{8,9},{9,8},{10,11... | collective-permute-start | bytes 1179656 | tf_op jit(solution)/shard_map/ppermute | solution.py:231
  33.5 4.9 %collective-permute-start.11 = (bf16[96,128]{1,0:T(8,128)(2,1)S(1)}, bf16[96,128]{1,0:T(8,128)(2,1)S(1)}, u32[]{:S(2)}, u32[]{:S(2)}) collective-permute-start(bf16[96,128]{1,0:T(8,128)(2,1)S(1)} %shard_map.63.p0), channel_id=1, source_target_pairs={{0,12},{4,8},{8,4},{12,0},{16,28},{20,24},{24,20},{28,16},{1,13},{... | collective-permute-start | bytes 73736 | tf_op jit(solution)/shard_map/ppermute | solution.py:231
  35.3 3.8 %collective-permute-start.10 = (bf16[96,128]{1,0:T(8,128)(2,1)S(1)}, bf16[96,128]{1,0:T(8,128)(2,1)S(1)}, u32[]{:S(2)}, u32[]{:S(2)}) collective-permute-start(bf16[96,128]{1,0:T(8,128)(2,1)S(1)} %shard_map.63.p0), channel_id=1, source_target_pairs={{0,8},{4,12},{8,0},{12,4},{16,24},{20,28},{24,16},{28,20},{1,9},{5... | collective-permute-start | bytes 73736 | tf_op jit(solution)/shard_map/ppermute | solution.py:231
  35.5 3.8 %collective-permute-start.9 = (bf16[96,128]{1,0:T(8,128)(2,1)S(1)}, bf16[96,128]{1,0:T(8,128)(2,1)S(1)}, u32[]{:S(2)}, u32[]{:S(2)}) collective-permute-start(bf16[96,128]{1,0:T(8,128)(2,1)S(1)} %shard_map.63.p0), channel_id=1, source_target_pairs={{0,4},{4,0},{8,12},{12,8},{16,20},{20,16},{24,28},{28,24},{1,5},{5... | collective-permute-start | bytes 73736 | tf_op jit(solution)/shard_map/ppermute | solution.py:231
